TPU v7x, 32 devices: a whole 2x2x4 slice. The times are simulated.
32 devices in a mesh: gx: 8 (over y, x, core), gy: 4 (over z).
Axes of the slice: x: 2, y: 2, z: 4, core: 2. Of those that a mesh axis runs over, the one named last changes fastest.
Arguments:
- fields: float32 [14, 48, 128, 512], P(None, None, 'gx', 'gy'), may hold values from -1.5 to 9, as said below
- register: float32 [14, 48, 128, 512], P(None, None, 'gx', 'gy'), may hold values from -0.15 to 0.15
Outputs:
- fields_next: float32 [14, 48, 128, 512], P(None, None, 'gx', 'gy')
- register_next: float32 [14, 48, 128, 512], P(None, None, 'gx', 'gy')
- flame_metrics: bfloat16 [5, 48, 128, 512], P(None, 'gy', 'gx')
Inputs may be any that keep to these rules, and one draw needn't show every extreme that they name: fields[0] lies in 0.5 to 1.5; velocities fields[1:4] / fields[0] lie within -1 to 1; fields[4] / fields[0] minus half the squared speed lies in 1 to 4; each species density over fields[0] lies in 0.01 to 0.7.
All inputs are finite; a program needn't handle non-finite values.
Results may differ from a plain program's by a relative error of at most 0.0014.
The roundings to bfloat16 on the way count: a program that leaves them out, or rounds other values in their place, can miss the bound.
Values may be sent and summed in bfloat16 or wider, within the bound.
No kernel may reach another device: no remote copies, remote signals or barrier semaphores. Data moves between devices by JAX's collectives and lax.ppermute only.
A program may use at most 192 MiB of HBM per device.

v0:
```python
import jax
import jax.numpy as jnp
import numpy as np
from jax import lax
from jax.sharding import PartitionSpec as P

GAMMA_LESS = 0.4
UNIVERSAL_R = 0.25
TIME_STEP = 0.25
SECTION_DECAY = -0.4178904745
SECTION_WEIGHT = 0.3792103129
GRAD_FLOOR = 0.1
PROGRESS_SCALE = 4.0
CENTRAL_WEIGHTS = (0.8, -0.2, 4.0 / 105.0, -1.0 / 280.0)
MOLAR_MASS = (2.0, 32.0, 16.0, 17.0, 18.0, 1.0, 33.0, 34.0, 28.0)
FORMATION_HEAT = (0.0, 0.0, 2.0, 0.3, -1.5, 3.0, 0.1, -0.4, 0.0)
ARRHENIUS_LIST = (
    (5, 1, (2, 3), 40.0, 2.0),
    (2, 0, (5, 3), 30.0, 1.2),
    (3, 0, (5, 4), 25.0, 0.8),
    (2, 4, (3, 3), 10.0, 1.6),
    (5, 1, (6,), 15.0, 0.2),
    (6, 5, (3, 3), 20.0, 0.3),
    (6, 6, (7, 1), 12.0, 0.4),
    (7, 8, (3, 3, 8), 8.0, 1.8),
)


def with_halo(block, sides, width):
    for axis, dim in sides:
        count = lax.axis_size(axis)
        forward = [(i, i + 1) for i in range(count - 1)]
        forward.append((count - 1, 0))
        backward = [(target, source) for source, target in forward]
        low = lax.ppermute(
            lax.slice_in_dim(block, block.shape[dim] - width, None, axis=dim), axis, forward
        )
        high = lax.ppermute(lax.slice_in_dim(block, 0, width, axis=dim), axis, backward)
        block = jnp.concatenate([low, block, high], axis=dim)
    return block


def make_table():
    table = np.zeros((14, 8))
    for column, kinetic_step_record in enumerate(ARRHENIUS_LIST):
        change = np.zeros(9)
        change[kinetic_step_record[0]] -= 1.0
        change[kinetic_step_record[1]] -= 1.0
        for product in kinetic_step_record[2]:
            change[product] += 1.0
        for species in range(9):
            mass_change = MOLAR_MASS[species] / 18.0 * change[species]
            table[5 + species, column] = mass_change
            table[4, column] -= FORMATION_HEAT[species] * mass_change
    return table


def inverse_weights():
    return np.array([18.0 / value for value in MOLAR_MASS])


def primitives(fields):
    velocity = fields[1:4] / fields[0]
    static_stress = GAMMA_LESS * (
        fields[4]
        - 0.5 * (fields[1] * velocity[0] + fields[2] * velocity[1] + fields[3] * velocity[2])
    )
    return (velocity, static_stress)


def reaction_rates(fields, static_stress):
    species_quantities = fields[5:14] * jnp.asarray(inverse_weights(), jnp.float32).reshape(
        9, 1, 1, 1
    )
    summed_quantity = jnp.sum(species_quantities, axis=0)
    cell_thermal_state = static_stress / (UNIVERSAL_R * summed_quantity)
    return jnp.stack(
        [
            kinetic_step_record[3]
            * jnp.exp(-kinetic_step_record[4] / cell_thermal_state)
            * species_quantities[kinetic_step_record[0]]
            * species_quantities[kinetic_step_record[1]]
            for kinetic_step_record in ARRHENIUS_LIST
        ]
    )


def directed_flux(fields, velocity, static_stress, direction):
    speed = velocity[direction]
    base = fields * speed
    select = jnp.asarray(np.eye(3)[direction].reshape(3, 1, 1, 1), jnp.float32)
    moment = base[1:4] + static_stress * select
    energy = base[4:5] + (static_stress * speed)[None]
    return jnp.concatenate([base[0:1], moment, energy, base[5:]], axis=0)


def rim_flux(piece, direction):
    velocity, static_stress = primitives(piece)
    return directed_flux(piece, velocity, static_stress, direction)


def central(extended, along, count):
    total = jnp.zeros(extended.shape[:along] + (count,) + extended.shape[along + 1 :], jnp.float32)
    for offset, weight in enumerate(CENTRAL_WEIGHTS, 1):
        ahead = lax.slice_in_dim(extended, 4 + offset, 4 + offset + count, axis=along)
        behind = lax.slice_in_dim(extended, 4 - offset, 4 - offset + count, axis=along)
        total = total + weight * (ahead - behind)
    return total


def flame_metrics(padded):
    scalar = padded[0]
    grad_z = (scalar[2:, 1:-1, 1:-1] - scalar[:-2, 1:-1, 1:-1]) * 0.5
    grad_x = (scalar[1:-1, 2:, 1:-1] - scalar[1:-1, :-2, 1:-1]) * 0.5
    grad_y = (scalar[1:-1, 1:-1, 2:] - scalar[1:-1, 1:-1, :-2]) * 0.5
    magnitude = jnp.maximum(
        jnp.sqrt(grad_x * grad_x + grad_y * grad_y + grad_z * grad_z), GRAD_FLOOR
    )
    normal_x = -grad_x / magnitude
    normal_y = -grad_y / magnitude
    normal_z = -grad_z / magnitude
    curvature = 0.5 * (normal_x[1:-1, 2:, 1:-1] - normal_x[1:-1, :-2, 1:-1])
    curvature = curvature + 0.5 * (normal_y[1:-1, 1:-1, 2:] - normal_y[1:-1, 1:-1, :-2])
    curvature = curvature + 0.5 * (normal_z[2:, 1:-1, 1:-1] - normal_z[:-2, 1:-1, 1:-1])
    inner = (normal_x[1:-1, 1:-1, 1:-1], normal_y[1:-1, 1:-1, 1:-1], normal_z[1:-1, 1:-1, 1:-1])
    speeds = padded[1:4]
    gradients = []
    for component in range(3):
        piece = speeds[component]
        along_x = (piece[2:-2, 3:-1, 2:-2] - piece[2:-2, 1:-3, 2:-2]) * 0.5
        along_y = (piece[2:-2, 2:-2, 3:-1] - piece[2:-2, 2:-2, 1:-3]) * 0.5
        along_z = (piece[3:-1, 2:-2, 2:-2] - piece[1:-3, 2:-2, 2:-2]) * 0.5
        gradients.append((along_x, along_y, along_z))
    strain = gradients[0][0] + gradients[1][1] + gradients[2][2]
    for component in range(3):
        for direction in range(3):
            strain = strain - inner[component] * inner[direction] * gradients[component][direction]
    return jnp.stack([inner[0], inner[1], inner[2], curvature, strain])


def per_device(fields, register):
    count_z = fields.shape[1]
    count_x = fields.shape[2]
    count_y = fields.shape[3]
    velocity, static_stress = primitives(fields)
    probe = jnp.concatenate(
        [(PROGRESS_SCALE * (fields[9] / fields[0]))[None], velocity], axis=0
    ).astype(jnp.bfloat16)
    bricks = lax.all_to_all(probe, "gy", split_axis=1, concat_axis=3, tiled=True)
    rimmed = with_halo(bricks, (("gx", 2), ("gy", 1)), 2)
    padded = jnp.concatenate([rimmed[:, :, :, -2:], rimmed, rimmed[:, :, :, :2]], axis=3)
    metrics = flame_metrics(padded.astype(jnp.float32)).astype(jnp.bfloat16)
    flux_x = directed_flux(fields, velocity, static_stress, 0)
    flux_y = directed_flux(fields, velocity, static_stress, 1)
    flux_z = directed_flux(fields, velocity, static_stress, 2)
    rates = reaction_rates(fields, static_stress)
    source = jnp.tensordot(
        jnp.asarray(make_table(), jnp.float32), rates, axes=1, precision=lax.Precision.HIGHEST
    )
    haloed = with_halo(fields, (("gx", 2), ("gy", 3)), 4)
    lower_x = rim_flux(haloed[:, :, :4, 4 : 4 + count_y], 0)
    upper_x = rim_flux(haloed[:, :, 4 + count_x :, 4 : 4 + count_y], 0)
    lower_y = rim_flux(haloed[:, :, 4 : 4 + count_x, :4], 1)
    upper_y = rim_flux(haloed[:, :, 4 : 4 + count_x, 4 + count_y :], 1)
    extended_x = jnp.concatenate([lower_x, flux_x, upper_x], axis=2)
    extended_y = jnp.concatenate([lower_y, flux_y, upper_y], axis=3)
    extended_z = jnp.concatenate([flux_z[:, -4:], flux_z, flux_z[:, :4]], axis=1)
    advection = (
        central(extended_x, 2, count_x)
        + central(extended_y, 3, count_y)
        + central(extended_z, 1, count_z)
    )
    register_next = SECTION_DECAY * register + TIME_STEP * (source - advection)
    fields_next = fields + SECTION_WEIGHT * register_next
    return (fields_next, register_next, metrics)


def solution(mesh):
    in_specs = (P(None, None, "gx", "gy"), P(None, None, "gx", "gy"))
    out_specs = (P(None, None, "gx", "gy"), P(None, None, "gx", "gy"), P(None, "gy", "gx", None))
    return jax.shard_map(
        per_device, mesh=mesh, in_specs=in_specs, out_specs=out_specs, check_vma=False
    )
```

profile of v0, /device:TPU:0, one launch (start us, length us, event | category | flops | bytes accessed | tf_op | source)
XLA Modules:
  0.0 242.5 jit_solution(14974858709711430738)
XLA Ops:
  0.7 3.3 %fusion.132 = (f32[14,48,4,128]{3,2,1,0:T(4,128)S(1)}, f32[14,48,4,128]{3,2,1,0:T(4,128)S(1)}) fusion(f32[14,48,16,128]{3,2,1,0:T(8,128)} %param.11), kind=kLoop, calls=%fused_computation.261 | loop fusion | bytes 5505024 | tf_op jit(solution)/shard_map/slice | solution.py:36
  4.0 1.3 copy.259
  5.3 3.3 %collective-permute-start = (f32[14,48,4,128]{3,1,2,0:T(8,128)}, f32[14,48,4,128]{3,1,2,0:T(8,128)}, u32[]{:S(2)}, u32[]{:S(2)}) collective-permute-start(f32[14,48,4,128]{3,1,2,0:T(8,128)} %copy.259), channel_id=1, source_target_pairs={{4,0},{8,4},{12,8},{16,12},{20,16},{24,20},{28,24},{0,28},{5,1},{9... | collective-permute-start | bytes 4128776 | tf_op jit(solution)/shard_map/ppermute | solution.py:38
  8.6 1.3 copy.260
  10.6 1.8 fusion.97
  12.7 1.1 copy.256
  13.8 4.9 %all-to-all-start = ((bf16[4,48,16,128]{3,2,0,1:T(8,128)(2,1)}), bf16[4,48,16,128]{3,2,0,1:T(8,128)(2,1)}, u32[]{:S(2)}, u32[]{:S(2)}) async-start(bf16[4,48,16,128]{3,2,0,1:T(8,128)(2,1)} %copy.256), calls=%async_computation | async-start | bytes 1572864 | tf_op jit(solution)/shard_map/all_to_all | solution.py:149
  18.7 2.1 fusion.92
  20.9 2.0 fusion.68
  22.9 2.0 fusion.66
  24.9 2.0 fusion.82
  26.9 6.4 %broadcast_multiply_fusion.2 = (f32[14,48,16,128]{3,2,1,0:T(8,128)}, f32[14,48,16,128]{3,2,1,0:T(8,128)}, f32[14,48,16,128]{3,2,1,0:T(8,128)}) fusion(f32[14,48,16,128]{3,2,1,0:T(8,128)S(1)} %bitcast.143, f32[48,16,128]{2,1,0:T(8,128)S(1)} %copy-done.14, f32[48,16,128]{2,1,0:T(8,128)S(1)} %copy-done.16, f32[48,16,128]{2,1,0:T(8,128)S(1)} %copy-done.15), kind=kLoop, calls=%fused_computation.56 | loop fusion | flops 4128768 | bytes 23199744 | tf_op jit(solution)/shard_map/mul | solution.py:90
  33.4 2.6 %fusion.131 = (f32[1,48,16,128]{3,2,1,0:T(8,128)}, f32[1,48,16,128]{3,2,1,0:T(8,128)}, f32[8,48,16,128]{3,2,1,0:T(8,128)}) fusion(f32[14,48,16,128]{3,2,1,0:T(8,128)} %get-tuple-element.40, f32[1,48,16,128]{3,2,1,0:T(8,128)S(1)} %get-tuple-element.22, f32[3,48,16,128]{3,2,1,0:T(8,128)S(1)} %get-tuple-element.18, f32[8,48,16,128]{3,2,1,0:T(8,128)} %fusion.82, ...), kind=kLoop, calls=%fused_computation.260 | loop fusion | flops 786432 | bytes 3932160 | tf_op jit(solution)/shard_map/slice | solution.py:94
  36.0 2.3 fusion.133
  38.4 3.5 %slice_add_fusion.2 = (f32[3,48,16,128]{3,2,1,0:T(8,128)}, f32[3,48,16,128]{3,2,1,0:T(8,128)}, f32[3,48,16,128]{3,2,1,0:T(8,128)S(1)}) fusion(f32[14,48,16,128]{3,2,1,0:T(8,128)} %get-tuple-element.40, f32[3]{0:T(128)S(1)} %copy-done.25, f32[48,16,128]{2,1,0:T(8,128)S(1)} %bitcast.144, f32[3]{0:T(128)S(1)} %copy-done.26, ...), kind=kLoop, calls=%fused_computation.70 | loop fusion | flops 1769472 | bytes 7471140 | tf_op jit(solution)/shard_map/add | solution.py:92
  41.9 2.1 fusion.134
  44.2 8.1 %fusion.1 = (f32[14,52,16,128]{3,2,1,0:T(8,128)}, f32[14,52,16,128]{3,2,1,0:T(8,128)}) fusion(f32[9,48,16,128]{3,2,1,0:T(8,128)S(1)} %slice.784, f32[1,48,16,128]{3,2,1,0:T(8,128)S(1)} %get-tuple-element.52, f32[3,48,16,128]{3,2,1,0:T(8,128)S(1)} %get-tuple-element.75, f32[1,48,16,128]{3,2,1,0:T(8,128)S(1)} %get-tuple-element.51), kind=kLoop, calls=%fused_computation.9 | loop fusion | flops 20873216 | bytes 17432576 | tf_op jit(solution)/shard_map/concatenate | solution.py:167
  52.3 1.7 copy.257
  54.4 0.9 fusion.135
  55.3 2.4 collective-permute-start.5
  57.7 9.9 %fusion.28 = f32[14,48,16,128]{3,0,2,1:T(8,128)} fusion(f32[14,8,1,1]{0,1,3,2:T(8,128)S(1)} %copy-done.24, f32[8,48,16,128]{3,2,1,0:T(8,128)} %get-tuple-element.70), kind=kOutput, calls=%fused_computation.52 | convolution fusion | flops 132120576 | bytes 8651200 | tf_op jit(solution)/shard_map/dot_general | solution.py:157
  67.6 11.2 %copy.251 = f32[14,48,16,128]{1,2,3,0:T(8,128)} copy(f32[14,48,16,128]{3,2,1,0:T(8,128)} %param.11) | data formatting | bytes 11010048 | tf_op args[0]
  78.8 2.4 %slice.744 = f32[9,48,16,128]{3,2,1,0:T(8,128)S(1)} slice(f32[14,48,16,128]{3,2,1,0:T(8,128)} %get-tuple-element.42), slice={[5:14], [0:48], [0:16], [0:128]} | slice | bytes 7077888 | tf_op jit(solution)/shard_map/slice | solution.py:94
  81.2 4.0 %slice.706 = f32[9,48,16,128]{3,2,1,0:T(8,128)} slice(f32[14,48,16,128]{3,2,1,0:T(8,128)} %get-tuple-element.40), slice={[5:14], [0:48], [0:16], [0:128]} | slice | bytes 7077888 | tf_op jit(solution)/shard_map/slice | solution.py:94
  85.2 1.7 pad_maximum_fusion.23
  87.0 3.5 %collective-permute-start.7 = (bf16[4,2,20,512]{3,2,1,0:T(8,128)(2,1)}, bf16[4,2,20,512]{3,2,1,0:T(8,128)(2,1)}, u32[]{:S(2)}, u32[]{:S(2)}) collective-permute-start(bf16[4,2,20,512]{3,2,1,0:T(8,128)(2,1)} %get-tuple-element.65), channel_id=1, source_target_pairs={{1,0},{2,1},{3,2},{0,3},{5,4},{6,5},{7,6},{4,7},{9,8},{10,9},{11,1... | collective-permute-start | bytes 491528 | tf_op jit(solution)/shard_map/ppermute | solution.py:38
  90.5 0.9 slice_bitcast_fusion.9
  91.4 1.9 copy.237
  93.4 1.9 broadcast_multiply_fusion.4
  95.3 1.1 copy-done.7
  97.2 0.9 slice_bitcast_fusion.8
  98.2 1.9 copy.245
  100.1 1.9 broadcast_multiply_fusion.3
  102.0 0.9 slice_add_fusion.10
  103.2 4.1 %copy.252 = f32[14,48,4,128]{1,2,3,0:T(4,128)} copy(f32[14,48,4,128]{3,1,2,0:T(8,128)} %collective-permute-done) | data formatting | bytes 2752512 | tf_op jit(solution)/shard_map/ppermute | solution.py:38
  107.3 4.1 %copy.250 = f32[14,48,4,128]{1,2,3,0:T(4,128)} copy(f32[14,48,4,128]{3,1,2,0:T(8,128)} %collective-permute-done.1) | data formatting | bytes 2752512 | tf_op jit(solution)/shard_map/ppermute | solution.py:35
  111.5 1.8 pad_maximum_fusion.18
  113.3 3.9 %collective-permute-start.2 = (f32[14,48,24,4]{1,2,3,0:T(8,128)S(1)}, f32[14,48,24,4]{1,2,3,0:T(8,128)S(1)}, u32[]{:S(2)}, u32[]{:S(2)}) collective-permute-start(f32[14,48,24,4]{1,2,3,0:T(8,128)S(1)} %get-tuple-element.31), channel_id=1, source_target_pairs={{1,0},{2,1},{3,2},{0,3},{5,4},{6,5},{7,6},{4,7},{9,8},{10,9},{11,1... | collective-permute-start | bytes 774152 | tf_op jit(solution)/shard_map/ppermute | solution.py:38
  117.5 6.9 %maximum_maximum_fusion.1 = (f32[14,48,20,128]{3,2,1,0:T(8,128)}, f32[14,48,20,128]{3,2,1,0:T(8,128)}) fusion(f32[9,48,4,128]{3,2,1,0:T(4,128)S(1)} %slice-done.2, f32[1,48,4,128]{3,2,1,0:T(4,128)S(1)} %copy-done.17, f32[3,48,4,128]{3,2,1,0:T(4,128)S(1)} %get-tuple-element.76, f32[1,48,4,128]{3,2,1,0:T(4,128)S(1)} %copy-done.18, ...), kind=kLoop, calls=%fused_computation.2 | loop fusion | flops 24084480 | bytes 22020096 | tf_op jit(solution)/shard_map/concatenate | solution.py:165
  124.3 5.0 %fusion.31 = f32[4,16,20,516]{3,2,1,0:T(8,128)S(1)} fusion(bf16[4,2,20,512]{3,2,1,0:T(8,128)(2,1)} %collective-permute-done.7, bf16[4,2,20,512]{3,2,1,0:T(8,128)(2,1)} %collective-permute-done.6, bf16[4,12,2,512]{3,2,1,0:T(2,128)(2,1)} %collective-permute-done.5, bf16[4,12,16,512]{3,2,1,0:T(8,128)(2,1)S(1)} %copy-done.6, ...), kind=kLoop, calls=%fused_computation.59 | loop fusion | flops 19814400 | bytes 3952640 | tf_op jit(solution)/shard_map/convert_element_type | solution.py:152
  129.6 1.2 negate_divide_fusion
  132.7 2.4 bitcast_dynamic-update-slice_fusion
  135.3 10.5 %collective-permute-done.3 = f32[14,48,24,4]{1,2,3,0:T(8,128)S(1)} collective-permute-done((f32[14,48,24,4]{1,2,3,0:T(8,128)S(1)}, f32[14,48,24,4]{1,2,3,0:T(8,128)S(1)}, u32[]{:S(2)}, u32[]{:S(2)}) %collective-permute-start.3) | collective-permute-done | bytes 258080 | tf_op jit(solution)/shard_map/ppermute | solution.py:35
  146.0 1.0 pad_maximum_fusion.19
  147.1 4.6 %copy.253 = f32[14,48,16,4]{3,2,1,0:T(8,128)} copy(f32[14,48,16,4]{1,2,3,0:T(8,128)} %get-tuple-element.80) | data formatting | bytes 344064 | tf_op jit(solution)/shard_map/concatenate | solution.py:94
  151.7 4.6 %copy.254 = f32[14,48,16,4]{3,2,1,0:T(8,128)} copy(f32[14,48,16,4]{1,2,3,0:T(8,128)} %get-tuple-element.81) | data formatting | bytes 344064 | tf_op jit(solution)/shard_map/concatenate | solution.py:94
  156.3 15.8 %pad_maximum_fusion = (f32[14,48,16,132]{3,2,1,0:T(8,128)}, f32[14,48,16,132]{3,2,1,0:T(8,128)}) fusion(f32[14,48,16,4]{3,2,1,0:T(8,128)} %copy.253, f32[9,48,16,128]{3,2,1,0:T(8,128)S(1)} %slice.744, f32[1,48,16,128]{3,2,1,0:T(8,128)} %get-tuple-element.48, f32[3,48,16,128]{3,2,1,0:T(8,128)} %get-tuple-element.74, f32[1,48,16,128]{3,2,1,0:T(8,128)} %get-tuple-element.47, ...), kind=kLoop, calls=%fused_computation | loop fusion | flops 11354112 | bytes 17203200 | tf_op jit(solution)/shard_map/concatenate | solution.py:166
  172.2 70.2 %multiply_add_fusion = (f32[14,48,16,128]{3,2,1,0:T(8,128)}, f32[14,48,16,128]{3,2,1,0:T(8,128)}) fusion(f32[14,48,16,128]{3,2,1,0:T(8,128)} %param.11, f32[14,52,16,128]{3,2,1,0:T(8,128)} %get-tuple-element.50, f32[14,52,16,128]{3,2,1,0:T(8,128)} %get-tuple-element.49, f32[14,48,16,132]{3,2,1,0:T(8,128)} %get-tuple-element.44, ...), kind=kLoop, calls=%fused_computation.50 | loop fusion | flops 56426496 | bytes 159645696 | tf_op jit(solution)/shard_map/add | solution.py:174
  (111 shorter events, 5.7 us)
Async XLA Ops:
  0.6 9.3 %copy-start.28 = (f32[9]{0:T(128)S(1)}, f32[9]{0:T(128)}, u32[]{:S(2)}) copy-start(f32[9]{0:T(128)} %constant.27.clone) | copy-start | bytes 112
  0.6 9.2 %copy-start = (f32[14,48,16,128]{3,2,1,0:T(8,128)S(1)}, f32[14,48,16,128]{3,2,1,0:T(8,128)}, u32[]{:S(2)}) copy-start(f32[14,48,16,128]{3,2,1,0:T(8,128)} %param.11) | copy-start | bytes 16515076
  5.3 85.2 %collective-permute-start = (f32[14,48,4,128]{3,1,2,0:T(8,128)}, f32[14,48,4,128]{3,1,2,0:T(8,128)}, u32[]{:S(2)}, u32[]{:S(2)}) collective-permute-start(f32[14,48,4,128]{3,1,2,0:T(8,128)} %copy.259), channel_id=1, source_target_pairs={{4,0},{8,4},{12,8},{16,12},{20,16},{24,20},{28,24},{0,28},{5,1},{9... | collective-permute-start | bytes 4128776 | tf_op jit(solution)/shard_map/ppermute | solution.py:38
  9.9 87.3 %collective-permute-start.1 = (f32[14,48,4,128]{3,1,2,0:T(8,128)}, f32[14,48,4,128]{3,1,2,0:T(8,128)}, u32[]{:S(2)}, u32[]{:S(2)}) collective-permute-start(f32[14,48,4,128]{3,1,2,0:T(8,128)} %copy.260), channel_id=1, source_target_pairs={{0,4},{4,8},{8,12},{12,16},{16,20},{20,24},{24,28},{28,0},{1,5},{5... | collective-permute-start | bytes 4128776 | tf_op jit(solution)/shard_map/ppermute | solution.py:35
  10.4 2.3 copy-start.1
  12.4 14.4 %slice-start = ((s8[5505024]{0:T(1024)(128)(4,1)}), s8[1310720]{0:T(1024)(128)(4,1)S(1)}, s32[]{:S(2)}) async-start(s8[5505024]{0:T(1024)(128)(4,1)} %bitcast.142), calls=%async_computation.1 | async-start | bytes 2621440
  13.8 38.5 %all-to-all-start = ((bf16[4,48,16,128]{3,2,0,1:T(8,128)(2,1)}), bf16[4,48,16,128]{3,2,0,1:T(8,128)(2,1)}, u32[]{:S(2)}, u32[]{:S(2)}) async-start(bf16[4,48,16,128]{3,2,0,1:T(8,128)(2,1)} %copy.256), calls=%async_computation | async-start | bytes 1572864 | tf_op jit(solution)/shard_map/all_to_all | solution.py:149
  18.7 8.2 %copy-start.14 = (f32[48,16,128]{2,1,0:T(8,128)S(1)}, f32[48,16,128]{2,1,0:T(8,128)}, u32[]{:S(2)}) copy-start(f32[48,16,128]{2,1,0:T(8,128)} %get-tuple-element.61) | copy-start | bytes 1179652
  18.7 8.2 %copy-start.15 = (f32[48,16,128]{2,1,0:T(8,128)S(1)}, f32[48,16,128]{2,1,0:T(8,128)}, u32[]{:S(2)}) copy-start(f32[48,16,128]{2,1,0:T(8,128)} %get-tuple-element.62) | copy-start | bytes 1179652
  18.7 8.2 %copy-start.16 = (f32[48,16,128]{2,1,0:T(8,128)S(1)}, f32[48,16,128]{2,1,0:T(8,128)}, u32[]{:S(2)}) copy-start(f32[48,16,128]{2,1,0:T(8,128)} %get-tuple-element.63) | copy-start | bytes 1179652
  18.7 8.2 %slice-start.1 = ((s8[5505024]{0:T(1024)(128)(4,1)}), s8[4194304]{0:T(1024)(128)(4,1)S(1)}, s32[]{:S(2)}) async-start(s8[5505024]{0:T(1024)(128)(4,1)} %bitcast.142), calls=%async_computation.2 | async-start | bytes 8388608
  33.4 5.0 %copy-start.2 = (f32[14,48,16,128]{3,2,1,0:T(8,128)S(1)}, f32[14,48,16,128]{3,2,1,0:T(8,128)}, u32[]{:S(2)}) copy-start(f32[14,48,16,128]{3,2,1,0:T(8,128)} %get-tuple-element.41) | copy-start | bytes 16515076
  33.4 5.0 %copy-start.25 = (f32[3]{0:T(128)S(1)}, f32[3]{0:T(128)}, u32[]{:S(2)}) copy-start(f32[3]{0:T(128)} %constant.29) | copy-start | bytes 40
  33.4 5.0 %copy-start.26 = (f32[3]{0:T(128)S(1)}, f32[3]{0:T(128)}, u32[]{:S(2)}) copy-start(f32[3]{0:T(128)} %constant.30) | copy-start | bytes 40
  33.4 5.0 %copy-start.27 = (f32[3]{0:T(128)S(1)}, f32[3]{0:T(128)}, u32[]{:S(2)}) copy-start(f32[3]{0:T(128)} %constant.31) | copy-start | bytes 40
  44.2 13.5 %copy-start.24 = (f32[14,8,1,1]{0,1,3,2:T(8,128)S(1)}, f32[14,8,1,1]{0,1,3,2:T(8,128)}, u32[]{:S(2)}) copy-start(f32[14,8,1,1]{0,1,3,2:T(8,128)} %constant.80) | copy-start | bytes 1348
  54.4 13.2 %copy-start.4 = (bf16[4,12,16,512]{3,2,1,0:T(8,128)(2,1)}, bf16[4,12,16,512]{3,2,1,0:T(8,128)(2,1)S(1)}, u32[]{:S(2)}) copy-start(bf16[4,12,16,512]{3,2,1,0:T(8,128)(2,1)S(1)} %all_to_all.16) | copy-start | bytes 2359300
  55.3 29.9 %collective-permute-start.5 = (bf16[4,12,2,512]{3,2,1,0:T(2,128)(2,1)}, bf16[4,12,2,512]{3,2,1,0:T(2,128)(2,1)}, u32[]{:S(2)}, u32[]{:S(2)}) collective-permute-start(bf16[4,12,2,512]{3,2,1,0:T(2,128)(2,1)} %get-tuple-element.67), channel_id=1, source_target_pairs={{4,0},{8,4},{12,8},{16,12},{20,16},{24,20},{28,24},{0,28},{5,1},{9... | collective-permute-start | bytes 294920 | tf_op jit(solution)/shard_map/ppermute | solution.py:38
  57.7 27.6 %collective-permute-start.4 = (bf16[4,12,2,512]{3,2,1,0:T(2,128)(2,1)}, bf16[4,12,2,512]{3,2,1,0:T(2,128)(2,1)}, u32[]{:S(2)}, u32[]{:S(2)}) collective-permute-start(bf16[4,12,2,512]{3,2,1,0:T(2,128)(2,1)} %get-tuple-element.66), channel_id=1, source_target_pairs={{0,4},{4,8},{8,12},{12,16},{16,20},{20,24},{24,28},{28,0},{1,5},{5... | collective-permute-start | bytes 294920 | tf_op jit(solution)/shard_map/ppermute | solution.py:35
  78.8 6.5 %copy-start.5 = (bf16[4,12,16,512]{3,2,1,0:T(8,128)(2,1)S(1)}, bf16[4,12,16,512]{3,2,1,0:T(8,128)(2,1)}, u32[]{:S(2)}) copy-start(bf16[4,12,16,512]{3,2,1,0:T(8,128)(2,1)} %copy-done.4) | copy-start | bytes 2359300
  87.0 37.4 %collective-permute-start.7 = (bf16[4,2,20,512]{3,2,1,0:T(8,128)(2,1)}, bf16[4,2,20,512]{3,2,1,0:T(8,128)(2,1)}, u32[]{:S(2)}, u32[]{:S(2)}) collective-permute-start(bf16[4,2,20,512]{3,2,1,0:T(8,128)(2,1)} %get-tuple-element.65), channel_id=1, source_target_pairs={{1,0},{2,1},{3,2},{0,3},{5,4},{6,5},{7,6},{4,7},{9,8},{10,9},{11,1... | collective-permute-start | bytes 491528 | tf_op jit(solution)/shard_map/ppermute | solution.py:38
  90.5 33.9 %collective-permute-start.6 = (bf16[4,2,20,512]{3,2,1,0:T(8,128)(2,1)}, bf16[4,2,20,512]{3,2,1,0:T(8,128)(2,1)}, u32[]{:S(2)}, u32[]{:S(2)}) collective-permute-start(bf16[4,2,20,512]{3,2,1,0:T(8,128)(2,1)} %get-tuple-element.64), channel_id=1, source_target_pairs={{0,1},{1,2},{2,3},{3,0},{4,5},{5,6},{6,7},{7,4},{8,9},{9,10},{10,1... | collective-permute-start | bytes 491528 | tf_op jit(solution)/shard_map/ppermute | solution.py:35
  95.3 1.1 copy-start.7
  102.0 1.2 copy-start.9
  111.4 5.8 %copy-start.8 = (f32[14,48,4,128]{3,2,1,0:T(4,128)S(1)}, f32[14,48,4,128]{3,2,1,0:T(4,128)}, u32[]{:S(2)}) copy-start(f32[14,48,4,128]{3,2,1,0:T(4,128)} %copy-done.7) | copy-start | bytes 4128772
  111.4 5.8 %copy-start.10 = (f32[14,48,4,128]{3,2,1,0:T(4,128)S(1)}, f32[14,48,4,128]{3,2,1,0:T(4,128)}, u32[]{:S(2)}) copy-start(f32[14,48,4,128]{3,2,1,0:T(4,128)} %copy-done.9) | copy-start | bytes 4128772
  111.4 5.8 %copy-start.21 = (f32[1,48,4,128]{3,2,1,0:T(4,128)S(1)}, f32[1,48,4,128]{3,2,1,0:T(4,128)}, u32[]{:S(2)}) copy-start(f32[1,48,4,128]{3,2,1,0:T(4,128)} %get-tuple-element.24) | copy-start | bytes 294916
  111.4 5.8 %copy-start.22 = (f32[1,48,4,128]{3,2,1,0:T(4,128)S(1)}, f32[1,48,4,128]{3,2,1,0:T(4,128)}, u32[]{:S(2)}) copy-start(f32[1,48,4,128]{3,2,1,0:T(4,128)} %get-tuple-element.26) | copy-start | bytes 294916
  111.4 6.0 %copy-start.3 = (f32[9,48,16,128]{3,2,1,0:T(8,128)S(1)}, f32[9,48,16,128]{3,2,1,0:T(8,128)}, u32[]{:S(2)}) copy-start(f32[9,48,16,128]{3,2,1,0:T(8,128)} %slice.706) | copy-start | bytes 10616836
  111.4 6.0 %slice-start.2 = ((f32[14,48,4,128]{3,2,1,0:T(4,128)}), f32[9,48,4,128]{3,2,1,0:T(4,128)S(1)}, s32[]{:S(2)}) async-start(f32[14,48,4,128]{3,2,1,0:T(4,128)} %copy-done.7), calls=%async_computation.3 | async-start | bytes 1769472 | tf_op jit(solution)/shard_map/slice | solution.py:94
  111.4 6.0 %slice-start.3 = ((f32[14,48,4,128]{3,2,1,0:T(4,128)}), f32[9,48,4,128]{3,2,1,0:T(4,128)S(1)}, s32[]{:S(2)}) async-start(f32[14,48,4,128]{3,2,1,0:T(4,128)} %copy-done.9), calls=%async_computation.4 | async-start | bytes 1769472 | tf_op jit(solution)/shard_map/slice | solution.py:94
  111.4 6.0 %copy-start.11 = (f32[3,48,16,128]{3,2,1,0:T(8,128)S(1)}, f32[3,48,16,128]{3,2,1,0:T(8,128)}, u32[]{:S(2)}) copy-start(f32[3,48,16,128]{3,2,1,0:T(8,128)} %get-tuple-element.73) | copy-start | bytes 3538948
  111.4 6.0 %copy-start.12 = (f32[1,48,16,128]{3,2,1,0:T(8,128)S(1)}, f32[1,48,16,128]{3,2,1,0:T(8,128)}, u32[]{:S(2)}) copy-start(f32[1,48,16,128]{3,2,1,0:T(8,128)} %get-tuple-element.38) | copy-start | bytes 1179652
  111.5 6.0 %copy-start.13 = (f32[1,48,16,128]{3,2,1,0:T(8,128)S(1)}, f32[1,48,16,128]{3,2,1,0:T(8,128)}, u32[]{:S(2)}) copy-start(f32[1,48,16,128]{3,2,1,0:T(8,128)} %get-tuple-element.39) | copy-start | bytes 1179652
  111.5 6.0 %copy-start.17 = (f32[1,48,4,128]{3,2,1,0:T(4,128)S(1)}, f32[1,48,4,128]{3,2,1,0:T(4,128)}, u32[]{:S(2)}) copy-start(f32[1,48,4,128]{3,2,1,0:T(4,128)} %get-tuple-element.23) | copy-start | bytes 294916
  111.5 6.0 %copy-start.18 = (f32[1,48,4,128]{3,2,1,0:T(4,128)S(1)}, f32[1,48,4,128]{3,2,1,0:T(4,128)}, u32[]{:S(2)}) copy-start(f32[1,48,4,128]{3,2,1,0:T(4,128)} %get-tuple-element.59) | copy-start | bytes 294916
  111.5 6.0 %copy-start.19 = (f32[1,48,4,128]{3,2,1,0:T(4,128)S(1)}, f32[1,48,4,128]{3,2,1,0:T(4,128)}, u32[]{:S(2)}) copy-start(f32[1,48,4,128]{3,2,1,0:T(4,128)} %get-tuple-element.25) | copy-start | bytes 294916
  111.5 6.0 %copy-start.20 = (f32[1,48,4,128]{3,2,1,0:T(4,128)S(1)}, f32[1,48,4,128]{3,2,1,0:T(4,128)}, u32[]{:S(2)}) copy-start(f32[1,48,4,128]{3,2,1,0:T(4,128)} %get-tuple-element.60) | copy-start | bytes 294916
  113.3 21.9 %collective-permute-start.2 = (f32[14,48,24,4]{1,2,3,0:T(8,128)S(1)}, f32[14,48,24,4]{1,2,3,0:T(8,128)S(1)}, u32[]{:S(2)}, u32[]{:S(2)}) collective-permute-start(f32[14,48,24,4]{1,2,3,0:T(8,128)S(1)} %get-tuple-element.31), channel_id=1, source_target_pairs={{1,0},{2,1},{3,2},{0,3},{5,4},{6,5},{7,6},{4,7},{9,8},{10,9},{11,1... | collective-permute-start | bytes 774152 | tf_op jit(solution)/shard_map/ppermute | solution.py:38
  117.1 28.6 %collective-permute-start.3 = (f32[14,48,24,4]{1,2,3,0:T(8,128)S(1)}, f32[14,48,24,4]{1,2,3,0:T(8,128)S(1)}, u32[]{:S(2)}, u32[]{:S(2)}) collective-permute-start(f32[14,48,24,4]{1,2,3,0:T(8,128)S(1)} %get-tuple-element.32), channel_id=1, source_target_pairs={{0,1},{1,2},{2,3},{3,0},{4,5},{5,6},{6,7},{7,4},{8,9},{9,10},{10,1... | collective-permute-start | bytes 774152 | tf_op jit(solution)/shard_map/ppermute | solution.py:35
  117.5 6.9 %copy-start.6 = (bf16[4,12,16,512]{3,2,1,0:T(8,128)(2,1)S(1)}, bf16[4,12,16,512]{3,2,1,0:T(8,128)(2,1)}, u32[]{:S(2)}) copy-start(bf16[4,12,16,512]{3,2,1,0:T(8,128)(2,1)} %copy-done.4) | copy-start | bytes 2359300
  135.1 12.0 %copy-start.23 = (bf16[5,12,16,512]{3,2,1,0:T(8,128)(2,1)}, bf16[5,12,16,512]{3,2,1,0:T(8,128)(2,1)S(1)}, u32[]{:S(2)}) copy-start(bf16[5,12,16,512]{3,2,1,0:T(8,128)(2,1)S(1)} %bitcast_dynamic-update-slice_fusion) | copy-start | bytes 2949124
where the time goes:
time: 244 us; the launch traced here: 243 us
  other arithmetic  149 us (61%)
  local copies, waits for them, and re-layouts  53.3 us (22%)
  starting transfers between devices  18 us (7%)
  waiting for transfers between devices  10.5 us (4%)
  matrix products  9.88 us (4%)
    add x1, other arithmetic, per_device(): fields_next = fields + SECTION_WEIGHT * register_next  70.2 us
    unnamed x68, local copies, waits for them, and re-layouts  15.9 us
    concatenate x1, other arithmetic, per_device(): extended_y = jnp.concatenate([lower_y, flux_y, upper_y], axis=3)  15.8 us
    ppermute x4, starting transfers between devices, with_halo(): lax.ppermute(lax.slice_in_dim(block, 0, width, axis=dim), axis, backward)  13.1 us
    unnamed x7, other arithmetic  10.6 us
    ppermute x4, waiting for transfers between devices, with_halo(): lax.ppermute(lax.slice_in_dim(block, block.shape[dim] - width, None, axis...  10.5 us
    mul x5, other arithmetic, directed_flux(): base = fields * speed  10.3 us
    dot_general x1, matrix products, per_device(): jnp.tensordot(jnp.asarray(make_table(), jnp.float32), rates, axes=1, prec...  9.88 us
  transfers between devices with their start and end apart: 9, of which 1 were waited for; matrix products, arithmetic and copies ran while one was open for 45% of the time, Pallas kernels for 0%

commit v1 on v0

v1 whole, which is shorter than its diff:
```python
import functools

import jax
import jax.numpy as jnp
import numpy as np
from jax import lax
from jax.experimental import pallas as pl
from jax.experimental.pallas import tpu as pltpu
from jax.sharding import PartitionSpec as P

GAMMA_LESS = 0.4
UNIVERSAL_R = 0.25
TIME_STEP = 0.25
SECTION_DECAY = -0.4178904745
SECTION_WEIGHT = 0.3792103129
GRAD_FLOOR = 0.1
PROGRESS_SCALE = 4.0
CENTRAL_WEIGHTS = (0.8, -0.2, 4.0 / 105.0, -1.0 / 280.0)
WHOLE_WEIGHTS = (672.0, -168.0, 32.0, -3.0)
WHOLE_SCALE = 1.0 / 840.0
MOLAR_MASS = (2.0, 32.0, 16.0, 17.0, 18.0, 1.0, 33.0, 34.0, 28.0)
FORMATION_HEAT = (0.0, 0.0, 2.0, 0.3, -1.5, 3.0, 0.1, -0.4, 0.0)
ARRHENIUS_LIST = (
    (5, 1, (2, 3), 40.0, 2.0),
    (2, 0, (5, 3), 30.0, 1.2),
    (3, 0, (5, 4), 25.0, 0.8),
    (2, 4, (3, 3), 10.0, 1.6),
    (5, 1, (6,), 15.0, 0.2),
    (6, 5, (3, 3), 20.0, 0.3),
    (6, 6, (7, 1), 12.0, 0.4),
    (7, 8, (3, 3, 8), 8.0, 1.8),
)
FIELDS = 14
FLOWS = 5
LAYERS = 4 * FIELDS + FLOWS
MIB = 1 << 20
F32 = jnp.float32
BF16 = jnp.bfloat16


def make_table():
    table = np.zeros((14, 8))
    for column, step in enumerate(ARRHENIUS_LIST):
        change = np.zeros(9)
        change[step[0]] -= 1.0
        change[step[1]] -= 1.0
        for product in step[2]:
            change[product] += 1.0
        for species in range(9):
            mass_change = MOLAR_MASS[species] / 18.0 * change[species]
            table[5 + species, column] = mass_change
            table[4, column] -= FORMATION_HEAT[species] * mass_change
    return table


def ring(axis):
    count = lax.axis_size(axis)
    forward = [(i, (i + 1) % count) for i in range(count)]
    backward = [(target, source) for source, target in forward]
    return forward, backward


def lane_cell(lane):
    place = lane % 64
    return place % 4 if place < 4 * FIELDS else 0


def face_matrix():
    weights = np.zeros((128, 128), np.float32)
    for lane in range(64):
        cell = lane_cell(lane)
        for k in range(4 - cell):
            weights[k, lane] = WHOLE_WEIGHTS[k + cell]
            weights[127 - k, 64 + lane] = -WHOLE_WEIGHTS[k + cell]
    return np.concatenate([weights, weights], axis=0)


def place_matrix():
    weights = np.zeros((128, 128), np.float32)
    for lane in range(64):
        cell = lane_cell(lane)
        weights[lane, 127 - cell] = 1.0
        weights[64 + lane, cell] = 1.0
    return weights


def line_matrix():
    weights = np.zeros((128, 128), np.float32)
    for out in range(128):
        for m in range(1, 5):
            if out + m < 128:
                weights[out + m, out] = WHOLE_WEIGHTS[m - 1]
            if out - m >= 0:
                weights[out - m, out] = -WHOLE_WEIGHTS[m - 1]
    return np.concatenate([weights, weights], axis=0)


def lane_mask(field):
    lanes = lax.broadcasted_iota(jnp.int32, (1, 128), 1) % 64
    mask = (lanes >= 4 * field) & (lanes < 4 * field + 4)
    if field < FLOWS:
        mask = mask | (lanes == 4 * FIELDS + field)
    return mask


def two_terms(value):
    high = value.astype(BF16)
    low = (value - high.astype(F32)).astype(BF16)
    return high, low


def in_vmem(count):
    return [pl.BlockSpec(memory_space=pltpu.VMEM)] * count


def in_hbm(count):
    return [pl.BlockSpec(memory_space=pltpu.HBM)] * count


def wrapped(start, size, depth):
    pieces = []
    at = start
    while at < start + size:
        inside = at % depth
        length = min(start + size - at, depth - inside)
        pieces.append(((at - start) * 16, length * 16, inside * 16))
        at += length
    return pieces


def front_kernel(
    count, fields_ref, flat, prim, main_ref, low_edge_ref, high_edge_ref, low_ref, high_ref, progress, edge, arrived
):
    rows = flat.shape[1]
    depth = rows // 16
    own = depth // count
    chunk = 256

    def arrival(step):
        there = pl.ds(pl.multiple_of(step * chunk, chunk), chunk)
        return pltpu.make_async_copy(
            fields_ref.at[:, there, :], flat.at[:, there, :], arrived.at[step]
        )

    for step in range(rows // chunk):
        arrival(step).start()

    def chunk_body(step, carry):
        arrival(step).wait()

        def fill(part, inner_carry):
            at = pl.ds(pl.multiple_of(step * chunk + part * 64, 64), 64)
            density = flat[0, at, :]
            mx, my, mz, energy = [flat[c, at, :] for c in range(1, 5)]
            u, v, w = mx / density, my / density, mz / density
            stress = GAMMA_LESS * (energy - 0.5 * (mx * u + my * v + mz * w))
            progress[at, :] = PROGRESS_SCALE * (flat[9, at, :] / density)
            prim[0, at, :] = u
            prim[1, at, :] = v
            prim[2, at, :] = w
            prim[3, at, :] = stress
            flat[4, at, :] = energy + stress
            return inner_carry

        lax.fori_loop(0, chunk // 64, fill, 0)
        planes = pl.ds(pl.multiple_of(step * 16, 16), 16)

        def layer(ref, index, x):
            return ref[index, pl.ds(step * chunk + x, 16, stride=16), :]

        for ref, layers, sign in ((low_ref, (0, 1, 2, 3), 1.0), (high_ref, (15, 14, 13, 12), -1.0)):
            speeds = [layer(prim, 0, x) for x in layers]
            for field in range(FIELDS):
                flux = [layer(flat, field, x) * speeds[k] for k, x in enumerate(layers)]
                if field == 1:
                    flux = [flux[k] + layer(prim, 3, x) for k, x in enumerate(layers)]
                for cell in range(4):
                    part = (sign * CENTRAL_WEIGHTS[cell]) * flux[0]
                    for k in range(1, 4 - cell):
                        part = part + (sign * CENTRAL_WEIGHTS[k + cell]) * flux[k]
                    high, low = two_terms(part)
                    ref[4 * field + cell, planes, :] = high
                    if cell == 0 and field < FLOWS:
                        ref[4 * FIELDS + field, planes, :] = low
        return carry

    lax.fori_loop(0, rows // chunk, chunk_body, 0)

    edge[...] = jnp.zeros(edge.shape, F32)
    for j in range(count):
        offset = 0
        for c in range(4):
            margin = 2 if c == 0 else 1
            for to, length, source in wrapped(own * j - margin, own + 2 * margin, depth):
                piece = progress[source : source + length, :] if c == 0 else prim[c - 1, source : source + length, :]
                main_ref[j, offset + to : offset + to + length, :] = piece.astype(BF16)
            offset += (own + 2 * margin) * 16
        for ref, first, second in ((low_edge_ref, 0, 1), (high_edge_ref, 15, 14)):
            for to, length, source in wrapped(own * j - 1, own + 2, depth):
                edge[to // 16 : (to + length) // 16, :] = progress[pl.ds(source + first, length // 16, stride=16), :]
            edge[own + 2 : 2 * own + 2, :] = progress[pl.ds(own * j * 16 + second, own, stride=16), :]
            for c in range(3):
                start = (c + 2) * own + 2
                edge[start : start + own, :] = prim[c, pl.ds(own * j * 16 + first, own, stride=16), :]
            ref[j, :, :] = edge[...].astype(BF16)


def front_part(fields, count):
    rows = fields.shape[1]
    depth = rows // 16
    own = depth // count
    main_rows = (4 * own + 10) * 16
    edge_rows = -(-(5 * own + 2) // 16) * 16
    return pl.pallas_call(
        functools.partial(front_kernel, count),
        in_specs=in_hbm(1),
        out_specs=in_vmem(7),
        out_shape=[
            jax.ShapeDtypeStruct((FIELDS, rows, 128), F32),
            jax.ShapeDtypeStruct((4, rows, 128), F32),
            jax.ShapeDtypeStruct((count, main_rows, 128), BF16),
            jax.ShapeDtypeStruct((count, edge_rows, 128), BF16),
            jax.ShapeDtypeStruct((count, edge_rows, 128), BF16),
            jax.ShapeDtypeStruct((LAYERS, depth, 128), BF16),
            jax.ShapeDtypeStruct((LAYERS, depth, 128), BF16),
        ],
        scratch_shapes=[
            pltpu.VMEM((rows, 128), F32),
            pltpu.VMEM((edge_rows, 128), F32),
            pltpu.SemaphoreType.DMA((rows // 256,)),
        ],
        compiler_params=pltpu.CompilerParams(vmem_limit_bytes=40 * MIB),
        cost_estimate=pl.CostEstimate(flops=100 * rows * 128, bytes_accessed=10 * MIB, transcendentals=0),
        name="front_part",
    )(fields)


def lines_kernel(flat, prim, weights_ref, terms, low_ref, high_ref, total):
    rows = flat.shape[1]
    half = rows // 2

    def fill(step, carry):
        at = pl.ds(pl.multiple_of(step * 32, 32), 32)
        v = prim[1, at, :]
        for field in range(FIELDS):
            flux = flat[field, at, :] * v
            if field == 2:
                flux = flux + prim[3, at, :]
            high, low = two_terms(flux)
            terms[field, at, 0:128] = high
            terms[field, at, 128:256] = low
        return carry

    lax.fori_loop(0, rows // 32, fill, 0)
    weights = weights_ref[...]
    for field in range(FIELDS):
        product = jnp.dot(terms[field], weights, preferred_element_type=F32)
        if field == 0:
            total[...] = product
        else:
            total[...] = jnp.where(lane_mask(field), product, total[...])
    value = total[...] * WHOLE_SCALE
    lanes = lax.broadcasted_iota(jnp.int32, (1, 128), 1)
    second = lanes % 64 >= 4 * FIELDS
    value = jnp.where(second, value - value.astype(BF16).astype(F32), value)
    turned = pltpu.roll(value, 64, 1)
    low_ref[...] = jnp.where(lanes < 64, value[0:half, :], turned[half:rows, :]).astype(BF16)
    high_ref[...] = jnp.where(lanes < 64, turned[0:half, :], value[half:rows, :]).astype(BF16)


def lines_part(flat, prim):
    rows = flat.shape[1]
    return pl.pallas_call(
        lines_kernel,
        in_specs=in_vmem(3),
        out_specs=in_vmem(3),
        out_shape=[
            jax.ShapeDtypeStruct((FIELDS, rows, 256), BF16),
            jax.ShapeDtypeStruct((rows // 2, 128), BF16),
            jax.ShapeDtypeStruct((rows // 2, 128), BF16),
        ],
        scratch_shapes=[pltpu.VMEM((rows, 128), F32)],
        compiler_params=pltpu.CompilerParams(vmem_limit_bytes=40 * MIB),
        cost_estimate=pl.CostEstimate(flops=300 * rows * 128, bytes_accessed=8 * MIB, transcendentals=0),
        name="lines_part",
    )(flat, prim, jnp.asarray(face_matrix(), BF16))


def sources(species, stress):
    moles = [species[k] * (18.0 / MOLAR_MASS[k]) for k in range(9)]
    summed = moles[0]
    for k in range(1, 9):
        summed = summed + moles[k]
    inverse_heat = UNIVERSAL_R * summed / stress
    e02 = jnp.exp(-0.2 * inverse_heat)
    e03 = jnp.exp(-0.3 * inverse_heat)
    e04 = e02 * e02
    e08 = e04 * e04
    e16 = e08 * e08
    powers = {0.2: e02, 0.3: e03, 0.4: e04, 0.8: e08, 1.6: e16}
    powers[1.2] = e08 * e04
    powers[1.8] = e16 * e02
    powers[2.0] = e16 * e04
    rates = [
        (step[3] * powers[step[4]]) * (moles[step[0]] * moles[step[1]]) for step in ARRHENIUS_LIST
    ]
    table = make_table()
    result = []
    for field in range(FIELDS):
        value = None
        for column in range(8):
            factor = float(table[field, column])
            if factor != 0.0:
                term = (TIME_STEP * factor) * rates[column]
                value = term if value is None else value + term
        result.append(value)
    return result


def windowed(flux, first, planes):
    window = {z: flux(z) for z in range(first - 4, first + 4)}
    for z in range(first, first + planes):
        window[z + 4] = flux(z + 4)
        change = None
        for m, weight in enumerate(CENTRAL_WEIGHTS, 1):
            term = (-TIME_STEP * weight) * (window[z + m] - window[z - m])
            change = term if change is None else change + term
        yield z, change


def inner_kernel(flat, prim, register, terms, line_ref, out, flux_x, along_y):
    rows = flat.shape[1]
    depth = rows // 16
    flux_x[:, 0:8, :] = jnp.zeros((depth, 8, 128), F32)
    flux_x[:, 24:32, :] = jnp.zeros((depth, 8, 128), F32)

    def react(step, carry):
        at = pl.ds(pl.multiple_of(step * 32, 32), 32)
        made = sources([flat[5 + k, at, :] for k in range(9)], prim[3, at, :])
        for field in range(FIELDS):
            kept = SECTION_DECAY * register[field, at, :]
            out[field, at, :] = kept if made[field] is None else kept + made[field]
        return carry

    lax.fori_loop(0, rows // 32, react, 0)

    def spread(field, flux, extra):
        for z in range(depth):
            flux_x[z, 8:24, :] = flux(0, z * 16, 16)
        for first in range(0, depth, 16):
            for tile in range(2):
                row = 8 * tile
                for z, change in windowed(lambda z: flux(2, (z % depth) * 16 + row, 8), first, 16):
                    for m, weight in enumerate(CENTRAL_WEIGHTS, 1):
                        at = 8 + row
                        change = change + (-TIME_STEP * weight) * (
                            flux_x[z, at + m : at + m + 8, :] - flux_x[z, at - m : at - m + 8, :]
                        )
                    extra(z * 16 + row, change)

    def across(field, carry):
        along_y[...] = jnp.dot(terms[field], line_ref[...], preferred_element_type=F32)

        def flux(direction, row, size):
            return flat[field, row : row + size, :] * prim[direction, row : row + size, :]

        def extra(row, change):
            at = slice(row, row + 8)
            out[field, at, :] += change + (-TIME_STEP * WHOLE_SCALE) * along_y[at, :]

        spread(field, flux, extra)
        return carry

    lax.fori_loop(0, FIELDS, across, 0)

    for z in range(depth):
        flux_x[z, 8:24, :] = prim[3, z * 16 : z * 16 + 16, :]
    for first in range(0, depth, 16):
        for tile in range(2):
            row = 8 * tile

            def stress(z):
                at = (z % depth) * 16 + row
                return prim[3, at : at + 8, :]

            for z, change in windowed(stress, first, 16):
                at = slice(z * 16 + row, z * 16 + row + 8)
                out[3, at, :] += change
                change = None
                for m, weight in enumerate(CENTRAL_WEIGHTS, 1):
                    low = 8 + row
                    term = (-TIME_STEP * weight) * (
                        flux_x[z, low + m : low + m + 8, :] - flux_x[z, low - m : low - m + 8, :]
                    )
                    change = term if change is None else change + term
                out[1, at, :] += change


def inner_part(flat, prim, register, terms):
    rows = flat.shape[1]
    depth = rows // 16
    return pl.pallas_call(
        inner_kernel,
        in_specs=in_vmem(5),
        out_specs=pl.BlockSpec(memory_space=pltpu.VMEM),
        out_shape=jax.ShapeDtypeStruct((FIELDS, rows, 128), F32),
        scratch_shapes=[
            pltpu.VMEM((depth, 32, 128), F32),
            pltpu.VMEM((rows, 128), F32),
        ],
        compiler_params=pltpu.CompilerParams(vmem_limit_bytes=40 * MIB),
        cost_estimate=pl.CostEstimate(
            flops=2000 * rows * 128, bytes_accessed=20 * MIB, transcendentals=10 * rows * 128
        ),
        name="inner_part",
    )(flat, prim, register, terms, jnp.asarray(line_matrix(), BF16))


def outer_kernel(
    part, flat, prim, prev, following, yprev, ynext, place_ref, fields_out, register_out,
    faces_x, along_y, message, fields_stage, register_stage, sent,
):
    rows = part.shape[1]
    depth = rows // 16
    half = rows // 2
    lanes = lax.broadcasted_iota(jnp.int32, (1, 128), 1)
    low = ynext[...].astype(F32)
    high = yprev[...].astype(F32)
    message[0:half, :] = jnp.where(lanes < 64, low, pltpu.roll(high, 64, 1)).astype(BF16)
    message[half:rows, :] = jnp.where(lanes < 64, pltpu.roll(low, 64, 1), high).astype(BF16)
    faces_x[...] = jnp.zeros(faces_x.shape, F32)
    place = place_ref[...]
    copies = []
    for field in range(FIELDS):
        for ref, layers in ((prev, (0, 1, 2, 3)), (following, (15, 14, 13, 12))):
            for cell, x in enumerate(layers):
                value = ref[4 * field + cell, :, :].astype(F32)
                if cell == 0 and field < FLOWS:
                    value = value + ref[4 * FIELDS + field, :, :].astype(F32)
                faces_x[pl.ds(x, depth, stride=16), :] = value
        held = message[...]
        picked = jnp.where(lane_mask(field), held, jnp.zeros_like(held))
        along_y[...] = jnp.dot(picked, place, preferred_element_type=F32)
        stored = part[field] - TIME_STEP * (along_y[...] + faces_x[...])
        register_stage[field] = stored
        before = flat[field]
        if field == 4:
            before = before - prim[3]
        fields_stage[field] = before + SECTION_WEIGHT * stored
        for index, (stage, ref) in enumerate(((register_stage, register_out), (fields_stage, fields_out))):
            copy = pltpu.make_async_copy(stage.at[field], ref.at[field], sent.at[index, field])
            copy.start()
            copies.append(copy)
    for copy in copies:
        copy.wait()


def outer_part(part, flat, prim, prev, following, yprev, ynext):
    rows = flat.shape[1]
    return pl.pallas_call(
        outer_kernel,
        in_specs=in_vmem(8),
        out_specs=in_hbm(2),
        out_shape=[jax.ShapeDtypeStruct((FIELDS, rows, 128), F32)] * 2,
        scratch_shapes=[
            pltpu.VMEM((rows, 128), F32),
            pltpu.VMEM((rows, 128), F32),
            pltpu.VMEM((rows, 128), BF16),
            pltpu.VMEM((FIELDS, rows, 128), F32),
            pltpu.VMEM((FIELDS, rows, 128), F32),
            pltpu.SemaphoreType.DMA((2, FIELDS)),
        ],
        compiler_params=pltpu.CompilerParams(vmem_limit_bytes=40 * MIB),
        cost_estimate=pl.CostEstimate(
            flops=100 * rows * 128, bytes_accessed=24 * MIB, transcendentals=0
        ),
        name="outer_part",
    )(part, flat, prim, prev, following, yprev, ynext, jnp.asarray(place_matrix(), BF16))


def lane_difference(values):
    lanes = lax.broadcasted_iota(jnp.int32, values[0].shape, 1)
    ahead = [pltpu.roll(value, 127, 1) for value in values]
    behind = [pltpu.roll(value, 1, 1) for value in values]
    count = len(values)
    return [
        jnp.where(lanes == 127, ahead[(j + 1) % count], ahead[j])
        - jnp.where(lanes == 0, behind[(j - 1) % count], behind[j])
        for j in range(count)
    ]


def inverse_length(a, b, c):
    return 1.0 * lax.rsqrt(jnp.maximum(a * a + b * b + c * c, GRAD_FLOOR * GRAD_FLOOR))


def metrics_kernel(count, own, blocks, out_ref, scalar, speed, normal, normal_z, edge, stage, sent):
    start_edge = (4 * own + 10) * 16
    half = (blocks.shape[1] - start_edge) // 2
    edge[...] = blocks[:, start_edge:, :].astype(F32)
    for j in range(count):
        for z in range(own + 4):
            scalar[j, pl.ds(z * 32 + 8, 16), :] = blocks[j, z * 16 : z * 16 + 16, :].astype(F32)
        for c in range(3):
            base = (own + 4 + c * (own + 2)) * 16
            for z in range(own + 2):
                speed[c, j, pl.ds(z * 32 + 8, 16), :] = blocks[
                    j, base + z * 16 : base + z * 16 + 16, :
                ].astype(F32)
        for side, row in ((0, 7), (half, 24)):
            scalar[j, pl.ds(32 + row, own + 2, stride=32), :] = edge[j, side : side + own + 2, :]
            for c in range(3):
                start = side + (c + 2) * own + 2
                speed[c, j, pl.ds(32 + row, own, stride=32), :] = edge[j, start : start + own, :]

    for side, inside, row in ((0, 8, 7), (half, 23, 24)):
        sign = 0.5 if row == 7 else -0.5
        lines = [edge[j, side + 1 : side + 1 + own, :] for j in range(count)]
        along_y = lane_difference(lines)
        for j in range(count):
            beyond = edge[j, side + own + 2 : side + 2 * own + 2, :]
            grad_x = sign * (scalar[j, pl.ds(64 + inside, own, stride=32), :] - beyond)
            grad_y = 0.5 * along_y[j]
            grad_z = 0.5 * (edge[j, side + 2 : side + 2 + own, :] - edge[j, side : side + own, :])
            normal[0, j, pl.ds(32 + row, own, stride=32), :] = -grad_x * inverse_length(
                grad_x, grad_y, grad_z
            )

    def window(z, row):
        return pl.ds(pl.multiple_of(z * 32, 32) + row, 16)

    def find_normals(z, carry):
        along_y = lane_difference([scalar[j, window(z + 1, 8), :] for j in range(count)])
        for j in range(count):
            grad_x = 0.5 * (scalar[j, window(z + 1, 9), :] - scalar[j, window(z + 1, 7), :])
            grad_y = 0.5 * along_y[j]
            grad_z = 0.5 * (scalar[j, window(z + 2, 8), :] - scalar[j, window(z, 8), :])
            scale = -inverse_length(grad_x, grad_y, grad_z)
            normal[0, j, window(z, 8), :] = grad_x * scale
            normal[1, j, window(z, 8), :] = grad_y * scale
            normal_z[j, z, :, :] = grad_z * scale
        return carry

    lax.fori_loop(0, own + 2, find_normals, 0)

    def find_metrics(z, carry):
        curve_y = lane_difference([normal[1, j, window(z + 1, 8), :] for j in range(count)])
        speed_y = [
            lane_difference([speed[c, j, window(z + 1, 8), :] for j in range(count)])
            for c in range(3)
        ]
        for j in range(count):
            lanes = slice(j * 128, j * 128 + 128)
            normals = [
                normal[0, j, window(z + 1, 8), :],
                normal[1, j, window(z + 1, 8), :],
                normal_z[j, z + 1, :, :],
            ]
            curvature = 0.5 * (
                (normal[0, j, window(z + 1, 9), :] - normal[0, j, window(z + 1, 7), :])
                + curve_y[j]
                + (normal_z[j, z + 2, :, :] - normal_z[j, z, :, :])
            )
            strain = None
            for c in range(3):
                slopes = [
                    speed[c, j, window(z + 1, 9), :] - speed[c, j, window(z + 1, 7), :],
                    speed_y[c][j],
                    speed[c, j, window(z + 2, 8), :] - speed[c, j, window(z, 8), :],
                ]
                along = normals[0] * slopes[0] + normals[1] * slopes[1] + normals[2] * slopes[2]
                term = slopes[c] - normals[c] * along
                strain = term if strain is None else strain + term
            for index, value in enumerate(normals + [curvature, 0.5 * strain]):
                stage[index, z, :, lanes] = value.astype(BF16)
        pltpu.make_async_copy(stage.at[:, z], out_ref.at[:, z], sent.at[z]).start()
        return carry

    lax.fori_loop(0, own, find_metrics, 0)
    for z in range(own):
        pltpu.make_async_copy(stage.at[:, z], out_ref.at[:, z], sent.at[z]).wait()


def metrics_part(blocks, own):
    count = blocks.shape[0]
    half = (blocks.shape[1] - (4 * own + 10) * 16) // 2
    shape = (5, own, 16, count * 128)
    return pl.pallas_call(
        functools.partial(metrics_kernel, count, own),
        in_specs=in_vmem(1),
        out_specs=in_hbm(1)[0],
        out_shape=jax.ShapeDtypeStruct(shape, BF16),
        scratch_shapes=[
            pltpu.VMEM((count, (own + 4) * 32, 128), F32),
            pltpu.VMEM((3, count, (own + 2) * 32, 128), F32),
            pltpu.VMEM((2, count, (own + 2) * 32, 128), F32),
            pltpu.VMEM((count, own + 2, 16, 128), F32),
            pltpu.VMEM((count, 2 * half, 128), F32),
            pltpu.VMEM(shape, BF16),
            pltpu.SemaphoreType.DMA((own,)),
        ],
        compiler_params=pltpu.CompilerParams(vmem_limit_bytes=40 * MIB),
        cost_estimate=pl.CostEstimate(
            flops=300 * own * 16 * 128 * count, bytes_accessed=3 * MIB, transcendentals=0
        ),
        name="flame_metrics",
    )(blocks)


def per_device(fields, register):
    depth, count_x, count_y = fields.shape[1:]
    flat = fields.reshape(FIELDS, depth * count_x, count_y)
    count = lax.axis_size("gy")
    own = depth // count
    x_forward, x_backward = ring("gx")
    y_forward, y_backward = ring("gy")

    flat, prim, main, edge_low, edge_high, low, high = front_part(flat, count)
    edge_prev = lax.ppermute(edge_high, "gx", x_forward)
    edge_next = lax.ppermute(edge_low, "gx", x_backward)
    following = lax.ppermute(low, "gx", x_backward)
    prev = lax.ppermute(high, "gx", x_forward)
    terms, ylow, yhigh = lines_part(flat, prim)
    blocks = lax.all_to_all(
        jnp.concatenate([main, edge_prev, edge_next], axis=1), "gy", 0, 0, tiled=True
    )
    ynext = lax.ppermute(ylow, "gy", y_backward)
    yprev = lax.ppermute(yhigh, "gy", y_forward)
    part = inner_part(flat, prim, register.reshape(flat.shape), terms)
    fields_next, register_next = outer_part(part, flat, prim, prev, following, yprev, ynext)
    metrics = metrics_part(blocks, own)
    return (fields_next.reshape(fields.shape), register_next.reshape(fields.shape), metrics)


def solution(mesh):
    in_specs = (P(None, None, "gx", "gy"), P(None, None, "gx", "gy"))
    out_specs = (P(None, None, "gx", "gy"), P(None, None, "gx", "gy"), P(None, "gy", "gx", None))
    return jax.shard_map(
        per_device, mesh=mesh, in_specs=in_specs, out_specs=out_specs, check_vma=False
    )
```

time: 244 us -> 59.7 us (0.24)
  other arithmetic: 149 us -> 1.06 us
  local copies, waits for them, and re-layouts: 53.3 us -> 8.32 us
  Pallas kernels: 0 us -> 31.9 us
  matrix products: 9.88 us -> 0 us
  waiting for transfers between devices: 10.5 us -> 1.96 us
  starting transfers between devices: 18 us -> 15.4 us
    add x8 -> x0, other arithmetic: 75.8 us -> none  [the longest x1 70.2 us: per_device(): fields_next = fields + SECTION_WEIGHT * register_next]
    pallas_call x0 -> x5, Pallas kernels: none -> 31.9 us  [the longest x1 15.7 us: inner_part(): pl.pallas_call(inner_kernel, in_specs=in_vmem(5), out_specs=pl.BlockSpec(...]
    concatenate x5 -> x1, other arithmetic: 31.9 us -> 1.06 us  [per_device(): jnp.concatenate([main, edge_prev, edge_next], axis=1)]
    ppermute x4 -> x0, local copies, waits for them, and re-layouts: 11.9 us -> none  [the longest x2 5.95 us: with_halo(): lax.ppermute(lax.slice_in_dim(block, 0, width, axis=dim), axis, backward)]
    slice x11 -> x0, local copies, waits for them, and re-layouts: 11 us -> none  [the longest x9 6.73 us: directed_flux(): return jnp.concatenate([base[0:1], moment, energy, base[5:]], axis=0)]
    unnamed x7 -> x0, other arithmetic: 10.6 us -> none
    slice x5 -> x0, other arithmetic: 10.5 us -> none  [the longest x3 7.05 us: directed_flux(): return jnp.concatenate([base[0:1], moment, energy, base[5:]], axis=0)]
    concatenate x3 -> x0, local copies, waits for them, and re-layouts: 10.4 us -> none  [the longest x2 9.24 us: directed_flux(): return jnp.concatenate([base[0:1], moment, energy, base[5:]], axis=0)]
  transfers between devices with their start and end apart: 9 -> 7, of which waited for: 1 -> 1; matrix products, arithmetic and copies ran while one was open for 45% -> 0% of each run, Pallas kernels for 0% -> 41%
where the time goes in v1:
time: 59.7 us; the launch traced here: 59.4 us
  Pallas kernels  31.9 us (53%)
  starting transfers between devices  15.4 us (26%)
  local copies, waits for them, and re-layouts  8.32 us (14%)
  waiting for transfers between devices  1.96 us (3%)
  other arithmetic  1.06 us (2%)
  between operations  0.73 us (1%)
    pallas_call x1, Pallas kernels, inner_part(): pl.pallas_call(inner_kernel, in_specs=in_vmem(5), out_specs=pl.BlockSpec(...  15.7 us
    unnamed x14, local copies, waits for them, and re-layouts  8.32 us
    all_to_all x1, starting transfers between devices, per_device(): lax.all_to_all(jnp.concatenate([main, edge_prev, edge_next], axis=1), 'gy...  5.63 us
    pallas_call x1, Pallas kernels, outer_part(): pl.pallas_call(outer_kernel, in_specs=in_vmem(8), out_specs=in_hbm(2), ou...  5.41 us
    pallas_call x1, Pallas kernels, metrics_part(): pl.pallas_call(functools.partial(metrics_kernel, count, own), in_specs=in...  4.53 us
    pallas_call x1, Pallas kernels, front_part(): pl.pallas_call(functools.partial(front_kernel, count), in_specs=in_hbm(1)...  3.36 us
    pallas_call x1, Pallas kernels, lines_part(): pl.pallas_call(lines_kernel, in_specs=in_vmem(3), out_specs=in_vmem(3), o...  2.9 us
    ppermute x1, starting transfers between devices, per_device(): edge_next = lax.ppermute(edge_low, 'gx', x_backward)  2.88 us
  transfers between devices with their start and end apart: 7, of which 1 were waited for; matrix products, arithmetic and copies ran while one was open for 0% of the time, Pallas kernels for 41%

profile of v1, /device:TPU:0, one launch (start us, length us, event | category | flops | bytes accessed | tf_op | source)
XLA Modules:
  0.0 59.4 jit_solution(7919202053263048189)
XLA Ops:
  0.6 3.4 %front_part.1 = (f32[14,768,128]{2,1,0:T(8,128)S(1)}, f32[4,768,128]{2,1,0:T(8,128)S(1)}, bf16[4,928,128]{2,1,0:T(8,128)(2,1)S(1)}, bf16[4,64,128]{2,1,0:T(8,128...) custom-call(f32[14,768,128]{2,1,0:T(8,128)} %bitcast.5), custom_call_target="tpu_custom_call" | custom-call | flops 9830400 | bytes 10485760 | tf_op jit(solution)/shard_map/front_part/pallas_call | solution.py:214
  4.0 0.0 copy-start
  4.0 2.4 %copy-done = f32[14,768,128]{2,1,0:T(8,128)} copy-done((f32[14,768,128]{2,1,0:T(8,128)}, f32[14,768,128]{2,1,0:T(8,128)S(1)}, u32[]{:S(2)}) %copy-start) | copy-done | bytes 5505048
  6.4 0.0 copy-start.6
  6.5 0.9 %copy-done.6 = bf16[61,48,128]{2,1,0:T(8,128)(2,1)} copy-done((bf16[61,48,128]{2,1,0:T(8,128)(2,1)}, bf16[61,48,128]{2,1,0:T(8,128)(2,1)S(1)}, u32[]{:S(2)}) %copy-start.6) | copy-done | bytes 749592
  7.3 0.5 collective-permute-start.4
  7.8 2.9 %collective-permute-start.5 = (bf16[4,64,128]{2,1,0:T(8,128)(2,1)S(1)}, bf16[4,64,128]{2,1,0:T(8,128)(2,1)S(1)}, u32[]{:S(2)}, u32[]{:S(2)}) collective-permute-start(bf16[4,64,128]{2,1,0:T(8,128)(2,1)S(1)} %get-tuple-element.26), channel_id=1, source_target_pairs={{4,0},{8,4},{12,8},{16,12},{20,16},{24,20},{28,24},{0,28},{5,1},{9... | collective-permute-start | bytes 196616 | tf_op jit(solution)/shard_map/ppermute | solution.py:620
  10.7 1.9 %collective-permute-done.4 = bf16[4,64,128]{2,1,0:T(8,128)(2,1)S(1)} collective-permute-done((bf16[4,64,128]{2,1,0:T(8,128)(2,1)S(1)}, bf16[4,64,128]{2,1,0:T(8,128)(2,1)S(1)}, u32[]{:S(2)}, u32[]{:S(2)}) %collective-permute-start.4) | collective-permute-done | bytes 65568 | tf_op jit(solution)/shard_map/ppermute | solution.py:619
  12.6 0.0 collective-permute-done.5
  12.6 0.0 copy-start.4
  12.6 1.1 %pad_maximum_fusion = bf16[4,1056,128]{2,1,0:T(8,128)(2,1)} fusion(bf16[4,64,128]{2,1,0:T(8,128)(2,1)S(1)} %collective-permute-done.5, bf16[4,64,128]{2,1,0:T(8,128)(2,1)S(1)} %collective-permute-done.4, bf16[4,928,128]{2,1,0:T(8,128)(2,1)S(1)} %get-tuple-element.24), kind=kLoop, calls=%fused_computation | loop fusion | flops 3244032 | bytes 2162688 | tf_op jit(solution)/shard_map/concatenate | solution.py:625
  13.7 5.6 %all-to-all-start = ((bf16[4,1056,128]{2,1,0:T(8,128)(2,1)}), bf16[4,1056,128]{2,1,0:T(8,128)(2,1)S(1)}, u32[]{:S(2)}, u32[]{:S(2)}) async-start(bf16[4,1056,128]{2,1,0:T(8,128)(2,1)} %pad_maximum_fusion), calls=%async_computation | async-start | bytes 2162688 | tf_op jit(solution)/shard_map/all_to_all | solution.py:624
  19.3 0.4 collective-permute-start
  19.7 2.2 %collective-permute-start.1 = (bf16[61,48,128]{2,1,0:T(8,128)(2,1)S(1)}, bf16[61,48,128]{2,1,0:T(8,128)(2,1)S(1)}, u32[]{:S(2)}, u32[]{:S(2)}) collective-permute-start(bf16[61,48,128]{2,1,0:T(8,128)(2,1)S(1)} %get-tuple-element.19), channel_id=1, source_target_pairs={{4,0},{8,4},{12,8},{16,12},{20,16},{24,20},{28,24},{0,28},{5,1},{9... | collective-permute-start | bytes 2248712 | tf_op jit(solution)/shard_map/ppermute | solution.py:621
  21.9 0.0 copy-done.4
  21.9 0.0 copy-start.1
  21.9 2.6 %copy-done.1 = f32[14,768,128]{2,1,0:T(8,128)S(1)} copy-done((f32[14,768,128]{2,1,0:T(8,128)S(1)}, f32[14,768,128]{2,1,0:T(8,128)}, u32[]{:S(2)}) %copy-start.1) | copy-done | bytes 5505048
  24.5 0.0 copy-start.3
  24.5 2.9 %lines_part.1 = (bf16[14,768,256]{2,1,0:T(8,128)(2,1)S(1)}, bf16[384,128]{1,0:T(8,128)(2,1)S(1)}, bf16[384,128]{1,0:T(8,128)(2,1)S(1)}) custom-call(f32[14,768,128]{2,1,0:T(8,128)S(1)} %copy-done.1, f32[4,768,128]{2,1,0:T(8,128)S(1)} %get-tuple-element.16.prim, bf16[256,128]{1,0:T(8,128)(2,1)S(1)} %copy-done.4), custom_call_target="tpu_custom_call" | custom-call | flops 29491200 | bytes 8388608 | tf_op jit(solution)/shard_map/lines_part/pallas_call | solution.py:273
  27.4 0.0 copy-start.2
  27.4 2.4 %copy-done.2 = bf16[14,768,256]{2,1,0:T(8,128)(2,1)} copy-done((bf16[14,768,256]{2,1,0:T(8,128)(2,1)}, bf16[14,768,256]{2,1,0:T(8,128)(2,1)S(1)}, u32[]{:S(2)}) %copy-start.2) | copy-done | bytes 5505048
  29.9 2.0 %collective-permute-start.2 = (bf16[384,128]{1,0:T(8,128)(2,1)S(1)}, bf16[384,128]{1,0:T(8,128)(2,1)S(1)}, u32[]{:S(2)}, u32[]{:S(2)}) collective-permute-start(bf16[384,128]{1,0:T(8,128)(2,1)S(1)} %get-tuple-element.20), channel_id=1, source_target_pairs={{0,1},{1,2},{2,3},{3,0},{4,5},{5,6},{6,7},{7,4},{8,9},{9,10},{10,1... | collective-permute-start | bytes 294920 | tf_op jit(solution)/shard_map/ppermute | solution.py:628
  31.9 1.8 %collective-permute-start.3 = (bf16[384,128]{1,0:T(8,128)(2,1)S(1)}, bf16[384,128]{1,0:T(8,128)(2,1)S(1)}, u32[]{:S(2)}, u32[]{:S(2)}) collective-permute-start(bf16[384,128]{1,0:T(8,128)(2,1)S(1)} %get-tuple-element.21), channel_id=1, source_target_pairs={{1,0},{2,1},{3,2},{0,3},{5,4},{6,5},{7,6},{4,7},{9,8},{10,9},{11,1... | collective-permute-start | bytes 294920 | tf_op jit(solution)/shard_map/ppermute | solution.py:627
  33.7 0.0 copy-done.3
  33.7 0.0 copy-start.5
  33.7 15.7 %inner_part.1.part = f32[14,768,128]{2,1,0:T(8,128)S(1)} custom-call(f32[14,768,128]{2,1,0:T(8,128)S(1)} %copy-done.1, f32[4,768,128]{2,1,0:T(8,128)S(1)} %get-tuple-element.16.prim, f32[14,768,128]{2,1,0:T(8,128)} %bitcast.4, bf16[14,768,256]{2,1,0:T(8,128)(2,1)} %copy-done.2, bf16[256,128]{1,0:T(8,128)(2,1)S(1)} %copy-done.3), custom_call_target="tpu_custom_call" | custom-call | flops 196608000 | bytes 20971520 | tf_op jit(solution)/shard_map/inner_part/pallas_call | solution.py:402
  49.4 0.0 collective-permute-done.2.yprev
  49.5 0.0 collective-permute-done.3.ynext
  49.5 0.0 collective-permute-done.prev
  49.5 0.0 collective-permute-done.1.following
  49.5 0.0 copy-done.5
  49.5 5.4 %outer_part.1 = (f32[14,768,128]{2,1,0:T(8,128)}, f32[14,768,128]{2,1,0:T(8,128)}) custom-call(f32[14,768,128]{2,1,0:T(8,128)S(1)} %inner_part.1.part, f32[14,768,128]{2,1,0:T(8,128)S(1)} %copy-done.1, f32[4,768,128]{2,1,0:T(8,128)S(1)} %get-tuple-element.16.prim, bf16[61,48,128]{2,1,0:T(8,128)(2,1)S(1)} %collective-permute-done.prev, ...), custom_call_target="tpu_custom_call" | custom-call | flops 9830400 | bytes 25165824 | tf_op jit(solution)/shard_map/outer_part/pallas_call | solution.py:460
  54.9 0.0 all-to-all-done.blocks
  54.9 4.5 %flame_metrics.1 = bf16[5,12,16,512]{3,2,1,0:T(8,128)(2,1)} custom-call(bf16[4,1056,128]{2,1,0:T(8,128)(2,1)S(1)} %all-to-all-done.blocks), custom_call_target="tpu_custom_call" | custom-call | flops 29491200 | bytes 3145728 | tf_op jit(solution)/shard_map/flame_metrics/pallas_call | solution.py:588
Async XLA Ops:
  4.0 2.4 %copy-start = (f32[14,768,128]{2,1,0:T(8,128)}, f32[14,768,128]{2,1,0:T(8,128)S(1)}, u32[]{:S(2)}) copy-start(f32[14,768,128]{2,1,0:T(8,128)S(1)} %get-tuple-element.15.flat) | copy-start | bytes 16515076
  6.4 0.9 %copy-start.6 = (bf16[61,48,128]{2,1,0:T(8,128)(2,1)}, bf16[61,48,128]{2,1,0:T(8,128)(2,1)S(1)}, u32[]{:S(2)}) copy-start(bf16[61,48,128]{2,1,0:T(8,128)(2,1)S(1)} %get-tuple-element.18) | copy-start | bytes 2248708
  7.3 5.3 %collective-permute-start.4 = (bf16[4,64,128]{2,1,0:T(8,128)(2,1)S(1)}, bf16[4,64,128]{2,1,0:T(8,128)(2,1)S(1)}, u32[]{:S(2)}, u32[]{:S(2)}) collective-permute-start(bf16[4,64,128]{2,1,0:T(8,128)(2,1)S(1)} %get-tuple-element.25), channel_id=1, source_target_pairs={{0,4},{4,8},{8,12},{12,16},{16,20},{20,24},{24,28},{28,0},{1,5},{5... | collective-permute-start | bytes 196616 | tf_op jit(solution)/shard_map/ppermute | solution.py:619
  7.8 4.8 %collective-permute-start.5 = (bf16[4,64,128]{2,1,0:T(8,128)(2,1)S(1)}, bf16[4,64,128]{2,1,0:T(8,128)(2,1)S(1)}, u32[]{:S(2)}, u32[]{:S(2)}) collective-permute-start(bf16[4,64,128]{2,1,0:T(8,128)(2,1)S(1)} %get-tuple-element.26), channel_id=1, source_target_pairs={{4,0},{8,4},{12,8},{16,12},{20,16},{24,20},{28,24},{0,28},{5,1},{9... | collective-permute-start | bytes 196616 | tf_op jit(solution)/shard_map/ppermute | solution.py:620
  12.6 9.3 %copy-start.4 = (bf16[256,128]{1,0:T(8,128)(2,1)S(1)}, bf16[256,128]{1,0:T(8,128)(2,1)}, u32[]{:S(2)}) copy-start(bf16[256,128]{1,0:T(8,128)(2,1)} %constant.6.clone.weights_ref) | copy-start | bytes 196612
  13.7 41.2 %all-to-all-start = ((bf16[4,1056,128]{2,1,0:T(8,128)(2,1)}), bf16[4,1056,128]{2,1,0:T(8,128)(2,1)S(1)}, u32[]{:S(2)}, u32[]{:S(2)}) async-start(bf16[4,1056,128]{2,1,0:T(8,128)(2,1)} %pad_maximum_fusion), calls=%async_computation | async-start | bytes 2162688 | tf_op jit(solution)/shard_map/all_to_all | solution.py:624
  19.3 30.2 %collective-permute-start = (bf16[61,48,128]{2,1,0:T(8,128)(2,1)}, bf16[61,48,128]{2,1,0:T(8,128)(2,1)S(1)}, u32[]{:S(2)}, u32[]{:S(2)}) collective-permute-start(bf16[61,48,128]{2,1,0:T(8,128)(2,1)} %copy-done.6), channel_id=1, source_target_pairs={{0,4},{4,8},{8,12},{12,16},{16,20},{20,24},{24,28},{28,0},{1,5},{5... | collective-permute-start | bytes 2248712 | tf_op jit(solution)/shard_map/ppermute | solution.py:622
  19.7 29.8 %collective-permute-start.1 = (bf16[61,48,128]{2,1,0:T(8,128)(2,1)S(1)}, bf16[61,48,128]{2,1,0:T(8,128)(2,1)S(1)}, u32[]{:S(2)}, u32[]{:S(2)}) collective-permute-start(bf16[61,48,128]{2,1,0:T(8,128)(2,1)S(1)} %get-tuple-element.19), channel_id=1, source_target_pairs={{4,0},{8,4},{12,8},{16,12},{20,16},{24,20},{28,24},{0,28},{5,1},{9... | collective-permute-start | bytes 2248712 | tf_op jit(solution)/shard_map/ppermute | solution.py:621
  21.9 2.6 %copy-start.1 = (f32[14,768,128]{2,1,0:T(8,128)S(1)}, f32[14,768,128]{2,1,0:T(8,128)}, u32[]{:S(2)}) copy-start(f32[14,768,128]{2,1,0:T(8,128)} %copy-done) | copy-start | bytes 16515076
  24.5 9.2 %copy-start.3 = (bf16[256,128]{1,0:T(8,128)(2,1)S(1)}, bf16[256,128]{1,0:T(8,128)(2,1)}, u32[]{:S(2)}) copy-start(bf16[256,128]{1,0:T(8,128)(2,1)} %constant.7.clone.line_ref) | copy-start | bytes 196612
  27.4 2.4 %copy-start.2 = (bf16[14,768,256]{2,1,0:T(8,128)(2,1)}, bf16[14,768,256]{2,1,0:T(8,128)(2,1)S(1)}, u32[]{:S(2)}) copy-start(bf16[14,768,256]{2,1,0:T(8,128)(2,1)S(1)} %get-tuple-element.17.terms) | copy-start | bytes 16515076
  29.9 19.6 %collective-permute-start.2 = (bf16[384,128]{1,0:T(8,128)(2,1)S(1)}, bf16[384,128]{1,0:T(8,128)(2,1)S(1)}, u32[]{:S(2)}, u32[]{:S(2)}) collective-permute-start(bf16[384,128]{1,0:T(8,128)(2,1)S(1)} %get-tuple-element.20), channel_id=1, source_target_pairs={{0,1},{1,2},{2,3},{3,0},{4,5},{5,6},{6,7},{7,4},{8,9},{9,10},{10,1... | collective-permute-start | bytes 294920 | tf_op jit(solution)/shard_map/ppermute | solution.py:628
  31.9 17.6 %collective-permute-start.3 = (bf16[384,128]{1,0:T(8,128)(2,1)S(1)}, bf16[384,128]{1,0:T(8,128)(2,1)S(1)}, u32[]{:S(2)}, u32[]{:S(2)}) collective-permute-start(bf16[384,128]{1,0:T(8,128)(2,1)S(1)} %get-tuple-element.21), channel_id=1, source_target_pairs={{1,0},{2,1},{3,2},{0,3},{5,4},{6,5},{7,6},{4,7},{9,8},{10,9},{11,1... | collective-permute-start | bytes 294920 | tf_op jit(solution)/shard_map/ppermute | solution.py:627
  33.7 15.8 %copy-start.5 = (bf16[128,128]{1,0:T(8,128)(2,1)S(1)}, bf16[128,128]{1,0:T(8,128)(2,1)}, u32[]{:S(2)}) copy-start(bf16[128,128]{1,0:T(8,128)(2,1)} %constant.8.clone.place_ref) | copy-start | bytes 98308

commit v2 on v1

--- a/solution.py
+++ b/solution.py
@@ -95,6 +95,17 @@
     return np.concatenate([weights, weights], axis=0)
 
 
+def planes_matrix():
+    weights = np.zeros((128, 128), np.float32)
+    for out in range(128):
+        for m in range(1, 5):
+            if out % 16 + m < 16:
+                weights[out, out + m] = WHOLE_WEIGHTS[m - 1]
+            if out % 16 - m >= 0:
+                weights[out, out - m] = -WHOLE_WEIGHTS[m - 1]
+    return np.concatenate([weights, weights], axis=1)
+
+
 def lane_mask(field):
     lanes = lax.broadcasted_iota(jnp.int32, (1, 128), 1) % 64
     mask = (lanes >= 4 * field) & (lanes < 4 * field + 4)
@@ -128,50 +139,107 @@
     return pieces
 
 
-def front_kernel(
-    count, fields_ref, flat, prim, main_ref, low_edge_ref, high_edge_ref, low_ref, high_ref, progress, edge, arrived
-):
-    rows = flat.shape[1]
+def probe_kernel(count, fields_ref, prim, main_ref, held, progress, arrived):
+    rows = prim.shape[1]
     depth = rows // 16
     own = depth // count
     chunk = 256
 
     def arrival(step):
         there = pl.ds(pl.multiple_of(step * chunk, chunk), chunk)
-        return pltpu.make_async_copy(
-            fields_ref.at[:, there, :], flat.at[:, there, :], arrived.at[step]
-        )
+        return [
+            pltpu.make_async_copy(
+                fields_ref.at[0:5, there, :], held.at[0:5, there, :], arrived.at[0, step]
+            ),
+            pltpu.make_async_copy(
+                fields_ref.at[9, there, :], held.at[5, there, :], arrived.at[1, step]
+            ),
+        ]
 
     for step in range(rows // chunk):
-        arrival(step).start()
+        for copy in arrival(step):
+            copy.start()
 
     def chunk_body(step, carry):
-        arrival(step).wait()
+        for copy in arrival(step):
+            copy.wait()
 
         def fill(part, inner_carry):
             at = pl.ds(pl.multiple_of(step * chunk + part * 64, 64), 64)
-            density = flat[0, at, :]
-            mx, my, mz, energy = [flat[c, at, :] for c in range(1, 5)]
+            density = held[0, at, :]
+            mx, my, mz, energy = [held[c, at, :] for c in range(1, 5)]
             u, v, w = mx / density, my / density, mz / density
             stress = GAMMA_LESS * (energy - 0.5 * (mx * u + my * v + mz * w))
-            progress[at, :] = PROGRESS_SCALE * (flat[9, at, :] / density)
+            progress[at, :] = PROGRESS_SCALE * (held[5, at, :] / density)
             prim[0, at, :] = u
             prim[1, at, :] = v
             prim[2, at, :] = w
             prim[3, at, :] = stress
-            flat[4, at, :] = energy + stress
+            prim[4, at, :] = energy + stress
             return inner_carry
 
         lax.fori_loop(0, chunk // 64, fill, 0)
+        return carry
+
+    lax.fori_loop(0, rows // chunk, chunk_body, 0)
+
+    for j in range(count):
+        offset = 0
+        for c in range(4):
+            margin = 2 if c == 0 else 1
+            for to, length, source in wrapped(own * j - margin, own + 2 * margin, depth):
+                piece = progress[source : source + length, :] if c == 0 else prim[c - 1, source : source + length, :]
+                main_ref[j, offset + to : offset + to + length, :] = piece.astype(BF16)
+            offset += (own + 2 * margin) * 16
+
+
+def probe_part(fields, count):
+    rows = fields.shape[1]
+    own = rows // 16 // count
+    main_rows = (4 * own + 10) * 16
+    return pl.pallas_call(
+        functools.partial(probe_kernel, count),
+        in_specs=in_hbm(1),
+        out_specs=in_vmem(2),
+        out_shape=[
+            jax.ShapeDtypeStruct((5, rows, 128), F32),
+            jax.ShapeDtypeStruct((count, main_rows, 128), BF16),
+        ],
+        scratch_shapes=[
+            pltpu.VMEM((6, rows, 128), F32),
+            pltpu.VMEM((rows, 128), F32),
+            pltpu.SemaphoreType.DMA((2, rows // 256)),
+        ],
+        compiler_params=pltpu.CompilerParams(vmem_limit_bytes=48 * MIB),
+        cost_estimate=pl.CostEstimate(flops=30 * rows * 128, bytes_accessed=5 * MIB, transcendentals=0),
+        name="probe_part",
+    )(fields)
+
+
+def faces_kernel(fields_ref, prim, flat, low_ref, high_ref, arrived):
+    rows = flat.shape[1]
+
+    def arrival(step):
+        there = pl.ds(pl.multiple_of(step * 256, 256), 256)
+        return pltpu.make_async_copy(
+            fields_ref.at[:, there, :], flat.at[:, there, :], arrived.at[step]
+        )
+
+    for step in range(rows // 256):
+        arrival(step).start()
+
+    def chunk_body(step, carry):
+        arrival(step).wait()
         planes = pl.ds(pl.multiple_of(step * 16, 16), 16)
 
         def layer(ref, index, x):
-            return ref[index, pl.ds(step * chunk + x, 16, stride=16), :]
+            return ref[index, pl.ds(step * 256 + x, 16, stride=16), :]
 
         for ref, layers, sign in ((low_ref, (0, 1, 2, 3), 1.0), (high_ref, (15, 14, 13, 12), -1.0)):
             speeds = [layer(prim, 0, x) for x in layers]
             for field in range(FIELDS):
-                flux = [layer(flat, field, x) * speeds[k] for k, x in enumerate(layers)]
+                source = (prim, 4) if field == 4 else (flat, field)
+                flux = [layer(*source, x) * speeds[k] for k, x in enumerate(layers)]
                 if field == 1:
                     flux = [flux[k] + layer(prim, 3, x) for k, x in enumerate(layers)]
                 for cell in range(4):
@@ -184,55 +252,26 @@
                         ref[4 * FIELDS + field, planes, :] = low
         return carry
 
-    lax.fori_loop(0, rows // chunk, chunk_body, 0)
-
-    edge[...] = jnp.zeros(edge.shape, F32)
-    for j in range(count):
-        offset = 0
-        for c in range(4):
-            margin = 2 if c == 0 else 1
-            for to, length, source in wrapped(own * j - margin, own + 2 * margin, depth):
-                piece = progress[source : source + length, :] if c == 0 else prim[c - 1, source : source + length, :]
-                main_ref[j, offset + to : offset + to + length, :] = piece.astype(BF16)
-            offset += (own + 2 * margin) * 16
-        for ref, first, second in ((low_edge_ref, 0, 1), (high_edge_ref, 15, 14)):
-            for to, length, source in wrapped(own * j - 1, own + 2, depth):
-                edge[to // 16 : (to + length) // 16, :] = progress[pl.ds(source + first, length // 16, stride=16), :]
-            edge[own + 2 : 2 * own + 2, :] = progress[pl.ds(own * j * 16 + second, own, stride=16), :]
-            for c in range(3):
-                start = (c + 2) * own + 2
-                edge[start : start + own, :] = prim[c, pl.ds(own * j * 16 + first, own, stride=16), :]
-            ref[j, :, :] = edge[...].astype(BF16)
-
-
-def front_part(fields, count):
+    lax.fori_loop(0, rows // 256, chunk_body, 0)
+
+
+def faces_part(fields, prim):
     rows = fields.shape[1]
     depth = rows // 16
-    own = depth // count
-    main_rows = (4 * own + 10) * 16
-    edge_rows = -(-(5 * own + 2) // 16) * 16
     return pl.pallas_call(
-        functools.partial(front_kernel, count),
-        in_specs=in_hbm(1),
-        out_specs=in_vmem(7),
+        faces_kernel,
+        in_specs=in_hbm(1) + in_vmem(1),
+        out_specs=in_vmem(3),
         out_shape=[
-            jax.ShapeDtypeStruct((FIELDS, rows, 128), F32),
-            jax.ShapeDtypeStruct((4, rows, 128), F32),
-            jax.ShapeDtypeStruct((count, main_rows, 128), BF16),
-            jax.ShapeDtypeStruct((count, edge_rows, 128), BF16),
-            jax.ShapeDtypeStruct((count, edge_rows, 128), BF16),
+            jax.ShapeDtypeStruct(fields.shape, F32),
             jax.ShapeDtypeStruct((LAYERS, depth, 128), BF16),
             jax.ShapeDtypeStruct((LAYERS, depth, 128), BF16),
         ],
-        scratch_shapes=[
-            pltpu.VMEM((rows, 128), F32),
-            pltpu.VMEM((edge_rows, 128), F32),
-            pltpu.SemaphoreType.DMA((rows // 256,)),
-        ],
+        scratch_shapes=[pltpu.SemaphoreType.DMA((rows // 256,))],
         compiler_params=pltpu.CompilerParams(vmem_limit_bytes=40 * MIB),
-        cost_estimate=pl.CostEstimate(flops=100 * rows * 128, bytes_accessed=10 * MIB, transcendentals=0),
-        name="front_part",
-    )(fields)
+        cost_estimate=pl.CostEstimate(flops=100 * rows * 128, bytes_accessed=6 * MIB, transcendentals=0),
+        name="faces_part",
+    )(fields, prim)
 
 
 def lines_kernel(flat, prim, weights_ref, terms, low_ref, high_ref, total):
@@ -243,7 +282,7 @@
         at = pl.ds(pl.multiple_of(step * 32, 32), 32)
         v = prim[1, at, :]
         for field in range(FIELDS):
-            flux = flat[field, at, :] * v
+            flux = (prim[4, at, :] if field == 4 else flat[field, at, :]) * v
             if field == 2:
                 flux = flux + prim[3, at, :]
             high, low = two_terms(flux)
@@ -280,7 +319,7 @@
             jax.ShapeDtypeStruct((rows // 2, 128), BF16),
         ],
         scratch_shapes=[pltpu.VMEM((rows, 128), F32)],
-        compiler_params=pltpu.CompilerParams(vmem_limit_bytes=40 * MIB),
+        compiler_params=pltpu.CompilerParams(vmem_limit_bytes=12 * MIB),
         cost_estimate=pl.CostEstimate(flops=300 * rows * 128, bytes_accessed=8 * MIB, transcendentals=0),
         name="lines_part",
     )(flat, prim, jnp.asarray(face_matrix(), BF16))
@@ -328,11 +367,9 @@
         yield z, change
 
 
-def inner_kernel(flat, prim, register, terms, line_ref, out, flux_x, along_y):
+def inner_kernel(flat, prim, register, terms, line_ref, planes_ref, out, along_y):
     rows = flat.shape[1]
     depth = rows // 16
-    flux_x[:, 0:8, :] = jnp.zeros((depth, 8, 128), F32)
-    flux_x[:, 24:32, :] = jnp.zeros((depth, 8, 128), F32)
 
     def react(step, carry):
         at = pl.ds(pl.multiple_of(step * 32, 32), 32)
@@ -344,40 +381,40 @@
 
     lax.fori_loop(0, rows // 32, react, 0)
 
-    def spread(field, flux, extra):
-        for z in range(depth):
-            flux_x[z, 8:24, :] = flux(0, z * 16, 16)
+    def along_x(flux):
+        high, low = two_terms(flux)
+        return jnp.dot(planes_ref[...], jnp.concatenate([high, low], axis=0), preferred_element_type=F32)
+
+    def spread(field, carried):
+        along_y[...] = jnp.dot(terms[field], line_ref[...], preferred_element_type=F32)
+        for first in range(0, depth, 8):
+            at = slice(first * 16, first * 16 + 128)
+            both = along_y[at, :] + along_x(carried(at) * prim[0, at, :])
+            out[field, at, :] += (-TIME_STEP * WHOLE_SCALE) * both
         for first in range(0, depth, 16):
-            for tile in range(2):
-                row = 8 * tile
-                for z, change in windowed(lambda z: flux(2, (z % depth) * 16 + row, 8), first, 16):
-                    for m, weight in enumerate(CENTRAL_WEIGHTS, 1):
-                        at = 8 + row
-                        change = change + (-TIME_STEP * weight) * (
-                            flux_x[z, at + m : at + m + 8, :] - flux_x[z, at - m : at - m + 8, :]
-                        )
-                    extra(z * 16 + row, change)
-
-    def across(field, carry):
-        along_y[...] = jnp.dot(terms[field], line_ref[...], preferred_element_type=F32)
-
-        def flux(direction, row, size):
-            return flat[field, row : row + size, :] * prim[direction, row : row + size, :]
-
-        def extra(row, change):
-            at = slice(row, row + 8)
-            out[field, at, :] += change + (-TIME_STEP * WHOLE_SCALE) * along_y[at, :]
-
-        spread(field, flux, extra)
+            for row in (0, 8):
+
+                def flux_z(z):
+                    at = (z % depth) * 16 + row
+                    return carried(slice(at, at + 8)) * prim[2, at : at + 8, :]
+
+                for z, change in windowed(flux_z, first, 16):
+                    at = slice(z * 16 + row, z * 16 + row + 8)
+                    out[field, at, :] += change
+
+    def across(index, carry):
+        field = index + (index >= 4).astype(jnp.int32)
+        spread(field, lambda at: flat[field, at, :])
         return carry
 
-    lax.fori_loop(0, FIELDS, across, 0)
-
-    for z in range(depth):
-        flux_x[z, 8:24, :] = prim[3, z * 16 : z * 16 + 16, :]
+    lax.fori_loop(0, FIELDS - 1, across, 0)
+    spread(4, lambda at: prim[4, at, :])
+
+    for first in range(0, depth, 8):
+        at = slice(first * 16, first * 16 + 128)
+        out[1, at, :] += (-TIME_STEP * WHOLE_SCALE) * along_x(prim[3, at, :])
     for first in range(0, depth, 16):
-        for tile in range(2):
-            row = 8 * tile
+        for row in (0, 8):
 
             def stress(z):
                 at = (z % depth) * 16 + row
@@ -386,38 +423,28 @@
             for z, change in windowed(stress, first, 16):
                 at = slice(z * 16 + row, z * 16 + row + 8)
                 out[3, at, :] += change
-                change = None
-                for m, weight in enumerate(CENTRAL_WEIGHTS, 1):
-                    low = 8 + row
-                    term = (-TIME_STEP * weight) * (
-                        flux_x[z, low + m : low + m + 8, :] - flux_x[z, low - m : low - m + 8, :]
-                    )
-                    change = term if change is None else change + term
-                out[1, at, :] += change
 
 
 def inner_part(flat, prim, register, terms):
     rows = flat.shape[1]
-    depth = rows // 16
     return pl.pallas_call(
         inner_kernel,
-        in_specs=in_vmem(5),
+        in_specs=in_vmem(6),
         out_specs=pl.BlockSpec(memory_space=pltpu.VMEM),
         out_shape=jax.ShapeDtypeStruct((FIELDS, rows, 128), F32),
         scratch_shapes=[
-            pltpu.VMEM((depth, 32, 128), F32),
             pltpu.VMEM((rows, 128), F32),
         ],
-        compiler_params=pltpu.CompilerParams(vmem_limit_bytes=40 * MIB),
+        compiler_params=pltpu.CompilerParams(vmem_limit_bytes=12 * MIB),
         cost_estimate=pl.CostEstimate(
             flops=2000 * rows * 128, bytes_accessed=20 * MIB, transcendentals=10 * rows * 128
         ),
         name="inner_part",
-    )(flat, prim, register, terms, jnp.asarray(line_matrix(), BF16))
+    )(flat, prim, register, terms, jnp.asarray(line_matrix(), BF16), jnp.asarray(planes_matrix(), BF16))
 
 
 def outer_kernel(
-    part, flat, prim, prev, following, yprev, ynext, place_ref, fields_out, register_out,
+    part, flat, prev, following, yprev, ynext, place_ref, fields_out, register_out,
     faces_x, along_y, message, fields_stage, register_stage, sent,
 ):
     rows = part.shape[1]
@@ -443,10 +470,7 @@
         along_y[...] = jnp.dot(picked, place, preferred_element_type=F32)
         stored = part[field] - TIME_STEP * (along_y[...] + faces_x[...])
         register_stage[field] = stored
-        before = flat[field]
-        if field == 4:
-            before = before - prim[3]
-        fields_stage[field] = before + SECTION_WEIGHT * stored
+        fields_stage[field] = flat[field] + SECTION_WEIGHT * stored
         for index, (stage, ref) in enumerate(((register_stage, register_out), (fields_stage, fields_out))):
             copy = pltpu.make_async_copy(stage.at[field], ref.at[field], sent.at[index, field])
             copy.start()
@@ -455,11 +479,11 @@
         copy.wait()
 
 
-def outer_part(part, flat, prim, prev, following, yprev, ynext):
+def outer_part(part, flat, prev, following, yprev, ynext):
     rows = flat.shape[1]
     return pl.pallas_call(
         outer_kernel,
-        in_specs=in_vmem(8),
+        in_specs=in_vmem(7),
         out_specs=in_hbm(2),
         out_shape=[jax.ShapeDtypeStruct((FIELDS, rows, 128), F32)] * 2,
         scratch_shapes=[
@@ -470,12 +494,12 @@
             pltpu.VMEM((FIELDS, rows, 128), F32),
             pltpu.SemaphoreType.DMA((2, FIELDS)),
         ],
-        compiler_params=pltpu.CompilerParams(vmem_limit_bytes=40 * MIB),
+        compiler_params=pltpu.CompilerParams(vmem_limit_bytes=20 * MIB),
         cost_estimate=pl.CostEstimate(
             flops=100 * rows * 128, bytes_accessed=24 * MIB, transcendentals=0
         ),
         name="outer_part",
-    )(part, flat, prim, prev, following, yprev, ynext, jnp.asarray(place_matrix(), BF16))
+    )(part, flat, prev, following, yprev, ynext, jnp.asarray(place_matrix(), BF16))
 
 
 def lane_difference(values):
@@ -494,19 +518,59 @@
     return 1.0 * lax.rsqrt(jnp.maximum(a * a + b * b + c * c, GRAD_FLOOR * GRAD_FLOOR))
 
 
-def metrics_kernel(count, own, blocks, out_ref, scalar, speed, normal, normal_z, edge, stage, sent):
-    start_edge = (4 * own + 10) * 16
-    half = (blocks.shape[1] - start_edge) // 2
-    edge[...] = blocks[:, start_edge:, :].astype(F32)
-    for j in range(count):
+def unpack_kernel(count, own, blocks, scalar, speed, low_ref, high_ref, edge):
+    edge[...] = jnp.zeros(edge.shape, F32)
+
+    def body(j, carry):
         for z in range(own + 4):
-            scalar[j, pl.ds(z * 32 + 8, 16), :] = blocks[j, z * 16 : z * 16 + 16, :].astype(F32)
+            scalar[j, z * 32 + 8 : z * 32 + 24, :] = blocks[j, z * 16 : z * 16 + 16, :].astype(F32)
         for c in range(3):
             base = (own + 4 + c * (own + 2)) * 16
             for z in range(own + 2):
-                speed[c, j, pl.ds(z * 32 + 8, 16), :] = blocks[
+                speed[c, j, z * 32 + 8 : z * 32 + 24, :] = blocks[
                     j, base + z * 16 : base + z * 16 + 16, :
                 ].astype(F32)
+        for ref, first, second in ((low_ref, 8, 9), (high_ref, 23, 22)):
+            edge[0 : own + 2, :] = scalar[j, pl.ds(32 + first, own + 2, stride=32), :]
+            edge[own + 2 : 2 * own + 2, :] = scalar[j, pl.ds(64 + second, own, stride=32), :]
+            for c in range(3):
+                start = (c + 2) * own + 2
+                edge[start : start + own, :] = speed[c, j, pl.ds(32 + first, own, stride=32), :]
+            ref[j, :, :] = edge[...].astype(BF16)
+        return carry
+
+    lax.fori_loop(0, count, body, 0)
+
+
+def unpack_part(blocks, own):
+    count = blocks.shape[0]
+    edge_rows = -(-(5 * own + 2) // 16) * 16
+    return pl.pallas_call(
+        functools.partial(unpack_kernel, count, own),
+        in_specs=in_vmem(1),
+        out_specs=in_vmem(4),
+        out_shape=[
+            jax.ShapeDtypeStruct((count, (own + 4) * 32, 128), F32),
+            jax.ShapeDtypeStruct((3, count, (own + 2) * 32, 128), F32),
+            jax.ShapeDtypeStruct((count, edge_rows, 128), BF16),
+            jax.ShapeDtypeStruct((count, edge_rows, 128), BF16),
+        ],
+        scratch_shapes=[pltpu.VMEM((edge_rows, 128), F32)],
+        compiler_params=pltpu.CompilerParams(vmem_limit_bytes=4 * MIB),
+        cost_estimate=pl.CostEstimate(
+            flops=10 * own * 16 * 128 * count, bytes_accessed=5 * MIB, transcendentals=0
+        ),
+        name="unpack_part",
+    )(blocks)
+
+
+def metrics_kernel(
+    count, own, scalar_in, speed_in, prev, following, scalar, speed, out_ref, normal, normal_z, edge, stage, sent
+):
+    half = prev.shape[1]
+    edge[:, 0:half, :] = prev[...].astype(F32)
+    edge[:, half:, :] = following[...].astype(F32)
+    for j in range(count):
         for side, row in ((0, 7), (half, 24)):
             scalar[j, pl.ds(32 + row, own + 2, stride=32), :] = edge[j, side : side + own + 2, :]
             for c in range(3):
@@ -581,54 +645,58 @@
         pltpu.make_async_copy(stage.at[:, z], out_ref.at[:, z], sent.at[z]).wait()
 
 
-def metrics_part(blocks, own):
-    count = blocks.shape[0]
-    half = (blocks.shape[1] - (4 * own + 10) * 16) // 2
+def metrics_part(scalar, speed, prev, following, own):
+    count, half = prev.shape[:2]
     shape = (5, own, 16, count * 128)
     return pl.pallas_call(
         functools.partial(metrics_kernel, count, own),
-        in_specs=in_vmem(1),
-        out_specs=in_hbm(1)[0],
-        out_shape=jax.ShapeDtypeStruct(shape, BF16),
+        in_specs=in_vmem(4),
+        out_specs=in_vmem(2) + in_hbm(1),
+        out_shape=[
+            jax.ShapeDtypeStruct(scalar.shape, F32),
+            jax.ShapeDtypeStruct(speed.shape, F32),
+            jax.ShapeDtypeStruct(shape, BF16),
+        ],
+        input_output_aliases={0: 0, 1: 1},
         scratch_shapes=[
-            pltpu.VMEM((count, (own + 4) * 32, 128), F32),
-            pltpu.VMEM((3, count, (own + 2) * 32, 128), F32),
             pltpu.VMEM((2, count, (own + 2) * 32, 128), F32),
             pltpu.VMEM((count, own + 2, 16, 128), F32),
             pltpu.VMEM((count, 2 * half, 128), F32),
             pltpu.VMEM(shape, BF16),
             pltpu.SemaphoreType.DMA((own,)),
         ],
-        compiler_params=pltpu.CompilerParams(vmem_limit_bytes=40 * MIB),
+        compiler_params=pltpu.CompilerParams(vmem_limit_bytes=10 * MIB),
         cost_estimate=pl.CostEstimate(
             flops=300 * own * 16 * 128 * count, bytes_accessed=3 * MIB, transcendentals=0
         ),
         name="flame_metrics",
-    )(blocks)
+    )(scalar, speed, prev, following)[2]
 
 
 def per_device(fields, register):
     depth, count_x, count_y = fields.shape[1:]
-    flat = fields.reshape(FIELDS, depth * count_x, count_y)
+    given = fields.reshape(FIELDS, depth * count_x, count_y)
     count = lax.axis_size("gy")
     own = depth // count
     x_forward, x_backward = ring("gx")
     y_forward, y_backward = ring("gy")
 
-    flat, prim, main, edge_low, edge_high, low, high = front_part(flat, count)
-    edge_prev = lax.ppermute(edge_high, "gx", x_forward)
-    edge_next = lax.ppermute(edge_low, "gx", x_backward)
+    prim, main = probe_part(given, count)
+    blocks = lax.all_to_all(main, "gy", 0, 0, tiled=True)
+    flat, low, high = faces_part(given, prim)
     following = lax.ppermute(low, "gx", x_backward)
     prev = lax.ppermute(high, "gx", x_forward)
     terms, ylow, yhigh = lines_part(flat, prim)
-    blocks = lax.all_to_all(
-        jnp.concatenate([main, edge_prev, edge_next], axis=1), "gy", 0, 0, tiled=True
-    )
     ynext = lax.ppermute(ylow, "gy", y_backward)
     yprev = lax.ppermute(yhigh, "gy", y_forward)
     part = inner_part(flat, prim, register.reshape(flat.shape), terms)
-    fields_next, register_next = outer_part(part, flat, prim, prev, following, yprev, ynext)
-    metrics = metrics_part(blocks, own)
+    blocks, part = lax.optimization_barrier((blocks, part))
+    scalar, speed, edge_low, edge_high = unpack_part(blocks, own)
+    edge_prev = lax.ppermute(edge_high, "gx", x_forward)
+    edge_next = lax.ppermute(edge_low, "gx", x_backward)
+    part, scalar = lax.optimization_barrier((part, scalar))
+    fields_next, register_next = outer_part(part, flat, prev, following, yprev, ynext)
+    metrics = metrics_part(scalar, speed, edge_prev, edge_next, own)
     return (fields_next.reshape(fields.shape), register_next.reshape(fields.shape), metrics)
 
 

time: 59.7 us -> 56.3 us (0.943)
  Pallas kernels: 31.9 us -> 26.2 us
  local copies, waits for them, and re-layouts: 8.32 us -> 11.1 us
  other arithmetic: 1.06 us -> 0 us
    pallas_call x3 -> x5, Pallas kernels: 24.5 us -> 19 us  [the longest x1 7.54 us: inner_part(): pl.pallas_call(inner_kernel, in_specs=in_vmem(6), out_specs=pl.BlockSpec(...]
    unnamed x14 -> x22, local copies, waits for them, and re-layouts: 8.32 us -> 11.1 us
    all_to_all x1, waiting for transfers between devices: 0.01 us -> 1.99 us  [per_device(): blocks = lax.all_to_all(main, 'gy', 0, 0, tiled=True)]
    ppermute x1, waiting for transfers between devices: 1.94 us -> 0.01 us  [per_device(): edge_prev = lax.ppermute(edge_high, 'gx', x_forward)]
    concatenate x1 -> x0, other arithmetic: 1.06 us -> none  [per_device(): jnp.concatenate([main, edge_prev, edge_next], axis=1)]
    all_to_all x1, starting transfers between devices: 5.63 us -> 6.45 us  [per_device(): blocks = lax.all_to_all(main, 'gy', 0, 0, tiled=True)]
  transfers between devices with their start and end apart: 7 -> 7, of which waited for: 1 -> 1; matrix products, arithmetic and copies ran while one was open for 0% -> 0% of each run, Pallas kernels for 41% -> 36%
where the time goes in v2:
time: 56.3 us; the launch traced here: 55.9 us
  Pallas kernels  26.2 us (47%)
  starting transfers between devices  15.8 us (28%)
  local copies, waits for them, and re-layouts  11.1 us (20%)
  waiting for transfers between devices  2.01 us (4%)
  between operations  0.79 us (1%)
    unnamed x22, local copies, waits for them, and re-layouts  11.1 us
    pallas_call x1, Pallas kernels, inner_part(): pl.pallas_call(inner_kernel, in_specs=in_vmem(6), out_specs=pl.BlockSpec(...  7.54 us
    pallas_call x1, Pallas kernels, outer_part(): pl.pallas_call(outer_kernel, in_specs=in_vmem(7), out_specs=in_hbm(2), ou...  6.64 us
    all_to_all x1, starting transfers between devices, per_device(): blocks = lax.all_to_all(main, 'gy', 0, 0, tiled=True)  6.45 us
    pallas_call x1, Pallas kernels, metrics_part(): pl.pallas_call(functools.partial(metrics_kernel, count, own), in_specs=in...  4.39 us
    pallas_call x1, Pallas kernels, lines_part(): pl.pallas_call(lines_kernel, in_specs=in_vmem(3), out_specs=in_vmem(3), o...  2.87 us
    ppermute x1, starting transfers between devices, per_device(): following = lax.ppermute(low, 'gx', x_backward)  2.63 us
    pallas_call x1, Pallas kernels, faces_part(): pl.pallas_call(faces_kernel, in_specs=in_hbm(1) + in_vmem(1), out_specs=i...  2.63 us
  transfers between devices with their start and end apart: 7, of which 1 were waited for; matrix products, arithmetic and copies ran while one was open for 0% of the time, Pallas kernels for 36%

profile of v2, /device:TPU:0, one launch (start us, length us, event | category | flops | bytes accessed | tf_op | source)
XLA Modules:
  0.0 55.9 jit_solution(11683690384639880466)
XLA Ops:
  0.6 1.8 %probe_part.1 = (f32[5,768,128]{2,1,0:T(8,128)S(1)}, bf16[4,928,128]{2,1,0:T(8,128)(2,1)S(1)}) custom-call(f32[14,768,128]{2,1,0:T(8,128)} %bitcast.4), custom_call_target="tpu_custom_call" | custom-call | flops 2949120 | bytes 5242880 | tf_op jit(solution)/shard_map/probe_part/pallas_call | solution.py:200
  2.5 0.0 copy-start.6
  2.5 0.9 %copy-done.6 = bf16[4,928,128]{2,1,0:T(8,128)(2,1)} copy-done((bf16[4,928,128]{2,1,0:T(8,128)(2,1)}, bf16[4,928,128]{2,1,0:T(8,128)(2,1)S(1)}, u32[]{:S(2)}) %copy-start.6) | copy-done | bytes 950296
  3.4 0.0 copy-start.9
  3.4 6.4 %all-to-all-start = ((bf16[4,928,128]{2,1,0:T(8,128)(2,1)}), bf16[4,928,128]{2,1,0:T(8,128)(2,1)S(1)}, u32[]{:S(2)}, u32[]{:S(2)}) async-start(bf16[4,928,128]{2,1,0:T(8,128)(2,1)} %copy-done.6), calls=%async_computation | async-start | bytes 1900544 | tf_op jit(solution)/shard_map/all_to_all | solution.py:685
  9.8 0.0 copy-start.2
  9.8 2.6 %copy-done.2 = f32[14,48,16,128]{3,2,1,0:T(8,128)S(1)} copy-done((f32[14,48,16,128]{3,2,1,0:T(8,128)S(1)}, f32[14,48,16,128]{3,2,1,0:T(8,128)}, u32[]{:S(2)}) %copy-start.2) | copy-done | bytes 5505048
  12.4 2.6 %faces_part.1 = (f32[14,768,128]{2,1,0:T(8,128)S(1)}, bf16[61,48,128]{2,1,0:T(8,128)(2,1)}, bf16[61,48,128]{2,1,0:T(8,128)(2,1)}) custom-call(f32[14,768,128]{2,1,0:T(8,128)S(1)} %bitcast.5, f32[5,768,128]{2,1,0:T(8,128)S(1)} %get-tuple-element.23.prim), custom_call_target="tpu_custom_call" | custom-call | flops 9830400 | bytes 6291456 | tf_op jit(solution)/shard_map/faces_part/pallas_call | solution.py:261
  15.0 0.0 copy-start
  15.1 0.0 copy-start.5
  15.1 0.0 copy-start.7
  15.1 0.0 copy-start.8
  15.1 0.1 collective-permute-start
  15.2 2.6 %collective-permute-start.1 = (bf16[61,48,128]{2,1,0:T(8,128)(2,1)}, bf16[61,48,128]{2,1,0:T(8,128)(2,1)}, u32[]{:S(2)}, u32[]{:S(2)}) collective-permute-start(bf16[61,48,128]{2,1,0:T(8,128)(2,1)} %get-tuple-element.31), channel_id=1, source_target_pairs={{4,0},{8,4},{12,8},{16,12},{20,16},{24,20},{28,24},{0,28},{5,1},{9... | collective-permute-start | bytes 2248712 | tf_op jit(solution)/shard_map/ppermute | solution.py:687
  17.8 0.0 copy-done.9
  17.8 2.9 %lines_part.1 = (bf16[14,768,256]{2,1,0:T(8,128)(2,1)S(1)}, bf16[384,128]{1,0:T(8,128)(2,1)S(1)}, bf16[384,128]{1,0:T(8,128)(2,1)S(1)}) custom-call(f32[14,768,128]{2,1,0:T(8,128)S(1)} %get-tuple-element.24.flat, f32[5,768,128]{2,1,0:T(8,128)S(1)} %get-tuple-element.23.prim, bf16[256,128]{1,0:T(8,128)(2,1)S(1)} %copy-done.9), custom_call_target="tpu_custom_call" | custom-call | flops 29491200 | bytes 8388608 | tf_op jit(solution)/shard_map/lines_part/pallas_call | solution.py:312
  20.7 2.1 %collective-permute-start.2 = (bf16[384,128]{1,0:T(8,128)(2,1)S(1)}, bf16[384,128]{1,0:T(8,128)(2,1)S(1)}, u32[]{:S(2)}, u32[]{:S(2)}) collective-permute-start(bf16[384,128]{1,0:T(8,128)(2,1)S(1)} %get-tuple-element.32), channel_id=1, source_target_pairs={{0,1},{1,2},{2,3},{3,0},{4,5},{5,6},{6,7},{7,4},{8,9},{9,10},{10,1... | collective-permute-start | bytes 294920 | tf_op jit(solution)/shard_map/ppermute | solution.py:691
  22.7 1.9 %collective-permute-start.3 = (bf16[384,128]{1,0:T(8,128)(2,1)S(1)}, bf16[384,128]{1,0:T(8,128)(2,1)S(1)}, u32[]{:S(2)}, u32[]{:S(2)}) collective-permute-start(bf16[384,128]{1,0:T(8,128)(2,1)S(1)} %get-tuple-element.33), channel_id=1, source_target_pairs={{1,0},{2,1},{3,2},{0,3},{5,4},{6,5},{7,6},{4,7},{9,8},{10,9},{11,1... | collective-permute-start | bytes 294920 | tf_op jit(solution)/shard_map/ppermute | solution.py:690
  24.6 0.0 copy-done
  24.6 0.0 copy-done.5
  24.6 0.0 copy-done.7
  24.6 0.0 copy-done.8
  24.6 0.0 copy-start.10
  24.6 7.5 %inner_part.1.part = f32[14,768,128]{2,1,0:T(8,128)S(1)} custom-call(f32[14,768,128]{2,1,0:T(8,128)S(1)} %get-tuple-element.24.flat, f32[5,768,128]{2,1,0:T(8,128)S(1)} %get-tuple-element.23.prim, f32[14,768,128]{2,1,0:T(8,128)S(1)} %bitcast.6, bf16[14,768,256]{2,1,0:T(8,128)(2,1)S(1)} %get-tuple-element.25.terms, bf16[256,128]{1,0:T(8,128)(2,1)S(1)} %copy-done.8, ...), custom_call_target="tpu_custom_call" | custom-call | flops 196608000 | bytes 20971520 | tf_op jit(solution)/shard_map/inner_part/pallas_call | solution.py:430
  32.2 0.0 copy-start.3
  32.2 2.4 %copy-done.3 = f32[14,768,128]{2,1,0:T(8,128)} copy-done((f32[14,768,128]{2,1,0:T(8,128)}, f32[14,768,128]{2,1,0:T(8,128)S(1)}, u32[]{:S(2)}) %copy-start.3) | copy-done | bytes 5505048
  34.6 2.0 %all-to-all-done.blocks = bf16[4,928,128]{2,1,0:T(8,128)(2,1)S(1)} async-done(((bf16[4,928,128]{2,1,0:T(8,128)(2,1)}), bf16[4,928,128]{2,1,0:T(8,128)(2,1)S(1)}, u32[]{:S(2)}, u32[]{:S(2)}) %all-to-all-start) | async-done | bytes 950304 | tf_op jit(solution)/shard_map/all_to_all | solution.py:685
  36.6 0.4 unpack_part.1
  37.0 0.1 collective-permute-start.4
  37.0 0.0 collective-permute-done.2.yprev
  37.1 2.6 %collective-permute-start.5 = (bf16[4,64,128]{2,1,0:T(8,128)(2,1)S(1)}, bf16[4,64,128]{2,1,0:T(8,128)(2,1)S(1)}, u32[]{:S(2)}, u32[]{:S(2)}) collective-permute-start(bf16[4,64,128]{2,1,0:T(8,128)(2,1)S(1)} %get-tuple-element.39), channel_id=1, source_target_pairs={{4,0},{8,4},{12,8},{16,12},{20,16},{24,20},{28,24},{0,28},{5,1},{9... | collective-permute-start | bytes 196616 | tf_op jit(solution)/shard_map/ppermute | solution.py:696
  39.7 0.0 collective-permute-done.3.ynext
  39.7 0.0 collective-permute-done.prev
  39.7 0.0 collective-permute-done.1.following
  39.7 0.0 copy-done.10
  39.7 0.0 copy-start.1
  39.7 2.6 %copy-done.1 = f32[14,768,128]{2,1,0:T(8,128)S(1)} copy-done((f32[14,768,128]{2,1,0:T(8,128)S(1)}, f32[14,768,128]{2,1,0:T(8,128)}, u32[]{:S(2)}) %copy-start.1) | copy-done | bytes 5505048
  42.3 0.0 copy-start.4
  42.3 2.6 %copy-done.4 = f32[14,768,128]{2,1,0:T(8,128)S(1)} copy-done((f32[14,768,128]{2,1,0:T(8,128)S(1)}, f32[14,768,128]{2,1,0:T(8,128)}, u32[]{:S(2)}) %copy-start.4) | copy-done | bytes 5505048
  44.8 6.6 %outer_part.1 = (f32[14,768,128]{2,1,0:T(8,128)}, f32[14,768,128]{2,1,0:T(8,128)}) custom-call(f32[14,768,128]{2,1,0:T(8,128)S(1)} %copy-done.4, f32[14,768,128]{2,1,0:T(8,128)S(1)} %copy-done.1, bf16[61,48,128]{2,1,0:T(8,128)(2,1)} %collective-permute-done.prev, bf16[61,48,128]{2,1,0:T(8,128)(2,1)} %collective-permute-done.1.following, ...), custom_call_target="tpu_custom_call" | custom-call | flops 9830400 | bytes 25165824 | tf_op jit(solution)/shard_map/outer_part/pallas_call | solution.py:484
  51.5 0.0 collective-permute-done.4.prev
  51.5 0.0 collective-permute-done.5.following
  51.5 4.4 %flame_metrics.1 = (f32[4,512,128]{2,1,0:T(8,128)S(1)}, f32[3,4,448,128]{3,2,1,0:T(8,128)S(1)}, bf16[5,12,16,512]{3,2,1,0:T(8,128)(2,1)}) custom-call(f32[4,512,128]{2,1,0:T(8,128)S(1)} %get-tuple-element.36.scalar_in, f32[3,4,448,128]{3,2,1,0:T(8,128)S(1)} %get-tuple-element.37.speed_in, ...), custom_call_target="tpu_custom_call", output_to_operand_aliasing={{0}: (0, {}), {1}: (1, {})} | custom-call | flops 29491200 | bytes 3145728 | tf_op jit(solution)/shard_map/flame_metrics/pallas_call | solution.py:651
Async XLA Ops:
  2.5 0.9 %copy-start.6 = (bf16[4,928,128]{2,1,0:T(8,128)(2,1)}, bf16[4,928,128]{2,1,0:T(8,128)(2,1)S(1)}, u32[]{:S(2)}) copy-start(bf16[4,928,128]{2,1,0:T(8,128)(2,1)S(1)} %get-tuple-element.22) | copy-start | bytes 2850820
  3.4 14.4 %copy-start.9 = (bf16[256,128]{1,0:T(8,128)(2,1)S(1)}, bf16[256,128]{1,0:T(8,128)(2,1)}, u32[]{:S(2)}) copy-start(bf16[256,128]{1,0:T(8,128)(2,1)} %constant.8.clone.weights_ref) | copy-start | bytes 196612
  3.4 33.2 %all-to-all-start = ((bf16[4,928,128]{2,1,0:T(8,128)(2,1)}), bf16[4,928,128]{2,1,0:T(8,128)(2,1)S(1)}, u32[]{:S(2)}, u32[]{:S(2)}) async-start(bf16[4,928,128]{2,1,0:T(8,128)(2,1)} %copy-done.6), calls=%async_computation | async-start | bytes 1900544 | tf_op jit(solution)/shard_map/all_to_all | solution.py:685
  9.8 2.6 %copy-start.2 = (f32[14,48,16,128]{3,2,1,0:T(8,128)S(1)}, f32[14,48,16,128]{3,2,1,0:T(8,128)}, u32[]{:S(2)}) copy-start(f32[14,48,16,128]{3,2,1,0:T(8,128)} %param.6) | copy-start | bytes 16515076
  15.0 9.6 %copy-start = (f32[14,768,128]{2,1,0:T(8,128)}, f32[14,768,128]{2,1,0:T(8,128)S(1)}, u32[]{:S(2)}) copy-start(f32[14,768,128]{2,1,0:T(8,128)S(1)} %get-tuple-element.24.flat) | copy-start | bytes 16515076
  15.1 9.6 %copy-start.5 = (f32[14,48,16,128]{3,2,1,0:T(8,128)S(1)}, f32[14,48,16,128]{3,2,1,0:T(8,128)}, u32[]{:S(2)}) copy-start(f32[14,48,16,128]{3,2,1,0:T(8,128)} %param.7) | copy-start | bytes 16515076
  15.1 9.6 %copy-start.7 = (bf16[128,256]{1,0:T(8,128)(2,1)S(1)}, bf16[128,256]{1,0:T(8,128)(2,1)}, u32[]{:S(2)}) copy-start(bf16[128,256]{1,0:T(8,128)(2,1)} %constant.10.clone.planes_ref) | copy-start | bytes 196612
  15.1 9.5 %copy-start.8 = (bf16[256,128]{1,0:T(8,128)(2,1)S(1)}, bf16[256,128]{1,0:T(8,128)(2,1)}, u32[]{:S(2)}) copy-start(bf16[256,128]{1,0:T(8,128)(2,1)} %constant.9.clone.line_ref) | copy-start | bytes 196612
  15.1 24.6 %collective-permute-start = (bf16[61,48,128]{2,1,0:T(8,128)(2,1)}, bf16[61,48,128]{2,1,0:T(8,128)(2,1)}, u32[]{:S(2)}, u32[]{:S(2)}) collective-permute-start(bf16[61,48,128]{2,1,0:T(8,128)(2,1)} %get-tuple-element.30), channel_id=1, source_target_pairs={{0,4},{4,8},{8,12},{12,16},{16,20},{20,24},{24,28},{28,0},{1,5},{5... | collective-permute-start | bytes 2248712 | tf_op jit(solution)/shard_map/ppermute | solution.py:688
  15.2 24.5 %collective-permute-start.1 = (bf16[61,48,128]{2,1,0:T(8,128)(2,1)}, bf16[61,48,128]{2,1,0:T(8,128)(2,1)}, u32[]{:S(2)}, u32[]{:S(2)}) collective-permute-start(bf16[61,48,128]{2,1,0:T(8,128)(2,1)} %get-tuple-element.31), channel_id=1, source_target_pairs={{4,0},{8,4},{12,8},{16,12},{20,16},{24,20},{28,24},{0,28},{5,1},{9... | collective-permute-start | bytes 2248712 | tf_op jit(solution)/shard_map/ppermute | solution.py:687
  20.7 16.4 %collective-permute-start.2 = (bf16[384,128]{1,0:T(8,128)(2,1)S(1)}, bf16[384,128]{1,0:T(8,128)(2,1)S(1)}, u32[]{:S(2)}, u32[]{:S(2)}) collective-permute-start(bf16[384,128]{1,0:T(8,128)(2,1)S(1)} %get-tuple-element.32), channel_id=1, source_target_pairs={{0,1},{1,2},{2,3},{3,0},{4,5},{5,6},{6,7},{7,4},{8,9},{9,10},{10,1... | collective-permute-start | bytes 294920 | tf_op jit(solution)/shard_map/ppermute | solution.py:691
  22.7 16.9 %collective-permute-start.3 = (bf16[384,128]{1,0:T(8,128)(2,1)S(1)}, bf16[384,128]{1,0:T(8,128)(2,1)S(1)}, u32[]{:S(2)}, u32[]{:S(2)}) collective-permute-start(bf16[384,128]{1,0:T(8,128)(2,1)S(1)} %get-tuple-element.33), channel_id=1, source_target_pairs={{1,0},{2,1},{3,2},{0,3},{5,4},{6,5},{7,6},{4,7},{9,8},{10,9},{11,1... | collective-permute-start | bytes 294920 | tf_op jit(solution)/shard_map/ppermute | solution.py:690
  24.6 15.1 %copy-start.10 = (bf16[128,128]{1,0:T(8,128)(2,1)S(1)}, bf16[128,128]{1,0:T(8,128)(2,1)}, u32[]{:S(2)}) copy-start(bf16[128,128]{1,0:T(8,128)(2,1)} %constant.11.clone.place_ref) | copy-start | bytes 98308
  32.2 2.4 %copy-start.3 = (f32[14,768,128]{2,1,0:T(8,128)}, f32[14,768,128]{2,1,0:T(8,128)S(1)}, u32[]{:S(2)}) copy-start(f32[14,768,128]{2,1,0:T(8,128)S(1)} %inner_part.1.part) | copy-start | bytes 16515076
  37.0 14.5 %collective-permute-start.4 = (bf16[4,64,128]{2,1,0:T(8,128)(2,1)S(1)}, bf16[4,64,128]{2,1,0:T(8,128)(2,1)S(1)}, u32[]{:S(2)}, u32[]{:S(2)}) collective-permute-start(bf16[4,64,128]{2,1,0:T(8,128)(2,1)S(1)} %get-tuple-element.38), channel_id=1, source_target_pairs={{0,4},{4,8},{8,12},{12,16},{16,20},{20,24},{24,28},{28,0},{1,5},{5... | collective-permute-start | bytes 196616 | tf_op jit(solution)/shard_map/ppermute | solution.py:695
  37.1 14.4 %collective-permute-start.5 = (bf16[4,64,128]{2,1,0:T(8,128)(2,1)S(1)}, bf16[4,64,128]{2,1,0:T(8,128)(2,1)S(1)}, u32[]{:S(2)}, u32[]{:S(2)}) collective-permute-start(bf16[4,64,128]{2,1,0:T(8,128)(2,1)S(1)} %get-tuple-element.39), channel_id=1, source_target_pairs={{4,0},{8,4},{12,8},{16,12},{20,16},{24,20},{28,24},{0,28},{5,1},{9... | collective-permute-start | bytes 196616 | tf_op jit(solution)/shard_map/ppermute | solution.py:696
  39.7 2.6 %copy-start.1 = (f32[14,768,128]{2,1,0:T(8,128)S(1)}, f32[14,768,128]{2,1,0:T(8,128)}, u32[]{:S(2)}) copy-start(f32[14,768,128]{2,1,0:T(8,128)} %copy-done) | copy-start | bytes 16515076
  42.3 2.6 %copy-start.4 = (f32[14,768,128]{2,1,0:T(8,128)S(1)}, f32[14,768,128]{2,1,0:T(8,128)}, u32[]{:S(2)}) copy-start(f32[14,768,128]{2,1,0:T(8,128)} %copy-done.3) | copy-start | bytes 16515076

commit v3 on v2

--- a/solution.py
+++ b/solution.py
@@ -33,7 +33,9 @@
 FIELDS = 14
 FLOWS = 5
 LAYERS = 4 * FIELDS + FLOWS
+FIRST = 5
 MIB = 1 << 20
+LONG = pl.CostEstimate(flops=10**10, bytes_accessed=10**6, transcendentals=0)
 F32 = jnp.float32
 BF16 = jnp.bfloat16
 
@@ -53,11 +55,9 @@
     return table
 
 
-def ring(axis):
+def ring(axis, distance):
     count = lax.axis_size(axis)
-    forward = [(i, (i + 1) % count) for i in range(count)]
-    backward = [(target, source) for source, target in forward]
-    return forward, backward
+    return [(i, (i + distance) % count) for i in range(count)]
 
 
 def lane_cell(lane):
@@ -128,18 +128,8 @@
     return [pl.BlockSpec(memory_space=pltpu.HBM)] * count
 
 
-def wrapped(start, size, depth):
-    pieces = []
-    at = start
-    while at < start + size:
-        inside = at % depth
-        length = min(start + size - at, depth - inside)
-        pieces.append(((at - start) * 16, length * 16, inside * 16))
-        at += length
-    return pieces
-
-
-def probe_kernel(count, fields_ref, prim, main_ref, held, progress, arrived):
+def probe_kernel(count, fields_ref, prim, *refs):
+    blocks, (held, progress, arrived) = refs[:count], refs[count:]
     rows = prim.shape[1]
     depth = rows // 16
     own = depth // count
@@ -183,14 +173,17 @@
 
     lax.fori_loop(0, rows // chunk, chunk_body, 0)
 
-    for j in range(count):
+    me = lax.axis_index("gy")
+    for distance in range(count):
+        first = own * lax.rem(me + distance, count) + depth
         offset = 0
         for c in range(4):
             margin = 2 if c == 0 else 1
-            for to, length, source in wrapped(own * j - margin, own + 2 * margin, depth):
-                piece = progress[source : source + length, :] if c == 0 else prim[c - 1, source : source + length, :]
-                main_ref[j, offset + to : offset + to + length, :] = piece.astype(BF16)
-            offset += (own + 2 * margin) * 16
+            for z in range(-margin, own + margin):
+                at = pl.ds(pl.multiple_of(lax.rem(first + z, depth) * 16, 16), 16)
+                plane = progress[at, :] if c == 0 else prim[c - 1, at, :]
+                blocks[distance][offset : offset + 16, :] = plane.astype(BF16)
+                offset += 16
 
 
 def probe_part(fields, count):
@@ -200,18 +193,16 @@
     return pl.pallas_call(
         functools.partial(probe_kernel, count),
         in_specs=in_hbm(1),
-        out_specs=in_vmem(2),
-        out_shape=[
-            jax.ShapeDtypeStruct((5, rows, 128), F32),
-            jax.ShapeDtypeStruct((count, main_rows, 128), BF16),
-        ],
+        out_specs=in_vmem(1 + count),
+        out_shape=[jax.ShapeDtypeStruct((5, rows, 128), F32)]
+        + [jax.ShapeDtypeStruct((main_rows, 128), BF16)] * count,
         scratch_shapes=[
             pltpu.VMEM((6, rows, 128), F32),
             pltpu.VMEM((rows, 128), F32),
             pltpu.SemaphoreType.DMA((2, rows // 256)),
         ],
         compiler_params=pltpu.CompilerParams(vmem_limit_bytes=48 * MIB),
-        cost_estimate=pl.CostEstimate(flops=30 * rows * 128, bytes_accessed=5 * MIB, transcendentals=0),
+        cost_estimate=LONG,
         name="probe_part",
     )(fields)
 
@@ -269,12 +260,15 @@
         ],
         scratch_shapes=[pltpu.SemaphoreType.DMA((rows // 256,))],
         compiler_params=pltpu.CompilerParams(vmem_limit_bytes=40 * MIB),
-        cost_estimate=pl.CostEstimate(flops=100 * rows * 128, bytes_accessed=6 * MIB, transcendentals=0),
+        cost_estimate=LONG,
         name="faces_part",
     )(fields, prim)
 
 
-def lines_kernel(flat, prim, weights_ref, terms, low_ref, high_ref, total):
+def lines_kernel(flat, prim, weights_ref, low_block, high_block, terms, low_ref, high_ref, total):
+    start = low_block.shape[0]
+    low_ref[0:start, :] = low_block[...]
+    high_ref[0:start, :] = high_block[...]
     rows = flat.shape[1]
     half = rows // 2
 
@@ -303,26 +297,27 @@
     second = lanes % 64 >= 4 * FIELDS
     value = jnp.where(second, value - value.astype(BF16).astype(F32), value)
     turned = pltpu.roll(value, 64, 1)
-    low_ref[...] = jnp.where(lanes < 64, value[0:half, :], turned[half:rows, :]).astype(BF16)
-    high_ref[...] = jnp.where(lanes < 64, turned[0:half, :], value[half:rows, :]).astype(BF16)
-
-
-def lines_part(flat, prim):
+    low_ref[start:, :] = jnp.where(lanes < 64, value[0:half, :], turned[half:rows, :]).astype(BF16)
+    high_ref[start:, :] = jnp.where(lanes < 64, turned[0:half, :], value[half:rows, :]).astype(BF16)
+
+
+def lines_part(flat, prim, low_block, high_block):
     rows = flat.shape[1]
+    message = low_block.shape[0] + rows // 2
     return pl.pallas_call(
         lines_kernel,
-        in_specs=in_vmem(3),
+        in_specs=in_vmem(5),
         out_specs=in_vmem(3),
         out_shape=[
             jax.ShapeDtypeStruct((FIELDS, rows, 256), BF16),
-            jax.ShapeDtypeStruct((rows // 2, 128), BF16),
-            jax.ShapeDtypeStruct((rows // 2, 128), BF16),
+            jax.ShapeDtypeStruct((message, 128), BF16),
+            jax.ShapeDtypeStruct((message, 128), BF16),
         ],
         scratch_shapes=[pltpu.VMEM((rows, 128), F32)],
         compiler_params=pltpu.CompilerParams(vmem_limit_bytes=12 * MIB),
-        cost_estimate=pl.CostEstimate(flops=300 * rows * 128, bytes_accessed=8 * MIB, transcendentals=0),
+        cost_estimate=LONG,
         name="lines_part",
-    )(flat, prim, jnp.asarray(face_matrix(), BF16))
+    )(flat, prim, jnp.asarray(face_matrix(), BF16), low_block, high_block)
 
 
 def sources(species, stress):
@@ -436,29 +431,28 @@
             pltpu.VMEM((rows, 128), F32),
         ],
         compiler_params=pltpu.CompilerParams(vmem_limit_bytes=12 * MIB),
-        cost_estimate=pl.CostEstimate(
-            flops=2000 * rows * 128, bytes_accessed=20 * MIB, transcendentals=10 * rows * 128
-        ),
+        cost_estimate=LONG,
         name="inner_part",
     )(flat, prim, register, terms, jnp.asarray(line_matrix(), BF16), jnp.asarray(planes_matrix(), BF16))
 
 
-def outer_kernel(
-    part, flat, prev, following, yprev, ynext, place_ref, fields_out, register_out,
+def add_faces(
+    chosen, part, flat, prev, following, yprev, ynext, place_ref, fields_out, register_out,
     faces_x, along_y, message, fields_stage, register_stage, sent,
 ):
     rows = part.shape[1]
     depth = rows // 16
     half = rows // 2
     lanes = lax.broadcasted_iota(jnp.int32, (1, 128), 1)
-    low = ynext[...].astype(F32)
-    high = yprev[...].astype(F32)
+    start = ynext.shape[0] - half
+    low = ynext[start:, :].astype(F32)
+    high = yprev[start:, :].astype(F32)
     message[0:half, :] = jnp.where(lanes < 64, low, pltpu.roll(high, 64, 1)).astype(BF16)
     message[half:rows, :] = jnp.where(lanes < 64, pltpu.roll(low, 64, 1), high).astype(BF16)
     faces_x[...] = jnp.zeros(faces_x.shape, F32)
     place = place_ref[...]
     copies = []
-    for field in range(FIELDS):
+    for slot, field in enumerate(chosen):
         for ref, layers in ((prev, (0, 1, 2, 3)), (following, (15, 14, 13, 12))):
             for cell, x in enumerate(layers):
                 value = ref[4 * field + cell, :, :].astype(F32)
@@ -469,37 +463,43 @@
         picked = jnp.where(lane_mask(field), held, jnp.zeros_like(held))
         along_y[...] = jnp.dot(picked, place, preferred_element_type=F32)
         stored = part[field] - TIME_STEP * (along_y[...] + faces_x[...])
-        register_stage[field] = stored
-        fields_stage[field] = flat[field] + SECTION_WEIGHT * stored
+        register_stage[slot] = stored
+        fields_stage[slot] = flat[field] + SECTION_WEIGHT * stored
         for index, (stage, ref) in enumerate(((register_stage, register_out), (fields_stage, fields_out))):
-            copy = pltpu.make_async_copy(stage.at[field], ref.at[field], sent.at[index, field])
+            copy = pltpu.make_async_copy(stage.at[slot], ref.at[field], sent.at[index, slot])
             copy.start()
             copies.append(copy)
-    for copy in copies:
+    return copies
+
+
+def faces_scratch(number, rows):
+    return [
+        pltpu.VMEM((rows, 128), F32),
+        pltpu.VMEM((rows, 128), F32),
+        pltpu.VMEM((rows, 128), BF16),
+        pltpu.VMEM((number, rows, 128), F32),
+        pltpu.VMEM((number, rows, 128), F32),
+        pltpu.SemaphoreType.DMA((2, number)),
+    ]
+
+
+def outer_kernel(chosen, *refs):
+    for copy in add_faces(chosen, *refs):
         copy.wait()
 
 
-def outer_part(part, flat, prev, following, yprev, ynext):
-    rows = flat.shape[1]
+def outer_part(chosen, operands):
+    rows = operands[0].shape[1]
     return pl.pallas_call(
-        outer_kernel,
+        functools.partial(outer_kernel, chosen),
         in_specs=in_vmem(7),
         out_specs=in_hbm(2),
         out_shape=[jax.ShapeDtypeStruct((FIELDS, rows, 128), F32)] * 2,
-        scratch_shapes=[
-            pltpu.VMEM((rows, 128), F32),
-            pltpu.VMEM((rows, 128), F32),
-            pltpu.VMEM((rows, 128), BF16),
-            pltpu.VMEM((FIELDS, rows, 128), F32),
-            pltpu.VMEM((FIELDS, rows, 128), F32),
-            pltpu.SemaphoreType.DMA((2, FIELDS)),
-        ],
-        compiler_params=pltpu.CompilerParams(vmem_limit_bytes=20 * MIB),
-        cost_estimate=pl.CostEstimate(
-            flops=100 * rows * 128, bytes_accessed=24 * MIB, transcendentals=0
-        ),
+        scratch_shapes=faces_scratch(len(chosen), rows),
+        compiler_params=pltpu.CompilerParams(vmem_limit_bytes=12 * MIB),
+        cost_estimate=LONG,
         name="outer_part",
-    )(part, flat, prev, following, yprev, ynext, jnp.asarray(place_matrix(), BF16))
+    )(*operands)
 
 
 def lane_difference(values):
@@ -514,21 +514,34 @@
     ]
 
 
+def in_pairs(total, work):
+    together = 2 if total % 2 == 0 else 1
+
+    def body(step, carry):
+        for offset in range(together):
+            work(step * together + offset)
+        return carry
+
+    lax.fori_loop(0, total // together, body, 0)
+
+
 def inverse_length(a, b, c):
     return 1.0 * lax.rsqrt(jnp.maximum(a * a + b * b + c * c, GRAD_FLOOR * GRAD_FLOOR))
 
 
-def unpack_kernel(count, own, blocks, scalar, speed, low_ref, high_ref, edge):
+def unpack_kernel(count, own, *refs):
+    blocks, (scalar, speed, low_ref, high_ref, edge) = refs[:count], refs[count:]
     edge[...] = jnp.zeros(edge.shape, F32)
-
-    def body(j, carry):
+    me = lax.axis_index("gy")
+    for distance, block in enumerate(blocks):
+        j = lax.rem(me - distance + count, count)
         for z in range(own + 4):
-            scalar[j, z * 32 + 8 : z * 32 + 24, :] = blocks[j, z * 16 : z * 16 + 16, :].astype(F32)
+            scalar[j, z * 32 + 8 : z * 32 + 24, :] = block[z * 16 : z * 16 + 16, :].astype(F32)
         for c in range(3):
             base = (own + 4 + c * (own + 2)) * 16
             for z in range(own + 2):
-                speed[c, j, z * 32 + 8 : z * 32 + 24, :] = blocks[
-                    j, base + z * 16 : base + z * 16 + 16, :
+                speed[c, j, z * 32 + 8 : z * 32 + 24, :] = block[
+                    base + z * 16 : base + z * 16 + 16, :
                 ].astype(F32)
         for ref, first, second in ((low_ref, 8, 9), (high_ref, 23, 22)):
             edge[0 : own + 2, :] = scalar[j, pl.ds(32 + first, own + 2, stride=32), :]
@@ -537,17 +550,14 @@
                 start = (c + 2) * own + 2
                 edge[start : start + own, :] = speed[c, j, pl.ds(32 + first, own, stride=32), :]
             ref[j, :, :] = edge[...].astype(BF16)
-        return carry
-
-    lax.fori_loop(0, count, body, 0)
 
 
 def unpack_part(blocks, own):
-    count = blocks.shape[0]
+    count = len(blocks)
     edge_rows = -(-(5 * own + 2) // 16) * 16
     return pl.pallas_call(
         functools.partial(unpack_kernel, count, own),
-        in_specs=in_vmem(1),
+        in_specs=in_vmem(count),
         out_specs=in_vmem(4),
         out_shape=[
             jax.ShapeDtypeStruct((count, (own + 4) * 32, 128), F32),
@@ -557,16 +567,17 @@
         ],
         scratch_shapes=[pltpu.VMEM((edge_rows, 128), F32)],
         compiler_params=pltpu.CompilerParams(vmem_limit_bytes=4 * MIB),
-        cost_estimate=pl.CostEstimate(
-            flops=10 * own * 16 * 128 * count, bytes_accessed=5 * MIB, transcendentals=0
-        ),
+        cost_estimate=LONG,
         name="unpack_part",
-    )(blocks)
-
-
-def metrics_kernel(
-    count, own, scalar_in, speed_in, prev, following, scalar, speed, out_ref, normal, normal_z, edge, stage, sent
-):
+    )(*blocks)
+
+
+def finish_kernel(count, own, chosen, *refs):
+    operands, refs = refs[:7], refs[7:]
+    scalar_in, speed_in, prev, following, _, _ = refs[:6]
+    fields_out, register_out, scalar, speed, out_ref = refs[6:11]
+    scratch, (normal, normal_z, edge, stage, sent) = refs[11:17], refs[17:]
+    copies = add_faces(chosen, *operands, fields_out, register_out, *scratch)
     half = prev.shape[1]
     edge[:, 0:half, :] = prev[...].astype(F32)
     edge[:, half:, :] = following[...].astype(F32)
@@ -593,7 +604,7 @@
     def window(z, row):
         return pl.ds(pl.multiple_of(z * 32, 32) + row, 16)
 
-    def find_normals(z, carry):
+    def find_normals(z):
         along_y = lane_difference([scalar[j, window(z + 1, 8), :] for j in range(count)])
         for j in range(count):
             grad_x = 0.5 * (scalar[j, window(z + 1, 9), :] - scalar[j, window(z + 1, 7), :])
@@ -603,11 +614,10 @@
             normal[0, j, window(z, 8), :] = grad_x * scale
             normal[1, j, window(z, 8), :] = grad_y * scale
             normal_z[j, z, :, :] = grad_z * scale
-        return carry
-
-    lax.fori_loop(0, own + 2, find_normals, 0)
-
-    def find_metrics(z, carry):
+
+    in_pairs(own + 2, find_normals)
+
+    def find_metrics(z):
         curve_y = lane_difference([normal[1, j, window(z + 1, 8), :] for j in range(count)])
         speed_y = [
             lane_difference([speed[c, j, window(z + 1, 8), :] for j in range(count)])
@@ -638,39 +648,43 @@
             for index, value in enumerate(normals + [curvature, 0.5 * strain]):
                 stage[index, z, :, lanes] = value.astype(BF16)
         pltpu.make_async_copy(stage.at[:, z], out_ref.at[:, z], sent.at[z]).start()
-        return carry
-
-    lax.fori_loop(0, own, find_metrics, 0)
+
+    in_pairs(own, find_metrics)
+    for copy in copies:
+        copy.wait()
     for z in range(own):
         pltpu.make_async_copy(stage.at[:, z], out_ref.at[:, z], sent.at[z]).wait()
 
 
-def metrics_part(scalar, speed, prev, following, own):
+def finish_part(chosen, operands, scalar, speed, prev, following, fields, register, own):
     count, half = prev.shape[:2]
+    rows = fields.shape[1]
     shape = (5, own, 16, count * 128)
-    return pl.pallas_call(
-        functools.partial(metrics_kernel, count, own),
-        in_specs=in_vmem(4),
-        out_specs=in_vmem(2) + in_hbm(1),
+    fields, register, _, _, metrics = pl.pallas_call(
+        functools.partial(finish_kernel, count, own, chosen),
+        in_specs=in_vmem(11) + in_hbm(2),
+        out_specs=in_hbm(2) + in_vmem(2) + in_hbm(1),
         out_shape=[
+            jax.ShapeDtypeStruct(fields.shape, F32),
+            jax.ShapeDtypeStruct(register.shape, F32),
             jax.ShapeDtypeStruct(scalar.shape, F32),
             jax.ShapeDtypeStruct(speed.shape, F32),
             jax.ShapeDtypeStruct(shape, BF16),
         ],
-        input_output_aliases={0: 0, 1: 1},
-        scratch_shapes=[
+        input_output_aliases={7: 2, 8: 3, 11: 0, 12: 1},
+        scratch_shapes=faces_scratch(len(chosen), rows)
+        + [
             pltpu.VMEM((2, count, (own + 2) * 32, 128), F32),
             pltpu.VMEM((count, own + 2, 16, 128), F32),
             pltpu.VMEM((count, 2 * half, 128), F32),
             pltpu.VMEM(shape, BF16),
             pltpu.SemaphoreType.DMA((own,)),
         ],
-        compiler_params=pltpu.CompilerParams(vmem_limit_bytes=10 * MIB),
-        cost_estimate=pl.CostEstimate(
-            flops=300 * own * 16 * 128 * count, bytes_accessed=3 * MIB, transcendentals=0
-        ),
-        name="flame_metrics",
-    )(scalar, speed, prev, following)[2]
+        compiler_params=pltpu.CompilerParams(vmem_limit_bytes=20 * MIB),
+        cost_estimate=LONG,
+        name="finish_part",
+    )(*operands, scalar, speed, prev, following, fields, register)
+    return fields, register, metrics
 
 
 def per_device(fields, register):
@@ -678,25 +692,33 @@
     given = fields.reshape(FIELDS, depth * count_x, count_y)
     count = lax.axis_size("gy")
     own = depth // count
-    x_forward, x_backward = ring("gx")
-    y_forward, y_backward = ring("gy")
-
-    prim, main = probe_part(given, count)
-    blocks = lax.all_to_all(main, "gy", 0, 0, tiled=True)
+    x_forward, x_backward = ring("gx", 1), ring("gx", -1)
+
+    prim, *blocks = probe_part(given, count)
+    for distance in range(2, count - 1):
+        blocks[distance] = lax.ppermute(blocks[distance], "gy", ring("gy", distance))
     flat, low, high = faces_part(given, prim)
+    terms, to_prev, to_next = lines_part(flat, prim, blocks[count - 1], blocks[1])
+    blocks[count - 1] = lax.ppermute(to_prev, "gy", ring("gy", -1))
+    blocks[1] = lax.ppermute(to_next, "gy", ring("gy", 1))
+    low, high, terms = lax.optimization_barrier((low, high, terms))
     following = lax.ppermute(low, "gx", x_backward)
     prev = lax.ppermute(high, "gx", x_forward)
-    terms, ylow, yhigh = lines_part(flat, prim)
-    ynext = lax.ppermute(ylow, "gy", y_backward)
-    yprev = lax.ppermute(yhigh, "gy", y_forward)
     part = inner_part(flat, prim, register.reshape(flat.shape), terms)
-    blocks, part = lax.optimization_barrier((blocks, part))
+    *blocks, part = lax.optimization_barrier((*blocks, part))
     scalar, speed, edge_low, edge_high = unpack_part(blocks, own)
     edge_prev = lax.ppermute(edge_high, "gx", x_forward)
     edge_next = lax.ppermute(edge_low, "gx", x_backward)
     part, scalar = lax.optimization_barrier((part, scalar))
-    fields_next, register_next = outer_part(part, flat, prev, following, yprev, ynext)
-    metrics = metrics_part(scalar, speed, edge_prev, edge_next, own)
+    operands = (
+        part, flat, prev, following, blocks[1], blocks[count - 1], jnp.asarray(place_matrix(), BF16)
+    )
+    first, last = tuple(range(FIRST)), tuple(range(FIRST, FIELDS))
+    fields_next, register_next = outer_part(first, operands)
+    edge_prev, edge_next, fields_next = lax.optimization_barrier((edge_prev, edge_next, fields_next))
+    fields_next, register_next, metrics = finish_part(
+        last, operands, scalar, speed, edge_prev, edge_next, fields_next, register_next, own
+    )
     return (fields_next.reshape(fields.shape), register_next.reshape(fields.shape), metrics)
 
 

time: 56.3 us -> 43.4 us (0.77)
  local copies, waits for them, and re-layouts: 11.1 us -> 0.04 us
  waiting for transfers between devices: 2.01 us -> 6.41 us
  Pallas kernels: 26.2 us -> 22.8 us
  starting transfers between devices: 15.8 us -> 13.3 us
    unnamed x22 -> x14, local copies, waits for them, and re-layouts: 11.1 us -> 0.04 us
    all_to_all x1 -> x0, starting transfers between devices: 6.45 us -> none  [per_device(): blocks = lax.all_to_all(main, 'gy', 0, 0, tiled=True)]
    ppermute x2 -> x3, waiting for transfers between devices: 0.01 us -> 6.4 us  [the longest x1 6.32 us: per_device(): blocks[count - 1] = lax.ppermute(to_prev, 'gy', ring('gy', -1))]
    ppermute x2 -> x3, starting transfers between devices: 3.94 us -> 7.98 us  [the longest x1 4.1 us: per_device(): lax.ppermute(blocks[distance], 'gy', ring('gy', distance))]
    pallas_call x3, Pallas kernels: 13.9 us -> 11 us  [the longest x1 5.56 us: finish_part(): pl.pallas_call(functools.partial(finish_kernel, count, own, chosen), in_s...]
    all_to_all x1 -> x0, waiting for transfers between devices: 1.99 us -> none  [per_device(): blocks = lax.all_to_all(main, 'gy', 0, 0, tiled=True)]
    pallas_call x1, Pallas kernels: 2.63 us -> 1.67 us  [faces_part(): pl.pallas_call(faces_kernel, in_specs=in_hbm(1) + in_vmem(1), out_specs=i...]
  transfers between devices with their start and end apart: 7 -> 7, of which waited for: 1 -> 2; matrix products, arithmetic and copies ran while one was open for 0% -> 0% of each run, Pallas kernels for 36% -> 35%
where the time goes in v3:
time: 43.4 us; the launch traced here: 43.3 us
  Pallas kernels  22.8 us (53%)
  starting transfers between devices  13.3 us (31%)
  waiting for transfers between devices  6.41 us (15%)
  between operations  0.74 us (2%)
    pallas_call x1, Pallas kernels, inner_part(): pl.pallas_call(inner_kernel, in_specs=in_vmem(6), out_specs=pl.BlockSpec(...  7.66 us
    ppermute x1, waiting for transfers between devices, per_device(): blocks[count - 1] = lax.ppermute(to_prev, 'gy', ring('gy', -1))  6.32 us
    pallas_call x1, Pallas kernels, finish_part(): pl.pallas_call(functools.partial(finish_kernel, count, own, chosen), in_s...  5.56 us
    ppermute x1, starting transfers between devices, per_device(): lax.ppermute(blocks[distance], 'gy', ring('gy', distance))  4.1 us
    pallas_call x1, Pallas kernels, lines_part(): pl.pallas_call(lines_kernel, in_specs=in_vmem(5), out_specs=in_vmem(3), o...  2.91 us
    ppermute x1, starting transfers between devices, per_device(): following = lax.ppermute(low, 'gx', x_backward)  2.64 us
    ppermute x1, starting transfers between devices, per_device(): edge_next = lax.ppermute(edge_low, 'gx', x_backward)  2.63 us
    pallas_call x1, Pallas kernels, outer_part(): pl.pallas_call(functools.partial(outer_kernel, chosen), in_specs=in_vmem(...  2.55 us
  transfers between devices with their start and end apart: 7, of which 2 were waited for; matrix products, arithmetic and copies ran while one was open for 0% of the time, Pallas kernels for 35%

profile of v3, /device:TPU:0, one launch (start us, length us, event | category | flops | bytes accessed | tf_op | source)
XLA Modules:
  0.0 43.3 jit_solution(12934470258870726004)
XLA Ops:
  0.6 0.0 copy-start
  0.6 2.0 %probe_part.1 = (f32[5,768,128]{2,1,0:T(8,128)S(1)}, bf16[928,128]{1,0:T(8,128)(2,1)S(1)}, bf16[928,128]{1,0:T(8,128)(2,1)S(1)}, bf16[928,128]{1,0:T(8,128)(2,1)S(1)}, bf16[928,128]{1,0:T(8,128)(2,1)S(1)}) custom-call(f32[14,768,128]{2,1,0:T(8,128)} %bitcast.4), custom_call_target="tpu_custom_call" | custom-call | flops 10000000000 | bytes 1000000 | tf_op jit(solution)/shard_map/probe_part/pallas_call | solution.py:193
  2.7 4.1 %collective-permute-start.1 = (bf16[928,128]{1,0:T(8,128)(2,1)S(1)}, bf16[928,128]{1,0:T(8,128)(2,1)S(1)}, u32[]{:S(2)}, u32[]{:S(2)}) collective-permute-start(bf16[928,128]{1,0:T(8,128)(2,1)S(1)} %get-tuple-element.42), channel_id=1, source_target_pairs={{0,2},{1,3},{2,0},{3,1},{4,6},{5,7},{6,4},{7,5},{8,10},{9,11},{10,... | collective-permute-start | bytes 712712 | tf_op jit(solution)/shard_map/ppermute | solution.py:699
  6.8 0.0 copy-done
  6.8 0.0 copy-start.3
  6.8 0.0 slice-start
  6.8 1.7 %faces_part.1 = (f32[14,768,128]{2,1,0:T(8,128)S(1)}, bf16[61,48,128]{2,1,0:T(8,128)(2,1)S(1)}, bf16[61,48,128]{2,1,0:T(8,128)(2,1)S(1)}) custom-call(f32[14,768,128]{2,1,0:T(8,128)S(1)} %bitcast.5, f32[5,768,128]{2,1,0:T(8,128)S(1)} %get-tuple-element.37.prim), custom_call_target="tpu_custom_call" | custom-call | flops 10000000000 | bytes 1000000 | tf_op jit(solution)/shard_map/faces_part/pallas_call | solution.py:252
  8.5 0.0 copy-done.3
  8.5 0.0 slice-start.1
  8.5 0.0 copy-start.1
  8.5 0.0 copy-start.2
  8.5 2.9 %lines_part.1 = (bf16[14,768,256]{2,1,0:T(8,128)(2,1)S(1)}, bf16[1312,128]{1,0:T(8,128)(2,1)S(1)}, bf16[1312,128]{1,0:T(8,128)(2,1)S(1)}) custom-call(f32[14,768,128]{2,1,0:T(8,128)S(1)} %get-tuple-element.38.flat.refs_1_, f32[5,768,128]{2,1,0:T(8,128)S(1)} %get-tuple-element.37.prim, bf16[256,128]{1,0:T(8,128)(2,1)S(1)} %copy-done.3, ...), custom_call_target="tpu_custom_call" | custom-call | flops 10000000000 | bytes 1000000 | tf_op jit(solution)/shard_map/lines_part/pallas_call | solution.py:307
  11.4 1.6 %collective-permute-start = (bf16[1312,128]{1,0:T(8,128)(2,1)S(1)}, bf16[1312,128]{1,0:T(8,128)(2,1)S(1)}, u32[]{:S(2)}, u32[]{:S(2)}) collective-permute-start(bf16[1312,128]{1,0:T(8,128)(2,1)S(1)} %get-tuple-element.41), channel_id=1, source_target_pairs={{0,1},{1,2},{2,3},{3,0},{4,5},{5,6},{6,7},{7,4},{8,9},{9,10},{10,1... | collective-permute-start | bytes 1007624 | tf_op jit(solution)/shard_map/ppermute | solution.py:703
  13.1 2.2 %collective-permute-start.2 = (bf16[1312,128]{1,0:T(8,128)(2,1)S(1)}, bf16[1312,128]{1,0:T(8,128)(2,1)S(1)}, u32[]{:S(2)}, u32[]{:S(2)}) collective-permute-start(bf16[1312,128]{1,0:T(8,128)(2,1)S(1)} %get-tuple-element.43), channel_id=1, source_target_pairs={{0,3},{1,0},{2,1},{3,2},{4,7},{5,4},{6,5},{7,6},{8,11},{9,8},{10,9... | collective-permute-start | bytes 1007624 | tf_op jit(solution)/shard_map/ppermute | solution.py:702
  15.3 0.0 collective-permute-start.3
  15.3 2.6 %collective-permute-start.4 = (bf16[61,48,128]{2,1,0:T(8,128)(2,1)S(1)}, bf16[61,48,128]{2,1,0:T(8,128)(2,1)S(1)}, u32[]{:S(2)}, u32[]{:S(2)}) collective-permute-start(bf16[61,48,128]{2,1,0:T(8,128)(2,1)S(1)} %get-tuple-element.56), channel_id=1, source_target_pairs={{0,28},{4,0},{8,4},{12,8},{16,12},{20,16},{24,20},{28,24},{1,29},{... | collective-permute-start | bytes 2248712 | tf_op jit(solution)/shard_map/ppermute | solution.py:705
  18.0 0.0 slice-done
  18.0 0.0 slice-done.1
  18.0 0.0 copy-done.1
  18.0 0.0 copy-done.2
  18.0 7.7 %inner_part.1.refs_0_ = f32[14,768,128]{2,1,0:T(8,128)S(1)} custom-call(f32[14,768,128]{2,1,0:T(8,128)S(1)} %get-tuple-element.38.flat.refs_1_, f32[5,768,128]{2,1,0:T(8,128)S(1)} %get-tuple-element.37.prim, f32[14,768,128]{2,1,0:T(8,128)S(1)} %bitcast.8, bf16[14,768,256]{2,1,0:T(8,128)(2,1)S(1)} %get-tuple-element.47.terms, bf16[256,128]{1,0:T(8,128)(2,1)S(1)} %copy-done.2, ...), custom_call_target="tpu_custom_call" | custom-call | flops 10000000000 | bytes 1000000 | tf_op jit(solution)/shard_map/inner_part/pallas_call | solution.py:425
  25.7 0.1 collective-permute-done.1.refs_2_
  25.7 0.0 collective-permute-done.refs_1_.refs_4_
  25.7 6.3 %collective-permute-done.2.refs_3_.refs_5_ = bf16[1312,128]{1,0:T(8,128)(2,1)S(1)} collective-permute-done((bf16[1312,128]{1,0:T(8,128)(2,1)S(1)}, bf16[1312,128]{1,0:T(8,128)(2,1)S(1)}, u32[]{:S(2)}, u32[]{:S(2)}) %collective-permute-start.2) | collective-permute-done | bytes 335904 | tf_op jit(solution)/shard_map/ppermute | solution.py:702
  32.1 0.0 copy-start.4
  32.1 0.4 unpack_part.1
  32.4 0.1 collective-permute-start.5
  32.5 2.6 %collective-permute-start.6 = (bf16[4,64,128]{2,1,0:T(8,128)(2,1)S(1)}, bf16[4,64,128]{2,1,0:T(8,128)(2,1)S(1)}, u32[]{:S(2)}, u32[]{:S(2)}) collective-permute-start(bf16[4,64,128]{2,1,0:T(8,128)(2,1)S(1)} %get-tuple-element.60), channel_id=1, source_target_pairs={{0,28},{4,0},{8,4},{12,8},{16,12},{20,16},{24,20},{28,24},{1,29},{... | collective-permute-start | bytes 196616 | tf_op jit(solution)/shard_map/ppermute | solution.py:711
  35.1 0.0 collective-permute-done.3.refs_2_
  35.1 0.0 collective-permute-done.4.refs_3_
  35.1 0.0 copy-done.4
  35.1 2.5 %outer_part.1 = (f32[14,768,128]{2,1,0:T(8,128)}, f32[14,768,128]{2,1,0:T(8,128)}) custom-call(f32[14,768,128]{2,1,0:T(8,128)S(1)} %inner_part.1.refs_0_, f32[14,768,128]{2,1,0:T(8,128)S(1)} %get-tuple-element.38.flat.refs_1_, bf16[61,48,128]{2,1,0:T(8,128)(2,1)S(1)} %collective-permute-done.3.refs_2_, ...), custom_call_target="tpu_custom_call" | custom-call | flops 10000000000 | bytes 1000000 | tf_op jit(solution)/shard_map/outer_part/pallas_call | solution.py:493
  37.7 0.0 collective-permute-done.5.refs_9_
  37.7 0.0 collective-permute-done.6.refs_10_
  37.7 5.6 %finish_part.1 = (f32[14,768,128]{2,1,0:T(8,128)}, f32[14,768,128]{2,1,0:T(8,128)}, f32[4,512,128]{2,1,0:T(8,128)S(1)}, f32[3,4,448,128]{3,2,1,0:T(8,128)S(1)}, bf16[5,12,16,512]{3,2,1,0:T(8,128)(2,1)}) custom-call(f32[14,768,128]{2,1,0:T(8,128)S(1)} %inner_part.1.refs_0_, ...), custom_call_target="tpu_custom_call", output_to_operand_aliasing={{2}: (7, {}), {3}: (8, {}), {0}: (11, {}), {1}: (12, {})} | custom-call | flops 10000000000 | bytes 1000000 | tf_op jit(solution)/shard_map/finish_part/pallas_call | solution.py:663
  (1 shorter events, 0.0 us)
Async XLA Ops:
  0.6 6.2 %copy-start = (f32[14,48,16,128]{3,2,1,0:T(8,128)S(1)}, f32[14,48,16,128]{3,2,1,0:T(8,128)}, u32[]{:S(2)}) copy-start(f32[14,48,16,128]{3,2,1,0:T(8,128)} %param.6) | copy-start | bytes 16515076
  2.7 23.0 %collective-permute-start.1 = (bf16[928,128]{1,0:T(8,128)(2,1)S(1)}, bf16[928,128]{1,0:T(8,128)(2,1)S(1)}, u32[]{:S(2)}, u32[]{:S(2)}) collective-permute-start(bf16[928,128]{1,0:T(8,128)(2,1)S(1)} %get-tuple-element.42), channel_id=1, source_target_pairs={{0,2},{1,3},{2,0},{3,1},{4,6},{5,7},{6,4},{7,5},{8,10},{9,11},{10,... | collective-permute-start | bytes 712712 | tf_op jit(solution)/shard_map/ppermute | solution.py:699
  6.8 1.7 %copy-start.3 = (bf16[256,128]{1,0:T(8,128)(2,1)S(1)}, bf16[256,128]{1,0:T(8,128)(2,1)}, u32[]{:S(2)}) copy-start(bf16[256,128]{1,0:T(8,128)(2,1)} %constant.8.clone.weights_ref) | copy-start | bytes 196612
  6.8 11.2 %slice-start = ((s8[5505024]{0:T(1024)(128)(4,1)}), s8[1310720]{0:T(1024)(128)(4,1)S(1)}, s32[]{:S(2)}) async-start(s8[5505024]{0:T(1024)(128)(4,1)} %bitcast.6), calls=%async_computation | async-start | bytes 2621440
  8.5 9.5 %slice-start.1 = ((s8[5505024]{0:T(1024)(128)(4,1)}), s8[4194304]{0:T(1024)(128)(4,1)S(1)}, s32[]{:S(2)}) async-start(s8[5505024]{0:T(1024)(128)(4,1)} %bitcast.6), calls=%async_computation.1 | async-start | bytes 8388608
  8.5 9.5 %copy-start.1 = (bf16[128,256]{1,0:T(8,128)(2,1)S(1)}, bf16[128,256]{1,0:T(8,128)(2,1)}, u32[]{:S(2)}) copy-start(bf16[128,256]{1,0:T(8,128)(2,1)} %constant.10.clone.planes_ref) | copy-start | bytes 196612
  8.5 9.5 %copy-start.2 = (bf16[256,128]{1,0:T(8,128)(2,1)S(1)}, bf16[256,128]{1,0:T(8,128)(2,1)}, u32[]{:S(2)}) copy-start(bf16[256,128]{1,0:T(8,128)(2,1)} %constant.9.clone.line_ref) | copy-start | bytes 196612
  11.4 14.3 %collective-permute-start = (bf16[1312,128]{1,0:T(8,128)(2,1)S(1)}, bf16[1312,128]{1,0:T(8,128)(2,1)S(1)}, u32[]{:S(2)}, u32[]{:S(2)}) collective-permute-start(bf16[1312,128]{1,0:T(8,128)(2,1)S(1)} %get-tuple-element.41), channel_id=1, source_target_pairs={{0,1},{1,2},{2,3},{3,0},{4,5},{5,6},{6,7},{7,4},{8,9},{9,10},{10,1... | collective-permute-start | bytes 1007624 | tf_op jit(solution)/shard_map/ppermute | solution.py:703
  13.1 19.0 %collective-permute-start.2 = (bf16[1312,128]{1,0:T(8,128)(2,1)S(1)}, bf16[1312,128]{1,0:T(8,128)(2,1)S(1)}, u32[]{:S(2)}, u32[]{:S(2)}) collective-permute-start(bf16[1312,128]{1,0:T(8,128)(2,1)S(1)} %get-tuple-element.43), channel_id=1, source_target_pairs={{0,3},{1,0},{2,1},{3,2},{4,7},{5,4},{6,5},{7,6},{8,11},{9,8},{10,9... | collective-permute-start | bytes 1007624 | tf_op jit(solution)/shard_map/ppermute | solution.py:702
  15.3 19.8 %collective-permute-start.3 = (bf16[61,48,128]{2,1,0:T(8,128)(2,1)S(1)}, bf16[61,48,128]{2,1,0:T(8,128)(2,1)S(1)}, u32[]{:S(2)}, u32[]{:S(2)}) collective-permute-start(bf16[61,48,128]{2,1,0:T(8,128)(2,1)S(1)} %get-tuple-element.55), channel_id=1, source_target_pairs={{0,4},{4,8},{8,12},{12,16},{16,20},{20,24},{24,28},{28,0},{1,5},{5... | collective-permute-start | bytes 2248712 | tf_op jit(solution)/shard_map/ppermute | solution.py:706
  15.3 19.8 %collective-permute-start.4 = (bf16[61,48,128]{2,1,0:T(8,128)(2,1)S(1)}, bf16[61,48,128]{2,1,0:T(8,128)(2,1)S(1)}, u32[]{:S(2)}, u32[]{:S(2)}) collective-permute-start(bf16[61,48,128]{2,1,0:T(8,128)(2,1)S(1)} %get-tuple-element.56), channel_id=1, source_target_pairs={{0,28},{4,0},{8,4},{12,8},{16,12},{20,16},{24,20},{28,24},{1,29},{... | collective-permute-start | bytes 2248712 | tf_op jit(solution)/shard_map/ppermute | solution.py:705
  32.1 3.1 %copy-start.4 = (bf16[128,128]{1,0:T(8,128)(2,1)S(1)}, bf16[128,128]{1,0:T(8,128)(2,1)}, u32[]{:S(2)}) copy-start(bf16[128,128]{1,0:T(8,128)(2,1)} %constant.11.clone.refs_6_) | copy-start | bytes 98308
  32.4 5.3 %collective-permute-start.5 = (bf16[4,64,128]{2,1,0:T(8,128)(2,1)S(1)}, bf16[4,64,128]{2,1,0:T(8,128)(2,1)S(1)}, u32[]{:S(2)}, u32[]{:S(2)}) collective-permute-start(bf16[4,64,128]{2,1,0:T(8,128)(2,1)S(1)} %get-tuple-element.59), channel_id=1, source_target_pairs={{0,4},{4,8},{8,12},{12,16},{16,20},{20,24},{24,28},{28,0},{1,5},{5... | collective-permute-start | bytes 196616 | tf_op jit(solution)/shard_map/ppermute | solution.py:710
  32.5 5.2 %collective-permute-start.6 = (bf16[4,64,128]{2,1,0:T(8,128)(2,1)S(1)}, bf16[4,64,128]{2,1,0:T(8,128)(2,1)S(1)}, u32[]{:S(2)}, u32[]{:S(2)}) collective-permute-start(bf16[4,64,128]{2,1,0:T(8,128)(2,1)S(1)} %get-tuple-element.60), channel_id=1, source_target_pairs={{0,28},{4,0},{8,4},{12,8},{16,12},{20,16},{24,20},{28,24},{1,29},{... | collective-permute-start | bytes 196616 | tf_op jit(solution)/shard_map/ppermute | solution.py:711

commit v4 on v3

--- a/solution.py
+++ b/solution.py
@@ -128,8 +128,65 @@
     return [pl.BlockSpec(memory_space=pltpu.HBM)] * count
 
 
+def far_kernel(count, fields_ref, *refs):
+    far = count - 3
+    blocks, (held, arrived) = refs[:far], refs[far:]
+    depth = fields_ref.shape[1] // 16
+    own = depth // count
+    me = lax.axis_index("gy")
+    copies = []
+    for slot in range(far):
+        first = own * lax.rem(me + slot + 2, count)
+        for part, (begin, to, size) in enumerate(((first + depth - 2, 0, 2), (first, 2, own), (first + own, own + 2, 2))):
+            source = pl.ds(pl.multiple_of(lax.rem(begin, depth) * 16, 16), size * 16)
+            target = pl.ds(to * 16, size * 16)
+            for index, (low, high, place) in enumerate(((0, 4, 0), (9, 10, 4))):
+                copy = pltpu.make_async_copy(
+                    fields_ref.at[low:high, source, :],
+                    held.at[slot, place : place + high - low, target, :],
+                    arrived.at[slot, part, index],
+                )
+                copy.start()
+                copies.append(copy)
+    for slot in range(far):
+        for copy in copies[6 * slot : 6 * slot + 6]:
+            copy.wait()
+        planes = (own + 4) * 16
+        for at in range(0, planes, 64):
+            size = min(64, planes - at)
+            rows = slice(at, at + size)
+            density = held[slot, 0, rows, :]
+            scalar = PROGRESS_SCALE * (held[slot, 4, rows, :] / density)
+            blocks[slot][rows, :] = scalar.astype(BF16)
+        for c in range(1, 4):
+            base = planes + (c - 1) * (own + 2) * 16 - 16
+            for at in range(16, planes - 16, 32):
+                rows = slice(at, min(at + 32, planes - 16))
+                speed = held[slot, c, rows, :] / held[slot, 0, rows, :]
+                blocks[slot][base + rows.start : base + rows.stop, :] = speed.astype(BF16)
+
+
+def far_part(fields, count):
+    rows = fields.shape[1]
+    own = rows // 16 // count
+    far = count - 3
+    return pl.pallas_call(
+        functools.partial(far_kernel, count),
+        in_specs=in_hbm(1),
+        out_specs=in_vmem(far),
+        out_shape=[jax.ShapeDtypeStruct(((4 * own + 10) * 16, 128), BF16)] * far,
+        scratch_shapes=[
+            pltpu.VMEM((far, 5, (own + 4) * 16, 128), F32),
+            pltpu.SemaphoreType.DMA((far, 3, 2)),
+        ],
+        compiler_params=pltpu.CompilerParams(vmem_limit_bytes=52 * MIB),
+        cost_estimate=LONG,
+        name="far_part",
+    )(fields)
+
+
 def probe_kernel(count, fields_ref, prim, *refs):
-    blocks, (held, progress, arrived) = refs[:count], refs[count:]
+    blocks, (held, progress, arrived) = refs[:3], refs[3:]
     rows = prim.shape[1]
     depth = rows // 16
     own = depth // count
@@ -174,7 +231,7 @@
     lax.fori_loop(0, rows // chunk, chunk_body, 0)
 
     me = lax.axis_index("gy")
-    for distance in range(count):
+    for block, distance in zip(blocks, (0, 1, count - 1)):
         first = own * lax.rem(me + distance, count) + depth
         offset = 0
         for c in range(4):
@@ -182,7 +239,7 @@
             for z in range(-margin, own + margin):
                 at = pl.ds(pl.multiple_of(lax.rem(first + z, depth) * 16, 16), 16)
                 plane = progress[at, :] if c == 0 else prim[c - 1, at, :]
-                blocks[distance][offset : offset + 16, :] = plane.astype(BF16)
+                block[offset : offset + 16, :] = plane.astype(BF16)
                 offset += 16
 
 
@@ -193,9 +250,9 @@
     return pl.pallas_call(
         functools.partial(probe_kernel, count),
         in_specs=in_hbm(1),
-        out_specs=in_vmem(1 + count),
+        out_specs=in_vmem(4),
         out_shape=[jax.ShapeDtypeStruct((5, rows, 128), F32)]
-        + [jax.ShapeDtypeStruct((main_rows, 128), BF16)] * count,
+        + [jax.ShapeDtypeStruct((main_rows, 128), BF16)] * 3,
         scratch_shapes=[
             pltpu.VMEM((6, rows, 128), F32),
             pltpu.VMEM((rows, 128), F32),
@@ -207,20 +264,10 @@
     )(fields)
 
 
-def faces_kernel(fields_ref, prim, flat, low_ref, high_ref, arrived):
+def faces_kernel(flat, prim, low_ref, high_ref):
     rows = flat.shape[1]
 
-    def arrival(step):
-        there = pl.ds(pl.multiple_of(step * 256, 256), 256)
-        return pltpu.make_async_copy(
-            fields_ref.at[:, there, :], flat.at[:, there, :], arrived.at[step]
-        )
-
-    for step in range(rows // 256):
-        arrival(step).start()
-
     def chunk_body(step, carry):
-        arrival(step).wait()
         planes = pl.ds(pl.multiple_of(step * 16, 16), 16)
 
         def layer(ref, index, x):
@@ -251,15 +298,10 @@
     depth = rows // 16
     return pl.pallas_call(
         faces_kernel,
-        in_specs=in_hbm(1) + in_vmem(1),
-        out_specs=in_vmem(3),
-        out_shape=[
-            jax.ShapeDtypeStruct(fields.shape, F32),
-            jax.ShapeDtypeStruct((LAYERS, depth, 128), BF16),
-            jax.ShapeDtypeStruct((LAYERS, depth, 128), BF16),
-        ],
-        scratch_shapes=[pltpu.SemaphoreType.DMA((rows // 256,))],
-        compiler_params=pltpu.CompilerParams(vmem_limit_bytes=40 * MIB),
+        in_specs=in_vmem(2),
+        out_specs=in_vmem(2),
+        out_shape=[jax.ShapeDtypeStruct((LAYERS, depth, 128), BF16)] * 2,
+        compiler_params=pltpu.CompilerParams(vmem_limit_bytes=4 * MIB),
         cost_estimate=LONG,
         name="faces_part",
     )(fields, prim)
@@ -689,15 +731,16 @@
 
 def per_device(fields, register):
     depth, count_x, count_y = fields.shape[1:]
-    given = fields.reshape(FIELDS, depth * count_x, count_y)
+    flat = fields.reshape(FIELDS, depth * count_x, count_y)
     count = lax.axis_size("gy")
     own = depth // count
     x_forward, x_backward = ring("gx", 1), ring("gx", -1)
 
-    prim, *blocks = probe_part(given, count)
-    for distance in range(2, count - 1):
-        blocks[distance] = lax.ppermute(blocks[distance], "gy", ring("gy", distance))
-    flat, low, high = faces_part(given, prim)
+    blocks = [None] * count
+    for slot, block in enumerate(far_part(flat, count)):
+        blocks[slot + 2] = lax.ppermute(block, "gy", ring("gy", slot + 2))
+    prim, blocks[0], blocks[1], blocks[count - 1] = probe_part(flat, count)
+    low, high = faces_part(flat, prim)
     terms, to_prev, to_next = lines_part(flat, prim, blocks[count - 1], blocks[1])
     blocks[count - 1] = lax.ppermute(to_prev, "gy", ring("gy", -1))
     blocks[1] = lax.ppermute(to_next, "gy", ring("gy", 1))

time: 43.4 us -> 44.5 us (1.025)
  the two profiles are of different devices: /device:TPU:0 before, /device:TPU:1 now
where the time goes in v4:
time: 44.5 us; the launch traced here: 44.4 us
  Pallas kernels  23.8 us (53%)
  starting transfers between devices  10.9 us (24%)
  waiting for transfers between devices  8.83 us (20%)
  between operations  0.79 us (2%)
    pallas_call x1, Pallas kernels, inner_part(): pl.pallas_call(inner_kernel, in_specs=in_vmem(6), out_specs=pl.BlockSpec(...  7.92 us
    pallas_call x1, Pallas kernels, finish_part(): pl.pallas_call(functools.partial(finish_kernel, count, own, chosen), in_s...  5.6 us
    ppermute x1, waiting for transfers between devices, per_device(): blocks[count - 1] = lax.ppermute(to_prev, 'gy', ring('gy', -1))  5.58 us
    ppermute x1, waiting for transfers between devices, per_device(): following = lax.ppermute(low, 'gx', x_backward)  3.24 us
    ppermute x1, starting transfers between devices, per_device(): blocks[slot + 2] = lax.ppermute(block, 'gy', ring('gy', slot + 2))  3.2 us
    pallas_call x1, Pallas kernels, lines_part(): pl.pallas_call(lines_kernel, in_specs=in_vmem(5), out_specs=in_vmem(3), o...  2.94 us
    ppermute x1, starting transfers between devices, per_device(): prev = lax.ppermute(high, 'gx', x_forward)  2.66 us
    pallas_call x1, Pallas kernels, outer_part(): pl.pallas_call(functools.partial(outer_kernel, chosen), in_specs=in_vmem(...  2.55 us
  transfers between devices with their start and end apart: 7, of which 2 were waited for; matrix products, arithmetic and copies ran while one was open for 0% of the time, Pallas kernels for 38%

profile of v4, /device:TPU:1, one launch (start us, length us, event | category | flops | bytes accessed | tf_op | source)
XLA Modules:
  0.0 44.4 jit_solution(1184018467330799823)
XLA Ops:
  0.6 0.0 slice-start.2
  0.6 1.3 %far_part.1 = bf16[928,128]{1,0:T(8,128)(2,1)S(1)} custom-call(f32[14,768,128]{2,1,0:T(8,128)} %bitcast.7), custom_call_target="tpu_custom_call" | custom-call | flops 10000000000 | bytes 1000000 | tf_op jit(solution)/shard_map/far_part/pallas_call | solution.py:173
  1.9 0.0 slice-start.3
  1.9 0.0 copy-start.2
  1.9 3.2 %collective-permute-start.1 = (bf16[928,128]{1,0:T(8,128)(2,1)S(1)}, bf16[928,128]{1,0:T(8,128)(2,1)S(1)}, u32[]{:S(2)}, u32[]{:S(2)}) collective-permute-start(bf16[928,128]{1,0:T(8,128)(2,1)S(1)} %far_part.1), channel_id=1, source_target_pairs={{0,2},{1,3},{2,0},{3,1},{4,6},{5,7},{6,4},{7,5},{8,10},{9,11},{10,... | collective-permute-start | bytes 712712 | tf_op jit(solution)/shard_map/ppermute | solution.py:741
  5.2 1.9 %probe_part.1 = (f32[5,768,128]{2,1,0:T(8,128)S(1)}, bf16[928,128]{1,0:T(8,128)(2,1)S(1)}, bf16[928,128]{1,0:T(8,128)(2,1)S(1)}, bf16[928,128]{1,0:T(8,128)(2,1)S(1)}) custom-call(f32[14,768,128]{2,1,0:T(8,128)} %bitcast.8), custom_call_target="tpu_custom_call" | custom-call | flops 10000000000 | bytes 1000000 | tf_op jit(solution)/shard_map/probe_part/pallas_call | solution.py:250
  7.0 0.0 slice-done.2
  7.0 0.0 slice-done.3
  7.0 0.0 copy-done.2
  7.0 2.9 %lines_part.1 = (bf16[14,768,256]{2,1,0:T(8,128)(2,1)S(1)}, bf16[1312,128]{1,0:T(8,128)(2,1)S(1)}, bf16[1312,128]{1,0:T(8,128)(2,1)S(1)}) custom-call(f32[14,768,128]{2,1,0:T(8,128)S(1)} %bitcast.11, f32[5,768,128]{2,1,0:T(8,128)S(1)} %get-tuple-element.35.prim, bf16[256,128]{1,0:T(8,128)(2,1)S(1)} %copy-done.2, ...), custom_call_target="tpu_custom_call" | custom-call | flops 10000000000 | bytes 1000000 | tf_op jit(solution)/shard_map/lines_part/pallas_call | solution.py:349
  10.0 1.3 %collective-permute-start = (bf16[1312,128]{1,0:T(8,128)(2,1)S(1)}, bf16[1312,128]{1,0:T(8,128)(2,1)S(1)}, u32[]{:S(2)}, u32[]{:S(2)}) collective-permute-start(bf16[1312,128]{1,0:T(8,128)(2,1)S(1)} %get-tuple-element.38), channel_id=1, source_target_pairs={{0,1},{1,2},{2,3},{3,0},{4,5},{5,6},{6,7},{7,4},{8,9},{9,10},{10,1... | collective-permute-start | bytes 1007624 | tf_op jit(solution)/shard_map/ppermute | solution.py:746
  11.3 0.0 slice-start
  11.3 0.0 slice-start.1
  11.3 0.0 copy-start
  11.3 0.0 copy-start.1
  11.3 2.0 %collective-permute-start.2 = (bf16[1312,128]{1,0:T(8,128)(2,1)S(1)}, bf16[1312,128]{1,0:T(8,128)(2,1)S(1)}, u32[]{:S(2)}, u32[]{:S(2)}) collective-permute-start(bf16[1312,128]{1,0:T(8,128)(2,1)S(1)} %get-tuple-element.39), channel_id=1, source_target_pairs={{0,3},{1,0},{2,1},{3,2},{4,7},{5,4},{6,5},{7,6},{8,11},{9,8},{10,9... | collective-permute-start | bytes 1007624 | tf_op jit(solution)/shard_map/ppermute | solution.py:745
  13.4 1.3 %faces_part.1 = (bf16[61,48,128]{2,1,0:T(8,128)(2,1)S(1)}, bf16[61,48,128]{2,1,0:T(8,128)(2,1)S(1)}) custom-call(f32[14,768,128]{2,1,0:T(8,128)S(1)} %bitcast.12, f32[5,768,128]{2,1,0:T(8,128)S(1)} %get-tuple-element.35.prim), custom_call_target="tpu_custom_call" | custom-call | flops 10000000000 | bytes 1000000 | tf_op jit(solution)/shard_map/faces_part/pallas_call | solution.py:299
  14.6 2.7 %collective-permute-start.3 = (bf16[61,48,128]{2,1,0:T(8,128)(2,1)S(1)}, bf16[61,48,128]{2,1,0:T(8,128)(2,1)S(1)}, u32[]{:S(2)}, u32[]{:S(2)}) collective-permute-start(bf16[61,48,128]{2,1,0:T(8,128)(2,1)S(1)} %get-tuple-element.51), channel_id=1, source_target_pairs={{0,4},{4,8},{8,12},{12,16},{16,20},{20,24},{24,28},{28,0},{1,5},{5... | collective-permute-start | bytes 2248712 | tf_op jit(solution)/shard_map/ppermute | solution.py:749
  17.3 0.0 collective-permute-start.4
  17.3 0.0 slice-done
  17.3 0.0 slice-done.1
  17.3 0.0 copy-done
  17.3 0.0 copy-done.1
  17.4 7.9 %inner_part.1.refs_0_ = f32[14,768,128]{2,1,0:T(8,128)S(1)} custom-call(f32[14,768,128]{2,1,0:T(8,128)S(1)} %bitcast.13, f32[5,768,128]{2,1,0:T(8,128)S(1)} %get-tuple-element.35.prim, f32[14,768,128]{2,1,0:T(8,128)S(1)} %bitcast.6, bf16[14,768,256]{2,1,0:T(8,128)(2,1)S(1)} %get-tuple-element.43.terms, bf16[256,128]{1,0:T(8,128)(2,1)S(1)} %copy-done.1, ...), custom_call_target="tpu_custom_call" | custom-call | flops 10000000000 | bytes 1000000 | tf_op jit(solution)/shard_map/inner_part/pallas_call | solution.py:467
  25.3 0.0 collective-permute-done.1.refs_2_
  25.3 0.0 collective-permute-done.refs_1_.refs_4_
  25.3 5.6 %collective-permute-done.2.refs_3_.refs_5_ = bf16[1312,128]{1,0:T(8,128)(2,1)S(1)} collective-permute-done((bf16[1312,128]{1,0:T(8,128)(2,1)S(1)}, bf16[1312,128]{1,0:T(8,128)(2,1)S(1)}, u32[]{:S(2)}, u32[]{:S(2)}) %collective-permute-start.2) | collective-permute-done | bytes 335904 | tf_op jit(solution)/shard_map/ppermute | solution.py:745
  30.9 0.0 copy-start.3
  30.9 0.4 unpack_part.1
  31.3 1.7 %collective-permute-start.5 = (bf16[4,64,128]{2,1,0:T(8,128)(2,1)S(1)}, bf16[4,64,128]{2,1,0:T(8,128)(2,1)S(1)}, u32[]{:S(2)}, u32[]{:S(2)}) collective-permute-start(bf16[4,64,128]{2,1,0:T(8,128)(2,1)S(1)} %get-tuple-element.55), channel_id=1, source_target_pairs={{0,4},{4,8},{8,12},{12,16},{16,20},{20,24},{24,28},{28,0},{1,5},{5... | collective-permute-start | bytes 196616 | tf_op jit(solution)/shard_map/ppermute | solution.py:753
  32.9 0.0 collective-permute-start.6
  32.9 0.0 collective-permute-done.3.refs_2_
  33.0 3.2 %collective-permute-done.4.refs_3_ = bf16[61,48,128]{2,1,0:T(8,128)(2,1)S(1)} collective-permute-done((bf16[61,48,128]{2,1,0:T(8,128)(2,1)S(1)}, bf16[61,48,128]{2,1,0:T(8,128)(2,1)S(1)}, u32[]{:S(2)}, u32[]{:S(2)}) %collective-permute-start.4) | collective-permute-done | bytes 749600 | tf_op jit(solution)/shard_map/ppermute | solution.py:748
  36.2 0.0 copy-done.3
  36.2 2.5 %outer_part.1 = (f32[14,768,128]{2,1,0:T(8,128)}, f32[14,768,128]{2,1,0:T(8,128)}) custom-call(f32[14,768,128]{2,1,0:T(8,128)S(1)} %inner_part.1.refs_0_, f32[14,768,128]{2,1,0:T(8,128)S(1)} %bitcast.14, bf16[61,48,128]{2,1,0:T(8,128)(2,1)S(1)} %collective-permute-done.3.refs_2_, bf16[61,48,128]{2,1,0:T(8,128)(2,1)S(1)} %collective-permute-done.4.refs_3_, ...), custom_call_target="tpu_custom_call" | custom-call | flops 10000000000 | bytes 1000000 | tf_op jit(solution)/shard_map/outer_part/pallas_call | solution.py:535
  38.7 0.0 collective-permute-done.5.refs_9_
  38.8 0.0 collective-permute-done.6.refs_10_
  38.8 5.6 %finish_part.1 = (f32[14,768,128]{2,1,0:T(8,128)}, f32[14,768,128]{2,1,0:T(8,128)}, f32[4,512,128]{2,1,0:T(8,128)S(1)}, f32[3,4,448,128]{3,2,1,0:T(8,128)S(1)}, bf16[5,12,16,512]{3,2,1,0:T(8,128)(2,1)}) custom-call(f32[14,768,128]{2,1,0:T(8,128)S(1)} %inner_part.1.refs_0_, ...), custom_call_target="tpu_custom_call", output_to_operand_aliasing={{2}: (7, {}), {3}: (8, {}), {0}: (11, {}), {1}: (12, {})} | custom-call | flops 10000000000 | bytes 1000000 | tf_op jit(solution)/shard_map/finish_part/pallas_call | solution.py:705
  (2 shorter events, 0.0 us)
Async XLA Ops:
  0.6 6.4 %slice-start.2 = ((s8[5505024]{0:T(1024)(128)(4,1)}), s8[1310720]{0:T(1024)(128)(4,1)S(1)}, s32[]{:S(2)}) async-start(s8[5505024]{0:T(1024)(128)(4,1)} %bitcast.9), calls=%async_computation.2 | async-start | bytes 2621440
  1.9 5.1 %slice-start.3 = ((s8[5505024]{0:T(1024)(128)(4,1)}), s8[4194304]{0:T(1024)(128)(4,1)S(1)}, s32[]{:S(2)}) async-start(s8[5505024]{0:T(1024)(128)(4,1)} %bitcast.9), calls=%async_computation.3 | async-start | bytes 8388608
  1.9 5.1 %copy-start.2 = (bf16[256,128]{1,0:T(8,128)(2,1)S(1)}, bf16[256,128]{1,0:T(8,128)(2,1)}, u32[]{:S(2)}) copy-start(bf16[256,128]{1,0:T(8,128)(2,1)} %constant.8.clone.weights_ref) | copy-start | bytes 196612
  1.9 23.3 %collective-permute-start.1 = (bf16[928,128]{1,0:T(8,128)(2,1)S(1)}, bf16[928,128]{1,0:T(8,128)(2,1)S(1)}, u32[]{:S(2)}, u32[]{:S(2)}) collective-permute-start(bf16[928,128]{1,0:T(8,128)(2,1)S(1)} %far_part.1), channel_id=1, source_target_pairs={{0,2},{1,3},{2,0},{3,1},{4,6},{5,7},{6,4},{7,5},{8,10},{9,11},{10,... | collective-permute-start | bytes 712712 | tf_op jit(solution)/shard_map/ppermute | solution.py:741
  10.0 15.3 %collective-permute-start = (bf16[1312,128]{1,0:T(8,128)(2,1)S(1)}, bf16[1312,128]{1,0:T(8,128)(2,1)S(1)}, u32[]{:S(2)}, u32[]{:S(2)}) collective-permute-start(bf16[1312,128]{1,0:T(8,128)(2,1)S(1)} %get-tuple-element.38), channel_id=1, source_target_pairs={{0,1},{1,2},{2,3},{3,0},{4,5},{5,6},{6,7},{7,4},{8,9},{9,10},{10,1... | collective-permute-start | bytes 1007624 | tf_op jit(solution)/shard_map/ppermute | solution.py:746
  11.3 6.0 %slice-start = ((s8[5505024]{0:T(1024)(128)(4,1)}), s8[4194304]{0:T(1024)(128)(4,1)S(1)}, s32[]{:S(2)}) async-start(s8[5505024]{0:T(1024)(128)(4,1)} %bitcast.4), calls=%async_computation | async-start | bytes 8388608
  11.3 6.0 %slice-start.1 = ((s8[5505024]{0:T(1024)(128)(4,1)}), s8[1310720]{0:T(1024)(128)(4,1)S(1)}, s32[]{:S(2)}) async-start(s8[5505024]{0:T(1024)(128)(4,1)} %bitcast.4), calls=%async_computation.1 | async-start | bytes 2621440
  11.3 6.0 %copy-start = (bf16[128,256]{1,0:T(8,128)(2,1)S(1)}, bf16[128,256]{1,0:T(8,128)(2,1)}, u32[]{:S(2)}) copy-start(bf16[128,256]{1,0:T(8,128)(2,1)} %constant.10.clone.planes_ref) | copy-start | bytes 196612
  11.3 6.0 %copy-start.1 = (bf16[256,128]{1,0:T(8,128)(2,1)S(1)}, bf16[256,128]{1,0:T(8,128)(2,1)}, u32[]{:S(2)}) copy-start(bf16[256,128]{1,0:T(8,128)(2,1)} %constant.9.clone.line_ref) | copy-start | bytes 196612
  11.3 19.5 %collective-permute-start.2 = (bf16[1312,128]{1,0:T(8,128)(2,1)S(1)}, bf16[1312,128]{1,0:T(8,128)(2,1)S(1)}, u32[]{:S(2)}, u32[]{:S(2)}) collective-permute-start(bf16[1312,128]{1,0:T(8,128)(2,1)S(1)} %get-tuple-element.39), channel_id=1, source_target_pairs={{0,3},{1,0},{2,1},{3,2},{4,7},{5,4},{6,5},{7,6},{8,11},{9,8},{10,9... | collective-permute-start | bytes 1007624 | tf_op jit(solution)/shard_map/ppermute | solution.py:745
  14.6 18.3 %collective-permute-start.3 = (bf16[61,48,128]{2,1,0:T(8,128)(2,1)S(1)}, bf16[61,48,128]{2,1,0:T(8,128)(2,1)S(1)}, u32[]{:S(2)}, u32[]{:S(2)}) collective-permute-start(bf16[61,48,128]{2,1,0:T(8,128)(2,1)S(1)} %get-tuple-element.51), channel_id=1, source_target_pairs={{0,4},{4,8},{8,12},{12,16},{16,20},{20,24},{24,28},{28,0},{1,5},{5... | collective-permute-start | bytes 2248712 | tf_op jit(solution)/shard_map/ppermute | solution.py:749
  17.3 18.9 %collective-permute-start.4 = (bf16[61,48,128]{2,1,0:T(8,128)(2,1)S(1)}, bf16[61,48,128]{2,1,0:T(8,128)(2,1)S(1)}, u32[]{:S(2)}, u32[]{:S(2)}) collective-permute-start(bf16[61,48,128]{2,1,0:T(8,128)(2,1)S(1)} %get-tuple-element.52), channel_id=1, source_target_pairs={{0,28},{4,0},{8,4},{12,8},{16,12},{20,16},{24,20},{28,24},{1,29},{... | collective-permute-start | bytes 2248712 | tf_op jit(solution)/shard_map/ppermute | solution.py:748
  30.9 5.3 %copy-start.3 = (bf16[128,128]{1,0:T(8,128)(2,1)S(1)}, bf16[128,128]{1,0:T(8,128)(2,1)}, u32[]{:S(2)}) copy-start(bf16[128,128]{1,0:T(8,128)(2,1)} %constant.11.clone.refs_6_) | copy-start | bytes 98308
  31.3 7.5 %collective-permute-start.5 = (bf16[4,64,128]{2,1,0:T(8,128)(2,1)S(1)}, bf16[4,64,128]{2,1,0:T(8,128)(2,1)S(1)}, u32[]{:S(2)}, u32[]{:S(2)}) collective-permute-start(bf16[4,64,128]{2,1,0:T(8,128)(2,1)S(1)} %get-tuple-element.55), channel_id=1, source_target_pairs={{0,4},{4,8},{8,12},{12,16},{16,20},{20,24},{24,28},{28,0},{1,5},{5... | collective-permute-start | bytes 196616 | tf_op jit(solution)/shard_map/ppermute | solution.py:753
  32.9 5.8 %collective-permute-start.6 = (bf16[4,64,128]{2,1,0:T(8,128)(2,1)S(1)}, bf16[4,64,128]{2,1,0:T(8,128)(2,1)S(1)}, u32[]{:S(2)}, u32[]{:S(2)}) collective-permute-start(bf16[4,64,128]{2,1,0:T(8,128)(2,1)S(1)} %get-tuple-element.56), channel_id=1, source_target_pairs={{0,28},{4,0},{8,4},{12,8},{16,12},{20,16},{24,20},{28,24},{1,29},{... | collective-permute-start | bytes 196616 | tf_op jit(solution)/shard_map/ppermute | solution.py:754

commit v5 on v4

--- a/solution.py
+++ b/solution.py
@@ -33,7 +33,7 @@
 FIELDS = 14
 FLOWS = 5
 LAYERS = 4 * FIELDS + FLOWS
-FIRST = 5
+FIRST = 4
 MIB = 1 << 20
 LONG = pl.CostEstimate(flops=10**10, bytes_accessed=10**6, transcendentals=0)
 F32 = jnp.float32
@@ -314,9 +314,12 @@
     rows = flat.shape[1]
     half = rows // 2
 
+    weights = weights_ref[...]
+
     def fill(step, carry):
-        at = pl.ds(pl.multiple_of(step * 32, 32), 32)
+        at = pl.ds(pl.multiple_of(step * 128, 128), 128)
         v = prim[1, at, :]
+        chosen = None
         for field in range(FIELDS):
             flux = (prim[4, at, :] if field == 4 else flat[field, at, :]) * v
             if field == 2:
@@ -324,16 +327,13 @@
             high, low = two_terms(flux)
             terms[field, at, 0:128] = high
             terms[field, at, 128:256] = low
+            both = jnp.concatenate([high, low], axis=1)
+            product = jnp.dot(both, weights, preferred_element_type=F32)
+            chosen = product if chosen is None else jnp.where(lane_mask(field), product, chosen)
+        total[at, :] = chosen
         return carry
 
-    lax.fori_loop(0, rows // 32, fill, 0)
-    weights = weights_ref[...]
-    for field in range(FIELDS):
-        product = jnp.dot(terms[field], weights, preferred_element_type=F32)
-        if field == 0:
-            total[...] = product
-        else:
-            total[...] = jnp.where(lane_mask(field), product, total[...])
+    lax.fori_loop(0, rows // 128, fill, 0)
     value = total[...] * WHOLE_SCALE
     lanes = lax.broadcasted_iota(jnp.int32, (1, 128), 1)
     second = lanes % 64 >= 4 * FIELDS
@@ -741,12 +741,11 @@
         blocks[slot + 2] = lax.ppermute(block, "gy", ring("gy", slot + 2))
     prim, blocks[0], blocks[1], blocks[count - 1] = probe_part(flat, count)
     low, high = faces_part(flat, prim)
+    following = lax.ppermute(low, "gx", x_backward)
+    prev = lax.ppermute(high, "gx", x_forward)
     terms, to_prev, to_next = lines_part(flat, prim, blocks[count - 1], blocks[1])
     blocks[count - 1] = lax.ppermute(to_prev, "gy", ring("gy", -1))
     blocks[1] = lax.ppermute(to_next, "gy", ring("gy", 1))
-    low, high, terms = lax.optimization_barrier((low, high, terms))
-    following = lax.ppermute(low, "gx", x_backward)
-    prev = lax.ppermute(high, "gx", x_forward)
     part = inner_part(flat, prim, register.reshape(flat.shape), terms)
     *blocks, part = lax.optimization_barrier((*blocks, part))
     scalar, speed, edge_low, edge_high = unpack_part(blocks, own)

time: 44.5 us -> 43.5 us (0.978)
  the two profiles are of different devices: /device:TPU:1 before, /device:TPU:0 now
where the time goes in v5:
time: 43.5 us; the launch traced here: 43.4 us
  Pallas kernels  23.7 us (54%)
  starting transfers between devices  13.4 us (31%)
  waiting for transfers between devices  5.51 us (13%)
  between operations  0.8 us (2%)
    pallas_call x1, Pallas kernels, inner_part(): pl.pallas_call(inner_kernel, in_specs=in_vmem(6), out_specs=pl.BlockSpec(...  7.92 us
    pallas_call x1, Pallas kernels, finish_part(): pl.pallas_call(functools.partial(finish_kernel, count, own, chosen), in_s...  5.89 us
    ppermute x1, waiting for transfers between devices, per_device(): blocks[count - 1] = lax.ppermute(to_prev, 'gy', ring('gy', -1))  4.65 us
    ppermute x1, starting transfers between devices, per_device(): blocks[slot + 2] = lax.ppermute(block, 'gy', ring('gy', slot + 2))  4.1 us
    pallas_call x1, Pallas kernels, lines_part(): pl.pallas_call(lines_kernel, in_specs=in_vmem(5), out_specs=in_vmem(3), o...  2.73 us
    ppermute x1, starting transfers between devices, per_device(): following = lax.ppermute(low, 'gx', x_backward)  2.63 us
    ppermute x1, starting transfers between devices, per_device(): edge_next = lax.ppermute(edge_low, 'gx', x_backward)  2.63 us
    pallas_call x1, Pallas kernels, outer_part(): pl.pallas_call(functools.partial(outer_kernel, chosen), in_specs=in_vmem(...  2.34 us
  transfers between devices with their start and end apart: 7, of which 2 were waited for; matrix products, arithmetic and copies ran while one was open for 0% of the time, Pallas kernels for 38%

profile of v5, /device:TPU:0, one launch (start us, length us, event | category | flops | bytes accessed | tf_op | source)
XLA Modules:
  0.0 43.4 jit_solution(14136922852444166756)
XLA Ops:
  0.6 0.0 slice-start.2
  0.6 1.3 %far_part.1 = bf16[928,128]{1,0:T(8,128)(2,1)S(1)} custom-call(f32[14,768,128]{2,1,0:T(8,128)} %bitcast.7), custom_call_target="tpu_custom_call" | custom-call | flops 10000000000 | bytes 1000000 | tf_op jit(solution)/shard_map/far_part/pallas_call | solution.py:173
  1.9 0.0 slice-start.3
  1.9 4.1 %collective-permute-start.1 = (bf16[928,128]{1,0:T(8,128)(2,1)S(1)}, bf16[928,128]{1,0:T(8,128)(2,1)S(1)}, u32[]{:S(2)}, u32[]{:S(2)}) collective-permute-start(bf16[928,128]{1,0:T(8,128)(2,1)S(1)} %far_part.1), channel_id=1, source_target_pairs={{0,2},{1,3},{2,0},{3,1},{4,6},{5,7},{6,4},{7,5},{8,10},{9,11},{10,... | collective-permute-start | bytes 712712 | tf_op jit(solution)/shard_map/ppermute | solution.py:741
  6.0 1.9 %probe_part.1 = (f32[5,768,128]{2,1,0:T(8,128)S(1)}, bf16[928,128]{1,0:T(8,128)(2,1)S(1)}, bf16[928,128]{1,0:T(8,128)(2,1)S(1)}, bf16[928,128]{1,0:T(8,128)(2,1)S(1)}) custom-call(f32[14,768,128]{2,1,0:T(8,128)} %bitcast.8), custom_call_target="tpu_custom_call" | custom-call | flops 10000000000 | bytes 1000000 | tf_op jit(solution)/shard_map/probe_part/pallas_call | solution.py:250
  7.9 0.0 slice-done.2
  7.9 0.0 slice-done.3
  7.9 0.0 copy-start.2
  7.9 0.0 slice-start
  8.0 1.3 %faces_part.1 = (bf16[61,48,128]{2,1,0:T(8,128)(2,1)S(1)}, bf16[61,48,128]{2,1,0:T(8,128)(2,1)S(1)}) custom-call(f32[14,768,128]{2,1,0:T(8,128)S(1)} %bitcast.11, f32[5,768,128]{2,1,0:T(8,128)S(1)} %get-tuple-element.32.prim), custom_call_target="tpu_custom_call" | custom-call | flops 10000000000 | bytes 1000000 | tf_op jit(solution)/shard_map/faces_part/pallas_call | solution.py:299
  9.2 0.1 collective-permute-start.3
  9.3 2.6 %collective-permute-start.4 = (bf16[61,48,128]{2,1,0:T(8,128)(2,1)S(1)}, bf16[61,48,128]{2,1,0:T(8,128)(2,1)S(1)}, u32[]{:S(2)}, u32[]{:S(2)}) collective-permute-start(bf16[61,48,128]{2,1,0:T(8,128)(2,1)S(1)} %get-tuple-element.46), channel_id=1, source_target_pairs={{0,28},{4,0},{8,4},{12,8},{16,12},{20,16},{24,20},{28,24},{1,29},{... | collective-permute-start | bytes 2248712 | tf_op jit(solution)/shard_map/ppermute | solution.py:744
  11.9 0.0 copy-done.2
  11.9 0.0 slice-start.1
  11.9 0.0 copy-start
  11.9 0.0 copy-start.1
  11.9 2.7 %lines_part.1 = (bf16[14,768,256]{2,1,0:T(8,128)(2,1)S(1)}, bf16[1312,128]{1,0:T(8,128)(2,1)S(1)}, bf16[1312,128]{1,0:T(8,128)(2,1)S(1)}) custom-call(f32[14,768,128]{2,1,0:T(8,128)S(1)} %bitcast.12, f32[5,768,128]{2,1,0:T(8,128)S(1)} %get-tuple-element.32.prim, bf16[256,128]{1,0:T(8,128)(2,1)S(1)} %copy-done.2, ...), custom_call_target="tpu_custom_call" | custom-call | flops 10000000000 | bytes 1000000 | tf_op jit(solution)/shard_map/lines_part/pallas_call | solution.py:349
  14.7 1.6 %collective-permute-start = (bf16[1312,128]{1,0:T(8,128)(2,1)S(1)}, bf16[1312,128]{1,0:T(8,128)(2,1)S(1)}, u32[]{:S(2)}, u32[]{:S(2)}) collective-permute-start(bf16[1312,128]{1,0:T(8,128)(2,1)S(1)} %get-tuple-element.35), channel_id=1, source_target_pairs={{0,1},{1,2},{2,3},{3,0},{4,5},{5,6},{6,7},{7,4},{8,9},{9,10},{10,1... | collective-permute-start | bytes 1007624 | tf_op jit(solution)/shard_map/ppermute | solution.py:748
  16.3 2.3 %collective-permute-start.2 = (bf16[1312,128]{1,0:T(8,128)(2,1)S(1)}, bf16[1312,128]{1,0:T(8,128)(2,1)S(1)}, u32[]{:S(2)}, u32[]{:S(2)}) collective-permute-start(bf16[1312,128]{1,0:T(8,128)(2,1)S(1)} %get-tuple-element.36), channel_id=1, source_target_pairs={{0,3},{1,0},{2,1},{3,2},{4,7},{5,4},{6,5},{7,6},{8,11},{9,8},{10,9... | collective-permute-start | bytes 1007624 | tf_op jit(solution)/shard_map/ppermute | solution.py:747
  18.6 0.0 slice-done
  18.6 0.0 slice-done.1
  18.6 0.0 copy-done
  18.6 0.0 copy-done.1
  18.6 7.9 %inner_part.1.refs_0_ = f32[14,768,128]{2,1,0:T(8,128)S(1)} custom-call(f32[14,768,128]{2,1,0:T(8,128)S(1)} %bitcast.13, f32[5,768,128]{2,1,0:T(8,128)S(1)} %get-tuple-element.32.prim, f32[14,768,128]{2,1,0:T(8,128)S(1)} %bitcast.6, bf16[14,768,256]{2,1,0:T(8,128)(2,1)S(1)} %get-tuple-element.37.terms, bf16[256,128]{1,0:T(8,128)(2,1)S(1)} %copy-done.1, ...), custom_call_target="tpu_custom_call" | custom-call | flops 10000000000 | bytes 1000000 | tf_op jit(solution)/shard_map/inner_part/pallas_call | solution.py:467
  26.5 0.0 collective-permute-done.1.refs_2_
  26.5 0.8 %collective-permute-done.refs_1_.refs_4_ = bf16[1312,128]{1,0:T(8,128)(2,1)S(1)} collective-permute-done((bf16[1312,128]{1,0:T(8,128)(2,1)S(1)}, bf16[1312,128]{1,0:T(8,128)(2,1)S(1)}, u32[]{:S(2)}, u32[]{:S(2)}) %collective-permute-start) | collective-permute-done | bytes 335904 | tf_op jit(solution)/shard_map/ppermute | solution.py:748
  27.4 4.7 %collective-permute-done.2.refs_3_.refs_5_ = bf16[1312,128]{1,0:T(8,128)(2,1)S(1)} collective-permute-done((bf16[1312,128]{1,0:T(8,128)(2,1)S(1)}, bf16[1312,128]{1,0:T(8,128)(2,1)S(1)}, u32[]{:S(2)}, u32[]{:S(2)}) %collective-permute-start.2) | collective-permute-done | bytes 335904 | tf_op jit(solution)/shard_map/ppermute | solution.py:747
  32.0 0.0 copy-start.3
  32.0 0.4 unpack_part.1
  32.4 0.1 collective-permute-start.5
  32.5 2.6 %collective-permute-start.6 = (bf16[4,64,128]{2,1,0:T(8,128)(2,1)S(1)}, bf16[4,64,128]{2,1,0:T(8,128)(2,1)S(1)}, u32[]{:S(2)}, u32[]{:S(2)}) collective-permute-start(bf16[4,64,128]{2,1,0:T(8,128)(2,1)S(1)} %get-tuple-element.50), channel_id=1, source_target_pairs={{0,28},{4,0},{8,4},{12,8},{16,12},{20,16},{24,20},{28,24},{1,29},{... | collective-permute-start | bytes 196616 | tf_op jit(solution)/shard_map/ppermute | solution.py:753
  35.1 0.0 collective-permute-done.3.refs_2_
  35.1 0.0 collective-permute-done.4.refs_3_
  35.1 0.0 copy-done.3
  35.1 2.3 %outer_part.1 = (f32[14,768,128]{2,1,0:T(8,128)}, f32[14,768,128]{2,1,0:T(8,128)}) custom-call(f32[14,768,128]{2,1,0:T(8,128)S(1)} %inner_part.1.refs_0_, f32[14,768,128]{2,1,0:T(8,128)S(1)} %bitcast.14, bf16[61,48,128]{2,1,0:T(8,128)(2,1)S(1)} %collective-permute-done.3.refs_2_, bf16[61,48,128]{2,1,0:T(8,128)(2,1)S(1)} %collective-permute-done.4.refs_3_, ...), custom_call_target="tpu_custom_call" | custom-call | flops 10000000000 | bytes 1000000 | tf_op jit(solution)/shard_map/outer_part/pallas_call | solution.py:535
  37.5 0.0 collective-permute-done.5.refs_9_
  37.5 0.0 collective-permute-done.6.refs_10_
  37.5 5.9 %finish_part.1 = (f32[14,768,128]{2,1,0:T(8,128)}, f32[14,768,128]{2,1,0:T(8,128)}, f32[4,512,128]{2,1,0:T(8,128)S(1)}, f32[3,4,448,128]{3,2,1,0:T(8,128)S(1)}, bf16[5,12,16,512]{3,2,1,0:T(8,128)(2,1)}) custom-call(f32[14,768,128]{2,1,0:T(8,128)S(1)} %inner_part.1.refs_0_, ...), custom_call_target="tpu_custom_call", output_to_operand_aliasing={{2}: (7, {}), {3}: (8, {}), {0}: (11, {}), {1}: (12, {})} | custom-call | flops 10000000000 | bytes 1000000 | tf_op jit(solution)/shard_map/finish_part/pallas_call | solution.py:705
  (2 shorter events, 0.0 us)
Async XLA Ops:
  0.6 7.3 %slice-start.2 = ((s8[5505024]{0:T(1024)(128)(4,1)}), s8[1310720]{0:T(1024)(128)(4,1)S(1)}, s32[]{:S(2)}) async-start(s8[5505024]{0:T(1024)(128)(4,1)} %bitcast.9), calls=%async_computation.2 | async-start | bytes 2621440
  1.9 6.0 %slice-start.3 = ((s8[5505024]{0:T(1024)(128)(4,1)}), s8[4194304]{0:T(1024)(128)(4,1)S(1)}, s32[]{:S(2)}) async-start(s8[5505024]{0:T(1024)(128)(4,1)} %bitcast.9), calls=%async_computation.3 | async-start | bytes 8388608
  1.9 24.6 %collective-permute-start.1 = (bf16[928,128]{1,0:T(8,128)(2,1)S(1)}, bf16[928,128]{1,0:T(8,128)(2,1)S(1)}, u32[]{:S(2)}, u32[]{:S(2)}) collective-permute-start(bf16[928,128]{1,0:T(8,128)(2,1)S(1)} %far_part.1), channel_id=1, source_target_pairs={{0,2},{1,3},{2,0},{3,1},{4,6},{5,7},{6,4},{7,5},{8,10},{9,11},{10,... | collective-permute-start | bytes 712712 | tf_op jit(solution)/shard_map/ppermute | solution.py:741
  7.9 4.0 %copy-start.2 = (bf16[256,128]{1,0:T(8,128)(2,1)S(1)}, bf16[256,128]{1,0:T(8,128)(2,1)}, u32[]{:S(2)}) copy-start(bf16[256,128]{1,0:T(8,128)(2,1)} %constant.8.clone.weights_ref) | copy-start | bytes 196612
  7.9 10.6 %slice-start = ((s8[5505024]{0:T(1024)(128)(4,1)}), s8[4194304]{0:T(1024)(128)(4,1)S(1)}, s32[]{:S(2)}) async-start(s8[5505024]{0:T(1024)(128)(4,1)} %bitcast.4), calls=%async_computation | async-start | bytes 8388608
  9.2 25.9 %collective-permute-start.3 = (bf16[61,48,128]{2,1,0:T(8,128)(2,1)S(1)}, bf16[61,48,128]{2,1,0:T(8,128)(2,1)S(1)}, u32[]{:S(2)}, u32[]{:S(2)}) collective-permute-start(bf16[61,48,128]{2,1,0:T(8,128)(2,1)S(1)} %get-tuple-element.45), channel_id=1, source_target_pairs={{0,4},{4,8},{8,12},{12,16},{16,20},{20,24},{24,28},{28,0},{1,5},{5... | collective-permute-start | bytes 2248712 | tf_op jit(solution)/shard_map/ppermute | solution.py:745
  9.3 25.8 %collective-permute-start.4 = (bf16[61,48,128]{2,1,0:T(8,128)(2,1)S(1)}, bf16[61,48,128]{2,1,0:T(8,128)(2,1)S(1)}, u32[]{:S(2)}, u32[]{:S(2)}) collective-permute-start(bf16[61,48,128]{2,1,0:T(8,128)(2,1)S(1)} %get-tuple-element.46), channel_id=1, source_target_pairs={{0,28},{4,0},{8,4},{12,8},{16,12},{20,16},{24,20},{28,24},{1,29},{... | collective-permute-start | bytes 2248712 | tf_op jit(solution)/shard_map/ppermute | solution.py:744
  11.9 6.6 %slice-start.1 = ((s8[5505024]{0:T(1024)(128)(4,1)}), s8[1310720]{0:T(1024)(128)(4,1)S(1)}, s32[]{:S(2)}) async-start(s8[5505024]{0:T(1024)(128)(4,1)} %bitcast.4), calls=%async_computation.1 | async-start | bytes 2621440
  11.9 6.6 %copy-start = (bf16[128,256]{1,0:T(8,128)(2,1)S(1)}, bf16[128,256]{1,0:T(8,128)(2,1)}, u32[]{:S(2)}) copy-start(bf16[128,256]{1,0:T(8,128)(2,1)} %constant.10.clone.planes_ref) | copy-start | bytes 196612
  11.9 6.6 %copy-start.1 = (bf16[256,128]{1,0:T(8,128)(2,1)S(1)}, bf16[256,128]{1,0:T(8,128)(2,1)}, u32[]{:S(2)}) copy-start(bf16[256,128]{1,0:T(8,128)(2,1)} %constant.9.clone.line_ref) | copy-start | bytes 196612
  14.7 12.7 %collective-permute-start = (bf16[1312,128]{1,0:T(8,128)(2,1)S(1)}, bf16[1312,128]{1,0:T(8,128)(2,1)S(1)}, u32[]{:S(2)}, u32[]{:S(2)}) collective-permute-start(bf16[1312,128]{1,0:T(8,128)(2,1)S(1)} %get-tuple-element.35), channel_id=1, source_target_pairs={{0,1},{1,2},{2,3},{3,0},{4,5},{5,6},{6,7},{7,4},{8,9},{9,10},{10,1... | collective-permute-start | bytes 1007624 | tf_op jit(solution)/shard_map/ppermute | solution.py:748
  16.3 15.7 %collective-permute-start.2 = (bf16[1312,128]{1,0:T(8,128)(2,1)S(1)}, bf16[1312,128]{1,0:T(8,128)(2,1)S(1)}, u32[]{:S(2)}, u32[]{:S(2)}) collective-permute-start(bf16[1312,128]{1,0:T(8,128)(2,1)S(1)} %get-tuple-element.36), channel_id=1, source_target_pairs={{0,3},{1,0},{2,1},{3,2},{4,7},{5,4},{6,5},{7,6},{8,11},{9,8},{10,9... | collective-permute-start | bytes 1007624 | tf_op jit(solution)/shard_map/ppermute | solution.py:747
  32.0 3.1 %copy-start.3 = (bf16[128,128]{1,0:T(8,128)(2,1)S(1)}, bf16[128,128]{1,0:T(8,128)(2,1)}, u32[]{:S(2)}) copy-start(bf16[128,128]{1,0:T(8,128)(2,1)} %constant.11.clone.refs_6_) | copy-start | bytes 98308
  32.4 5.1 %collective-permute-start.5 = (bf16[4,64,128]{2,1,0:T(8,128)(2,1)S(1)}, bf16[4,64,128]{2,1,0:T(8,128)(2,1)S(1)}, u32[]{:S(2)}, u32[]{:S(2)}) collective-permute-start(bf16[4,64,128]{2,1,0:T(8,128)(2,1)S(1)} %get-tuple-element.49), channel_id=1, source_target_pairs={{0,4},{4,8},{8,12},{12,16},{16,20},{20,24},{24,28},{28,0},{1,5},{5... | collective-permute-start | bytes 196616 | tf_op jit(solution)/shard_map/ppermute | solution.py:752
  32.5 5.0 %collective-permute-start.6 = (bf16[4,64,128]{2,1,0:T(8,128)(2,1)S(1)}, bf16[4,64,128]{2,1,0:T(8,128)(2,1)S(1)}, u32[]{:S(2)}, u32[]{:S(2)}) collective-permute-start(bf16[4,64,128]{2,1,0:T(8,128)(2,1)S(1)} %get-tuple-element.50), channel_id=1, source_target_pairs={{0,28},{4,0},{8,4},{12,8},{16,12},{20,16},{24,20},{28,24},{1,29},{... | collective-permute-start | bytes 196616 | tf_op jit(solution)/shard_map/ppermute | solution.py:753
